TPU v7x, 256 devices: a whole 4x4x8 slice. The times are simulated.
256 devices in a mesh: group: 4 (over z_lo), fsdp: 32 (over x, z_hi, y), seq: 2 (over core).
Axes of the slice: x: 4, y: 4, z: 8 (z_hi: 2, z_lo: 4; z = z_hi * 4 + z_lo), core: 2. Of those that a mesh axis runs over, the one named last changes fastest.
Arguments:
- gen_noise: bfloat16 [3, 4096, 64], P(None, 'fsdp'), may hold values from -5 to 5
- score_noise: bfloat16 [3, 4096, 64], P(None, 'fsdp'), may hold values from -128 to 128
- gen_steps: int32 [3], replicated, may hold values from 0 to 999
- score_steps: int32 [3], replicated, may hold values from 0 to 999
- gen_embed: bfloat16 [64, 3072], replicated, may hold values from -0.75 to 0.75
- gen_modulation: bfloat16 [256, 15360], P(None, 'fsdp'), may hold values from -0.375 to 0.375
- gen_proj: bfloat16 [3072, 3072], P('fsdp', ('group', 'seq')), may hold values from -0.109375 to 0.109375
- gen_final: bfloat16 [3072, 64], replicated, may hold values from -0.109375 to 0.109375
- teacher_embed: bfloat16 [64, 3072], replicated, may hold values from -0.75 to 0.75
- teacher_modulation: bfloat16 [256, 15360], P(None, 'fsdp'), may hold values from -0.375 to 0.375
- teacher_proj: bfloat16 [3072, 3072], P('fsdp', ('group', 'seq')), may hold values from -0.109375 to 0.109375
- teacher_final: bfloat16 [3072, 64], replicated, may hold values from -0.109375 to 0.109375
- fake_embed: bfloat16 [64, 3072], replicated, may hold values from -0.75 to 0.75
- fake_modulation: bfloat16 [256, 15360], P(None, 'fsdp'), may hold values from -0.375 to 0.375
- fake_proj: bfloat16 [3072, 3072], P('fsdp', ('group', 'seq')), may hold values from -0.109375 to 0.109375
- fake_final: bfloat16 [3072, 64], replicated, may hold values from -0.109375 to 0.109375
Outputs:
- samples: float32 [3, 4096, 64], P(None, 'fsdp')
- gen_grad: float32 [3072, 3072], P('fsdp', ('group', 'seq'))
- fake_grad: float32 [3072, 3072], P('fsdp', ('group', 'seq'))
All inputs are finite; a program needn't handle non-finite values.
Results may differ from a plain program's by a relative error of at most 0.0063.
Values may be sent and summed in bfloat16 or wider, within the bound.
No kernel may reach another device: no remote copies, remote signals or barrier semaphores. Data moves between devices by JAX's collectives and lax.ppermute only.
A program may use at most 128 MiB of HBM per device.

v0:
```python
import math

import jax
import jax.numpy as jnp
from jax import lax
from jax.sharding import PartitionSpec as P

S = 4096
STEPS = 1000


norm_epsilon = 1e-06
gap_epsilon = 1e-05


def time_features(steps, embed_width):
    times = (steps.astype(jnp.float32) + 1.0) / (STEPS + 1.0)
    half = embed_width // 2
    frequency = jnp.exp(-jnp.log(10000.0) * jnp.arange(half, dtype=jnp.float32) / half)
    angles = 1000.0 * times[:, None] * frequency[None, :]
    embedding = jnp.concatenate([jnp.cos(angles), jnp.sin(angles)], axis=1)
    return (times, jax.nn.silu(embedding).astype(jnp.bfloat16))


def modulation_vectors(conditioning, weights):
    partial_mods = jnp.dot(conditioning, weights, preferred_element_type=jnp.float32).astype(
        jnp.bfloat16
    )
    gathered = lax.all_gather(partial_mods, "fsdp", axis=1, tiled=True)
    return gathered.astype(jnp.float32).reshape(conditioning.shape[0], 5, -1)


def layer_norm(values):
    average = jnp.mean(values, axis=-1, keepdims=True)
    squares = jnp.mean(values * values, axis=-1, keepdims=True)
    inverse_rms = lax.rsqrt(squares - average * average + norm_epsilon)
    return ((values - average) * inverse_rms, inverse_rms)


def gelu_grad(preactivation, upstream):
    return jax.vjp(lambda inner_value: jax.nn.gelu(inner_value, approximate=True), preactivation)[
        1
    ](upstream)[0]


def net_forward(latents, modulations, w_embed, w_proj, w_final):
    images, tokens, channels = latents.shape
    model_width = w_embed.shape[1]
    hidden = jnp.dot(
        latents.reshape(images * tokens, channels), w_embed, preferred_element_type=jnp.float32
    ).reshape(images, tokens, model_width)
    normed, _ = layer_norm(hidden)
    shaped = (
        (normed * (1.0 + modulations[:, 1:2, :]) + modulations[:, 0:1, :])
        .astype(jnp.bfloat16)
        .reshape(images * tokens, model_width)
    )
    preactivation = jnp.dot(
        shaped,
        lax.all_gather(w_proj, "fsdp", axis=0, tiled=True),
        preferred_element_type=jnp.float32,
    )
    activated = jax.nn.gelu(preactivation, approximate=True).astype(jnp.bfloat16)
    gathered = lax.all_gather(activated, ("group", "seq"), axis=1, tiled=True).reshape(
        images, tokens, model_width
    )
    residual = hidden + modulations[:, 2:3, :] * gathered.astype(jnp.float32)
    normed_two, inverse_rms = layer_norm(residual)
    output = (normed_two * (1.0 + modulations[:, 4:5, :]) + modulations[:, 3:4, :]).astype(
        jnp.bfloat16
    )
    velocity = jnp.dot(
        output.reshape(images * tokens, model_width), w_final, preferred_element_type=jnp.float32
    )
    return (velocity.reshape(images, tokens, -1), (shaped, preactivation, normed_two, inverse_rms))


def net_backward(cotangent, stored, modulations, w_final, column_start):
    shaped, preactivation, normed_two, inverse_rms = stored
    images, tokens = (cotangent.shape[0], cotangent.shape[1])
    model_width = shaped.shape[1]
    columns = preactivation.shape[1]
    cot_small = cotangent.reshape(images * tokens, -1).astype(jnp.bfloat16)
    local_mods = lax.dynamic_slice_in_dim(modulations, column_start, columns, 2)
    out_grad = lax.dot_general(
        cot_small, w_final, (((1,), (1,)), ((), ())), preferred_element_type=jnp.float32
    ).reshape(images, tokens, model_width)
    norm_grad = out_grad * (1.0 + modulations[:, 4:5, :])
    first_moment = jnp.mean(norm_grad, axis=-1, keepdims=True)
    second_moment = jnp.mean(norm_grad * normed_two, axis=-1, keepdims=True)
    full_grad = inverse_rms * (norm_grad - first_moment - normed_two * second_moment)
    residual_grad = lax.dynamic_slice_in_dim(full_grad, column_start, columns, 2)
    activation_grad = (residual_grad * local_mods[:, 2:3, :]).reshape(images * tokens, columns)
    preact_grad = gelu_grad(preactivation, activation_grad).astype(jnp.bfloat16)
    return lax.psum_scatter(
        lax.dot_general(
            shaped, preact_grad, (((0,), (0,)), ((), ())), preferred_element_type=jnp.float32
        ),
        "fsdp",
        scatter_dimension=0,
        tiled=True,
    )


def shards(
    gen_noise,
    score_noise,
    gen_steps,
    score_steps,
    gen_embed,
    gen_modulation,
    gen_proj,
    gen_final,
    teacher_embed,
    teacher_modulation,
    teacher_proj,
    teacher_final,
    fake_embed,
    fake_modulation,
    fake_proj,
    fake_final,
):
    columns = gen_proj.shape[1]
    column_start = lax.axis_index(("group", "seq")) * columns
    images, tokens, channels = gen_noise.shape
    loss_scale = 1.0 / math.sqrt(images * S)
    embed_width = gen_modulation.shape[0]
    gen_time, gen_cond = time_features(gen_steps, embed_width)
    score_time, score_cond = time_features(score_steps, embed_width)
    gen_mods = modulation_vectors(gen_cond, gen_modulation)
    gen_velocity, gen_stored = net_forward(gen_noise, gen_mods, gen_embed, gen_proj, gen_final)
    samples = gen_noise.astype(jnp.float32) - gen_time[:, None, None] * gen_velocity
    noise_values = score_noise.astype(jnp.float32)
    noise_time = score_time[:, None, None]
    noised = ((1.0 - noise_time) * samples + noise_time * noise_values).astype(jnp.bfloat16)
    teacher_mods = modulation_vectors(score_cond, teacher_modulation)
    teacher_vel, _ = net_forward(noised, teacher_mods, teacher_embed, teacher_proj, teacher_final)
    fake_mods = modulation_vectors(score_cond, fake_modulation)
    fake_vel, fake_stored = net_forward(noised, fake_mods, fake_embed, fake_proj, fake_final)
    distance = jnp.abs(samples - noised.astype(jnp.float32) + noise_time * teacher_vel)
    gap_total = lax.psum(jnp.sum(distance, axis=(1, 2)), "fsdp")
    gap = gap_total / (S * channels) + gap_epsilon
    gen_cot = (
        -(gen_time[:, None, None] * noise_time * loss_scale)
        * (teacher_vel - fake_vel)
        / gap[:, None, None]
    )
    fake_cot = loss_scale * (fake_vel - noise_values + samples)
    gen_grad = net_backward(gen_cot, gen_stored, gen_mods, gen_final, column_start)
    fake_grad = net_backward(fake_cot, fake_stored, fake_mods, fake_final, column_start)
    return (samples, gen_grad, fake_grad)


def solution(mesh):
    placed = (
        P(None, "fsdp", None),
        P(None, "fsdp", None),
        P(),
        P(),
        P(),
        P(None, "fsdp"),
        P("fsdp", ("group", "seq")),
        P(),
        P(),
        P(None, "fsdp"),
        P("fsdp", ("group", "seq")),
        P(),
        P(),
        P(None, "fsdp"),
        P("fsdp", ("group", "seq")),
        P(),
    )
    return jax.shard_map(
        shards,
        mesh=mesh,
        in_specs=placed,
        out_specs=(P(None, "fsdp", None), P("fsdp", ("group", "seq")), P("fsdp", ("group", "seq"))),
        check_vma=False,
    )
```

profile of v0, /device:TPU:1, one launch (start us, length us, event | category | flops | bytes accessed | tf_op | source)
XLA Modules:
  0.0 990.0 jit_solution(5358586820611991763)
XLA Ops:
  7.2 0.7 all-gather.10.cloned.1.call-update
  7.9 0.0 all-gather.12.cloned.1.call-start
  8.0 1.3 multiply_negate_fusion
  9.3 0.1 multiply_cosine_fusion
  9.4 1.1 fusion.16
  10.5 106.9 %all-gather = bf16[32,480,3]{1,2,0:T(4,128)(2,1)S(1)} all-gather(bf16[1,480,3]{1,2,0:T(4,128)(2,1)S(1)} %fusion.16), channel_id=1, replica_groups=mesh['group'=4,'fsdp'=32,'seq'=2] {'fsdp'}, dimensions={0}, use_global_device_ids=true | all-gather | bytes 95040 | tf_op jit(solution)/shard_map/all_gather | solution.py:29
  117.4 0.2 reshape.250
  117.6 0.1 reshape.232
  117.8 1.9 fusion.90
  119.7 1.0 slice_add_fusion.4
  120.7 1.2 copy-done.2
  121.9 1.2 add_convert_fusion.5
  123.1 4.0 multiply_convert_fusion.1
  127.1 0.0 all-gather.18.cloned.1.call-start
  127.2 0.7 all-gather.18.cloned.1.call-update
  127.9 0.5 all-gather.14.cloned.1.call-update
  128.5 0.2 fusion.18
  128.7 93.6 %all-gather.2 = bf16[32,480,3]{1,2,0:T(4,128)(2,1)S(1)} all-gather(bf16[1,480,3]{1,2,0:T(4,128)(2,1)S(1)} %fusion.18), channel_id=1, replica_groups=mesh['group'=4,'fsdp'=32,'seq'=2] {'fsdp'}, dimensions={0}, use_global_device_ids=true | all-gather | bytes 95040 | tf_op jit(solution)/shard_map/all_gather | solution.py:29
  222.3 0.2 reshape.254
  222.5 0.9 reshape.238
  223.4 2.4 slice_add_fusion
  225.8 0.8 copy_bitcast_fusion.10
  226.7 4.3 fusion.10
  231.1 3.5 subtract_multiply_fusion.1
  234.8 2.0 fusion.65
  236.8 0.9 fusion.88
  237.7 2.2 copy-done.1
  239.9 2.6 add_convert_fusion.1
  242.5 29.0 %all-gather.18.cloned.1.call-done = bf16[3072,384]{1,0:T(8,128)(2,1)} async-done(((bf16[96,384]{1,0:T(8,128)(2,1)}), bf16[3072,384]{1,0:T(8,128)(2,1)}) %all-gather.18.cloned.1.call-update) | async-done | bytes 2359312 | tf_op jit(solution)/shard_map/all_gather | solution.py:60
  271.4 4.7 multiply_convert_fusion
  276.2 0.0 all-gather.16.cloned.1.call-start
  276.2 0.2 fusion.17
  276.4 96.4 %all-gather.1 = bf16[32,480,3]{1,2,0:T(4,128)(2,1)S(1)} all-gather(bf16[1,480,3]{1,2,0:T(4,128)(2,1)S(1)} %fusion.17), channel_id=1, replica_groups=mesh['group'=4,'fsdp'=32,'seq'=2] {'fsdp'}, dimensions={0}, use_global_device_ids=true | all-gather | bytes 95040 | tf_op jit(solution)/shard_map/all_gather | solution.py:29
  372.9 0.2 reshape.252
  373.1 0.9 reshape.235
  374.0 2.4 fusion.91
  376.4 1.9 fusion.89
  378.4 2.2 copy-done.4
  380.6 2.6 add_convert_fusion.3
  383.2 4.7 fusion.40
  387.9 0.0 reduce-scatter.5.cloned.1.call-start
  388.0 0.9 constant_dynamic-slice_fusion
  388.9 12.0 %all-gather.20.cloned.1.call-done = bf16[384,3072]{1,0:T(8,128)(2,1)} async-done(((bf16[384,384]{1,0:T(8,128)(2,1)}), bf16[384,3072]{1,0:T(8,128)(2,1)}) %all-gather.20.cloned.1.call-update) | async-done | bytes 2359312 | tf_op jit(solution)/shard_map/all_gather | solution.py:64
  400.9 4.3 fusion.13
  405.2 3.6 subtract_multiply_fusion
  408.8 0.9 fusion.4
  409.7 1.1 fusion.86
  410.8 0.2 fusion.43
  411.0 0.4 fusion.32
  411.5 0.1 copy-done.5
  411.5 3.8 fusion.93
  415.4 0.3 reduce-scatter.3.cloned.1.call-start
  415.7 0.5 copy-done.21
  416.2 0.1 constant_dynamic-slice_fusion.1
  416.3 29.0 %all-gather.16.cloned.1.call-done = bf16[384,3072]{1,0:T(8,128)(2,1)} async-done(((bf16[384,384]{1,0:T(8,128)(2,1)}), bf16[384,3072]{1,0:T(8,128)(2,1)}) %all-gather.16.cloned.1.call-update) | async-done | bytes 2359312 | tf_op jit(solution)/shard_map/all_gather | solution.py:64
  445.3 4.3 fusion.12
  449.7 3.9 abs_reduce_fusion
  453.5 102.0 %psum.7 = f32[3]{0:T(128)S(1)} all-reduce(f32[3]{0:T(128)S(1)} %get-tuple-element.67), channel_id=1, replica_groups=mesh['group'=4,'fsdp'=32,'seq'=2] {'fsdp'}, use_global_device_ids=true, to_apply=%region_13.14 | all-reduce | flops 3 | bytes 24 | tf_op jit(solution)/shard_map/psum | solution.py:141
  555.6 3.5 fusion.87
  559.1 1.3 fusion.46
  560.4 0.4 fusion.25
  560.8 3.8 fusion.92
  564.6 152.2 %reduce-scatter.5.cloned.1.call-done = f32[96,384]{1,0:T(8,128)} async-done(((f32[3072,384]{1,0:T(8,128)}), f32[96,384]{1,0:T(8,128)}) %reduce-scatter.5.cloned.1.call-update) | async-done | bytes 147472 | tf_op jit(solution)/shard_map/reduce_scatter | solution.py:95
  716.8 266.3 %reduce-scatter.3.cloned.1.call-done = f32[96,384]{1,0:T(8,128)} async-done(((f32[3072,384]{1,0:T(8,128)}), f32[96,384]{1,0:T(8,128)}) %reduce-scatter.3.cloned.1.call-update) | async-done | bytes 147472 | tf_op jit(solution)/shard_map/reduce_scatter | solution.py:95
  (91 shorter events, 0.7 us)
Async XLA Ops:
  7.2 227.5 %copy-start = (bf16[3072,64]{0,1:T(8,128)(2,1)S(1)}, bf16[3072,64]{0,1:T(8,128)(2,1)}, u32[]{:S(2)}) copy-start(bf16[3072,64]{0,1:T(8,128)(2,1)} %param.23) | copy-start | bytes 1179652
  7.2 115.9 %all-gather.10.cloned.1.call-start = ((), (), s32[]{:S(2)}) async-start(), calls=%async_computation.2 | async-start | bytes 2433024 | tf_op jit(solution)/shard_map/all_gather | solution.py:60
  7.9 218.8 %all-gather.12.cloned.1.call-start = ((), (), s32[]{:S(2)}) async-start(), calls=%async_computation.3 | async-start | bytes 2654208 | tf_op jit(solution)/shard_map/all_gather | solution.py:64
  119.7 2.2 copy-start.2
  123.0 5.5 copy-start.16
  127.1 144.3 %all-gather.18.cloned.1.call-start = ((), (), s32[]{:S(2)}) async-start(), calls=%async_computation.6 | async-start | bytes 2433024 | tf_op jit(solution)/shard_map/all_gather | solution.py:60
  127.9 255.3 %all-gather.14.cloned.1.call-start = ((), (), s32[]{:S(2)}) async-start(), calls=%async_computation.4 | async-start | bytes 2433024 | tf_op jit(solution)/shard_map/all_gather | solution.py:60
  128.5 272.4 %all-gather.20.cloned.1.call-start = ((), (), s32[]{:S(2)}) async-start(), calls=%async_computation.7 | async-start | bytes 2654208 | tf_op jit(solution)/shard_map/all_gather | solution.py:64
  226.6 8.0 copy-start.12
  226.7 4.3 copy-start.7
  231.1 3.6 copy-start.18
  231.1 3.6 copy-start.19
  231.1 3.6 copy-start.25
  231.1 3.6 copy-start.27
  231.1 3.6 copy-start.28
  234.7 3.1 copy-start.3
  234.7 2.1 copy-start.15
  237.7 2.2 copy-start.1
  242.5 33.8 %copy-start.17 = (bf16[256,480]{0,1:T(8,128)(2,1)S(1)}, bf16[256,480]{0,1:T(8,128)(2,1)}, u32[]{:S(2)}) copy-start(bf16[256,480]{0,1:T(8,128)(2,1)} %param.25) | copy-start | bytes 737284
  276.2 169.2 %all-gather.16.cloned.1.call-start = ((), (), s32[]{:S(2)}) async-start(), calls=%async_computation.5 | async-start | bytes 2654208 | tf_op jit(solution)/shard_map/all_gather | solution.py:64
  378.3 2.2 copy-start.4
  383.2 4.8 copy-start.23
  383.2 4.8 copy-start.24
  383.2 4.8 copy-start.22
  387.9 329.0 %reduce-scatter.5.cloned.1.call-start = ((), (), s32[]{:S(2)}) async-start(), calls=%async_computation.9 | async-start | bytes 4866048 | tf_op jit(solution)/shard_map/reduce_scatter | solution.py:95
  400.9 4.3 copy-start.6
  405.2 3.6 copy-start.9
  408.7 0.9 copy-start.14
  408.8 0.9 copy-start.20
  409.7 1.4 copy-start.11
  409.7 1.9 copy-start.5
  415.4 0.8 copy-start.21
  415.4 34.2 %copy-start.26 = (f32[3]{0:T(128)S(1)}, f32[3]{0:T(128)}, u32[]{:S(2)}) copy-start(f32[3]{0:T(128)} %get-tuple-element.53) | copy-start | bytes 40
  415.4 567.7 %reduce-scatter.3.cloned.1.call-start = ((), (), s32[]{:S(2)}) async-start(), calls=%async_computation.8 | async-start | bytes 4866048 | tf_op jit(solution)/shard_map/reduce_scatter | solution.py:95
  445.3 4.3 copy-start.8
  445.3 4.3 copy-start.29
  449.6 106.0 %copy-start.13 = (f32[3,3072]{1,0:T(4,128)S(1)}, f32[3,3072]{1,0:T(4,128)}, u32[]{:S(2)}) copy-start(f32[3,3072]{1,0:T(4,128)} %copy-done.12) | copy-start | bytes 110596
  555.6 4.9 copy-start.10
Sparse Core Ops, SparseCore 0:
  11.5 95.8 all-gather.9
  127.3 49.3 all-gather.11
  180.1 91.2 all-gather.17
  274.8 90.1 all-gather.13
  366.6 34.2 all-gather.19
  402.5 42.7 all-gather.15
  451.4 265.3 reduce-scatter.4
  722.9 260.1 reduce-scatter.2
where the time goes:
time: 991 us; the launch traced here: 990 us
  waiting for transfers between devices  490 us (49%)
  blocking collectives  399 us (40%)
  matrix products  38.7 us (4%)
  other arithmetic  36 us (4%)
  between operations  14.7 us (1%)
  local copies, waits for them, and re-layouts  10.7 us (1%)
    reduce_scatter x2, waiting for transfers between devices, net_backward(): lax.psum_scatter(lax.dot_general(shaped, preact_grad, (((0,), (0,)), ((),...  419 us
    all_gather x3, blocking collectives, modulation_vectors(): gathered = lax.all_gather(partial_mods, 'fsdp', axis=1, tiled=True)  297 us
    psum x1, blocking collectives, shards(): gap_total = lax.psum(jnp.sum(distance, axis=(1, 2)), 'fsdp')  102 us
    all_gather x3, waiting for transfers between devices, net_forward(): lax.all_gather(activated, ('group', 'seq'), axis=1, tiled=True)  41 us
    all_gather x3, waiting for transfers between devices, net_forward(): lax.all_gather(w_proj, 'fsdp', axis=0, tiled=True)  29 us
  transfers between devices with their start and end apart: 8, of which 5 were waited for; matrix products, arithmetic and copies ran while one was open for 8% of the time, Pallas kernels for 0%

commit v1 on v0

v1 whole, which is shorter than its diff:
```python
import functools
import math

import jax
import jax.numpy as jnp
from jax import lax
from jax.experimental import pallas as pl
from jax.experimental.pallas import tpu as pltpu
from jax.sharding import Mesh
from jax.sharding import PartitionSpec as P

S = 4096
STEPS = 1000
D = 3072
C = 64
IMAGES = 3

norm_epsilon = 1e-06
gap_epsilon = 1e-05

F32 = jnp.float32
BF16 = jnp.bfloat16

XY = ("x", "y")
XHY = ("x", "h", "y")
COMBINE = ("h", "g", "s")
OWNERS = 16
TOKENS = 256
HALF = 128
OWNED = 16
ROWS = 96
WIDE = 128
NARROW = 64
COLS = WIDE + NARROW
PACKED = 864
BLOCK = 512

SWAP_H = [(0, 1), (1, 0)]


def params():
    return pltpu.CompilerParams(vmem_limit_bytes=56 * 1024 * 1024)


def smem():
    return pl.BlockSpec(memory_space=pltpu.SMEM)


def whole(shape):
    zeros = (0,) * len(shape)
    return pl.BlockSpec(shape, lambda *_: zeros)


def dot(a, b):
    return jnp.dot(a, b, preferred_element_type=F32)


def time_features(steps, embed_width):
    times = (steps.astype(F32) + 1.0) / (STEPS + 1.0)
    half = embed_width // 2
    frequency = jnp.exp(-jnp.log(10000.0) * jnp.arange(half, dtype=F32) / half)
    angles = 1000.0 * times[:, None] * frequency[None, :]
    embedding = jnp.concatenate([jnp.cos(angles), jnp.sin(angles)], axis=1)
    return (times, jax.nn.silu(embedding).astype(BF16))


def to_row(numbers):
    shape = (numbers[0].shape[0], OWNED, 128)
    lane = lax.broadcasted_iota(jnp.int32, shape, 2)
    token = lax.broadcasted_iota(jnp.int32, shape, 1)
    total = jnp.zeros(shape, F32)
    for k, number in enumerate(numbers):
        total = jnp.where(lane == token + OWNED * k, number, total)
    return jnp.sum(total, axis=1, keepdims=True)


def from_row(row, k):
    shape = (row.shape[0], OWNED, 128)
    lane = lax.broadcasted_iota(jnp.int32, shape, 2)
    token = lax.broadcasted_iota(jnp.int32, shape, 1)
    return jnp.sum(jnp.where(lane == token + OWNED * k, row, 0.0), axis=2, keepdims=True)


def local_lanes(load, place_ref):
    h = place_ref[0]
    tile = load(pl.ds(pl.multiple_of(place_ref[1], 128), 128))
    middle = load(pl.ds(pl.multiple_of(place_ref[2], 128), 128))
    part = jnp.where(h == 0, middle[:, :NARROW], middle[:, NARROW:])
    return jnp.concatenate([tile, part], axis=1)


def local_rows(final_ref, place_ref):
    tile = final_ref[pl.ds(pl.multiple_of(place_ref[1], 128), 128), :]
    part = final_ref[pl.ds(pl.multiple_of(place_ref[3], 64), NARROW), :]
    return jnp.concatenate([tile, part], axis=0)


def unpack_weights(packed_ref, net, w_ref):
    for chunk in range(16):
        x, y = chunk // 4, chunk % 4
        for h in range(2):
            k = (x * 8 + h * 4 + y) * ROWS
            w_ref[k : k + ROWS, :WIDE] = packed_ref[chunk, net * 192 + h * ROWS : net * 192 + (h + 1) * ROWS, :]
            if net < 2:
                part = packed_ref[chunk, 576 + h * ROWS : 576 + (h + 1) * ROWS, net * NARROW : (net + 1) * NARROW]
            else:
                part = packed_ref[chunk, 768:864, h * NARROW : (h + 1) * NARROW]
            w_ref[k : k + ROWS, WIDE:] = part


def forward(x, embed_ref, mods_ref, final_ref, w_ref, hidden_ref, shaped_ref, place_ref):
    sums = jnp.zeros((TOKENS, 128), F32)
    squares = jnp.zeros((TOKENS, 128), F32)
    for b in range(D // BLOCK):
        cut = slice(b * BLOCK, (b + 1) * BLOCK)
        hidden = dot(x, embed_ref[:, cut])
        hidden_ref[:, cut] = hidden
        for j in range(BLOCK // 128):
            piece = hidden[:, j * 128 : (j + 1) * 128]
            sums = sums + piece
            squares = squares + piece * piece
    average = jnp.sum(sums, axis=1, keepdims=True) / D
    square = jnp.sum(squares, axis=1, keepdims=True) / D
    inverse = lax.rsqrt(square - average * average + norm_epsilon)
    preactivation = jnp.zeros((TOKENS, COLS), F32)
    for b in range(D // BLOCK):
        cut = slice(b * BLOCK, (b + 1) * BLOCK)
        normed = (hidden_ref[:, cut] - average) * inverse
        shaped = (normed * (1.0 + mods_ref[0, 1:2, cut]) + mods_ref[0, 0:1, cut]).astype(BF16)
        shaped_ref[:, cut] = shaped
        preactivation = preactivation + dot(shaped, w_ref[cut, :])
    activated = jax.nn.gelu(preactivation, approximate=True).astype(BF16).astype(F32)
    own_hidden = dot(x, local_lanes(lambda at: embed_ref[:, at], place_ref))
    gate = local_lanes(lambda at: mods_ref[0, 2:3, at], place_ref)
    scale = local_lanes(lambda at: mods_ref[0, 4:5, at], place_ref)
    residual = own_hidden + gate * activated
    total = jnp.sum(residual, axis=1, keepdims=True)
    total_square = jnp.sum(residual * residual, axis=1, keepdims=True)
    own_mean = total / COLS
    final = local_rows(final_ref, place_ref)
    centred = ((residual - own_mean) * (1.0 + scale)).astype(BF16)
    ones = jnp.ones((8, COLS), BF16)
    column = dot(jnp.concatenate([ones, jnp.broadcast_to(scale, (8, COLS)).astype(BF16)], axis=0), final)
    column = column[0:1] + column[8:9]
    partial = dot(centred, final) + own_mean * column
    return preactivation, residual, partial, total, total_square


def owned(value):
    return value.reshape(OWNERS, OWNED, value.shape[-1])


def final_sums(mods_ref, final_ref):
    scales = [mods_ref[i, 4:5, :] for i in range(IMAGES)]
    shifts = [mods_ref[i, 3:4, :] for i in range(IMAGES)]
    left = jnp.concatenate(scales + shifts + [jnp.ones((2, D), F32)], axis=0).astype(BF16)
    sums = dot(left, final_ref[...])
    return [sums[i : i + 1] + sums[6:7] for i in range(IMAGES)], [sums[3 + i : 4 + i] for i in range(IMAGES)]


def pack_kernel(place_ref, *refs):
    mine, other, out_ref = refs[:3], refs[3], refs[4]
    h = place_ref[0]

    def half(block, which):
        return jnp.where(which == 0, block[:, :NARROW], block[:, NARROW:])

    tiles, parts = [], []
    for n in range(3):
        block = mine[n][...]
        tile = jnp.where(h == 0, block[:, :128], block[:, 256:])
        part = half(block[:, 128:256], h)
        sent = other[n]
        if n < 2:
            sent_part = other[3][:, n * NARROW : (n + 1) * NARROW]
        else:
            sent_part = other[4][:, :NARROW]
        tiles.append(jnp.where(h == 0, tile, sent))
        tiles.append(jnp.where(h == 0, sent, tile))
        parts.append((jnp.where(h == 0, part, sent_part), jnp.where(h == 0, sent_part, part)))
    low = jnp.concatenate([parts[0][0], parts[1][0]], axis=1)
    high = jnp.concatenate([parts[0][1], parts[1][1]], axis=1)
    last = jnp.concatenate([parts[2][0], parts[2][1]], axis=1)
    out_ref[0] = jnp.concatenate(tiles + [low, high, last], axis=0)


def generator_kernel(place_ref, own_ref, other_ref, embed_ref, mods_ref, final_ref, packed_ref,
                     part_ref, shaped_ref, pre_ref, res_ref, w_ref, hidden_ref):
    i = pl.program_id(0)
    h = place_ref[0]

    @pl.when(i == 0)
    def _():
        unpack_weights(packed_ref, 0, w_ref)
        part_ref[:, 24:32, :] = jnp.zeros((OWNERS, 8, 128), F32)

    own, other = own_ref[0], other_ref[0]
    x = jnp.concatenate([jnp.where(h == 0, own, other), jnp.where(h == 0, other, own)], axis=0)
    pre, res, partial, total, square = forward(
        x, embed_ref, mods_ref, final_ref, w_ref, hidden_ref, shaped_ref.at[0], place_ref
    )
    pre_ref[0] = pre
    res_ref[0] = res
    pieces = owned(partial)
    part_ref[:, pl.ds(pl.multiple_of(i * 8, 8), 8), :] = jnp.concatenate([pieces[:, :8], pieces[:, 8:]], axis=2)
    part_ref[:, pl.ds(24 + i, 1), :] = to_row([owned(total), owned(square)])


def samples_kernel(place_ref, time_ref, got_ref, noise_ref, mods_ref, final_ref,
                   out_ref, keep_ref, sums_ref):
    total = jnp.sum(got_ref[...], axis=0)
    scales, shifts = final_sums(mods_ref, final_ref)
    packed = []
    for i in range(IMAGES):
        block = total[8 * i : 8 * i + 8]
        partial = jnp.concatenate([block[:, :C], block[:, C:]], axis=0)
        row = total[24 + i : 25 + i][None]
        average = from_row(row, 0)[0] / D
        square = from_row(row, 1)[0] / D
        inverse = lax.rsqrt(square - average * average + norm_epsilon)
        inner = inverse * (partial - average * scales[i])
        velocity = inner + shifts[i]
        noise = noise_ref[i, pl.ds(pl.multiple_of(place_ref[4], 16), OWNED), :].astype(F32)
        samples = noise - time_ref[i] * velocity
        packed.append(jnp.concatenate([samples[:8], samples[8:]], axis=1))
        at = slice(i * OWNED, (i + 1) * OWNED)
        keep_ref[0, at, :] = samples
        keep_ref[1, at, :] = inner
        keep_ref[2, at, :] = jnp.broadcast_to(average, (OWNED, C))
        keep_ref[3, at, :] = jnp.broadcast_to(inverse, (OWNED, C))
    sums_ref[...] = jnp.concatenate(scales + [jnp.zeros((5, C), F32)], axis=0)
    out_ref[...] = jnp.broadcast_to(jnp.concatenate(packed, axis=0)[None], out_ref.shape)


def mix(samples, noise, t):
    return ((1.0 - t) * samples + t * noise).astype(BF16)


def score_kernel(place_ref, time_ref, got_ref, own_ref, other_ref,
                 t_embed_ref, f_embed_ref, t_mods_ref, f_mods_ref, t_final_ref, f_final_ref, packed_ref,
                 part_ref, samples_ref, shaped_ref, pre_ref, res_ref,
                 t_w_ref, f_w_ref, hidden_ref, t_shaped_ref):
    i = pl.program_id(0)
    h = place_ref[0]

    @pl.when(i == 0)
    def _():
        unpack_weights(packed_ref, 1, t_w_ref)
        unpack_weights(packed_ref, 2, f_w_ref)
        part_ref[:, 48:56, :] = jnp.zeros((OWNERS, 8, 128), F32)

    got = got_ref[:, pl.ds(pl.multiple_of(i * 8, 8), 8), :]
    samples = jnp.concatenate([got[:, :, :C], got[:, :, C:]], axis=1).reshape(TOKENS, C)
    samples_ref[0] = jnp.where(h == 0, samples[:HALF], samples[HALF:])
    own, other = own_ref[0].astype(F32), other_ref[0].astype(F32)
    noise = jnp.concatenate([jnp.where(h == 0, own, other), jnp.where(h == 0, other, own)], axis=0)
    noised = mix(samples, noise, time_ref[i])
    _, _, t_partial, t_total, t_square = forward(
        noised, t_embed_ref, t_mods_ref, t_final_ref, t_w_ref, hidden_ref, t_shaped_ref, place_ref
    )
    pre, res, f_partial, f_total, f_square = forward(
        noised, f_embed_ref, f_mods_ref, f_final_ref, f_w_ref, hidden_ref, shaped_ref.at[0], place_ref
    )
    pre_ref[0] = pre
    res_ref[0] = res
    part_ref[:, pl.ds(pl.multiple_of(i * 16, 16), 16), :] = owned(jnp.concatenate([t_partial, f_partial], axis=1))
    part_ref[:, pl.ds(48 + i, 1), :] = to_row([owned(v) for v in (t_total, t_square, f_total, f_square)])


def cotangent_kernel(place_ref, gen_time_ref, time_ref, got_ref, noise_ref, keep_ref, sums_ref,
                     t_mods_ref, f_mods_ref, t_final_ref, f_final_ref, out_ref):
    loss_scale = 1.0 / math.sqrt(IMAGES * S)
    total = jnp.sum(got_ref[...], axis=0)
    t_scales, t_shifts = final_sums(t_mods_ref, t_final_ref)
    f_scales, f_shifts = final_sums(f_mods_ref, f_final_ref)
    lane = lax.broadcasted_iota(jnp.int32, (1, 128), 1)
    cots, rows = [], []
    for i in range(IMAGES):
        block = total[16 * i : 16 * i + 16]
        row = total[48 + i : 49 + i][None]

        def inner(partial, k, scale):
            average = from_row(row, k)[0] / D
            square = from_row(row, k + 1)[0] / D
            inverse = lax.rsqrt(square - average * average + norm_epsilon)
            return inverse * (partial - average * scale), average, inverse

        t_inner, _, _ = inner(block[:, :C], 0, t_scales[i])
        f_inner, f_average, f_inverse = inner(block[:, C:], 2, f_scales[i])
        teacher, fake = t_inner + t_shifts[i], f_inner + f_shifts[i]
        at = slice(i * OWNED, (i + 1) * OWNED)
        samples, g_inner = keep_ref[0, at, :], keep_ref[1, at, :]
        g_average, g_inverse = keep_ref[2, at, 0:1], keep_ref[3, at, 0:1]
        noise = noise_ref[i, pl.ds(pl.multiple_of(place_ref[4], 16), OWNED), :].astype(F32)
        t = time_ref[i]
        noised = mix(samples, noise, t).astype(F32)
        distance = jnp.sum(jnp.abs(samples - noised + t * teacher))
        gen_cot = (-(gen_time_ref[i] * t * loss_scale) * (teacher - fake)).astype(BF16).astype(F32)
        fake_cot = (loss_scale * (fake - noise + samples)).astype(BF16).astype(F32)
        numbers = []
        for cot, column, value, average, inverse in (
            (fake_cot, f_scales[i], f_inner, f_average, f_inverse),
            (gen_cot, sums_ref[i : i + 1, :], g_inner, g_average, g_inverse),
        ):
            first = jnp.sum(cot * column, axis=1, keepdims=True) / D
            second = jnp.sum(cot * value, axis=1, keepdims=True) / D
            slope = inverse * inverse * second
            numbers += [inverse, slope, average * slope - inverse * first]
        cots.append(jnp.concatenate([fake_cot, gen_cot], axis=1))
        numbers_row = to_row([number[None] for number in numbers])[0]
        numbers_row = jnp.where(lane == 96, distance, numbers_row)
        for _ in range(3):
            rounded = numbers_row.astype(BF16).astype(F32)
            rows.append(rounded)
            numbers_row = numbers_row - rounded
    rows.append(jnp.zeros((7, 128), F32))
    packed = jnp.concatenate(cots + rows, axis=0).astype(BF16)
    out_ref[...] = jnp.broadcast_to(packed[None], out_ref.shape)


def gelu_slope(v):
    a, b = math.sqrt(2.0 / math.pi), 0.044715
    t = jnp.tanh(a * (v + b * (v * v * v)))
    return 0.5 * (1.0 + t) + 0.5 * v * (1.0 - t * t) * (a * (1.0 + 3.0 * b * (v * v)))


def gradient_kernel(place_ref, got_ref, gap_ref, f_mods_ref, g_mods_ref, f_final_ref, g_final_ref,
                    f_pre_ref, f_res_ref, g_pre_ref, g_res_ref, f_shaped_ref, g_shaped_ref,
                    out_ref, f_left_ref, g_left_ref):
    @pl.when(pl.program_id(0) == 0)
    def _():
        gaps = jnp.sum(gap_ref[...], axis=0)
        for i in range(IMAGES):
            inverse_gap = 1.0 / (gaps[i : i + 1, :] / (S * C) + gap_epsilon)
            inverse_gap = jnp.concatenate([inverse_gap, inverse_gap[:, :NARROW]], axis=1)
            cots = got_ref[:, 16 * i : 16 * i + 16, :].reshape(TOKENS, 128)
            row = got_ref[:, 48:64, :].astype(F32)
            row = row[:, 3 * i : 3 * i + 1] + row[:, 3 * i + 1 : 3 * i + 2] + row[:, 3 * i + 2 : 3 * i + 3]
            for net, (mods_ref, final_ref, pre_ref, res_ref, left_ref) in enumerate((
                (f_mods_ref, f_final_ref, f_pre_ref, f_res_ref, f_left_ref),
                (g_mods_ref, g_final_ref, g_pre_ref, g_res_ref, g_left_ref),
            )):
                inverse, slope, offset = [from_row(row, 3 * net + k).reshape(TOKENS, 1) for k in range(3)]
                final = local_rows(final_ref, place_ref)
                cot = cots[:, net * C : (net + 1) * C]
                out_grad = lax.dot_general(cot, final, (((1,), (1,)), ((), ())), preferred_element_type=F32)
                scale = local_lanes(lambda at: mods_ref[i, 4:5, at], place_ref)
                gate = local_lanes(lambda at: mods_ref[i, 2:3, at], place_ref)
                res_grad = inverse * (out_grad * (1.0 + scale)) - slope * res_ref[i] + offset
                act_grad = res_grad * gate
                if net == 1:
                    act_grad = act_grad * inverse_gap
                grad = act_grad * gelu_slope(pre_ref[i])
                turned = jnp.concatenate([grad, jnp.zeros((TOKENS, NARROW), F32)], axis=1).T
                left_ref[:, i * TOKENS : (i + 1) * TOKENS] = turned[:COLS].astype(BF16)

    f_grad = dot(f_left_ref[...], f_shaped_ref[...].reshape(IMAGES * TOKENS, 768))
    g_grad = dot(g_left_ref[...], g_shaped_ref[...].reshape(IMAGES * TOKENS, 768))
    narrow = jnp.concatenate([f_grad[WIDE:], g_grad[WIDE:]], axis=0)
    for n, block in enumerate((f_grad[:WIDE], g_grad[:WIDE], narrow)):
        turned = block.T.astype(BF16)
        for h in range(2):
            for y in range(4):
                k = (h * 4 + y) * ROWS
                out_ref[y, n, h * ROWS : (h + 1) * ROWS, :] = turned[k : k + ROWS]


def sum_kernel(place_ref, got_ref, keep_ref, send_ref):
    h = place_ref[0]
    total = got_ref[0, 0].astype(F32)
    for k in range(1, 16):
        total = total + got_ref[k, 0].astype(F32)
    keep_ref[0] = jnp.where(h == 0, total[:ROWS], total[ROWS:])
    send_ref[0] = jnp.where(h == 0, total[ROWS:], total[:ROWS])


def place_kernel(place_ref, keep_ref, other_ref, gen_ref, fake_ref):
    h = place_ref[0]

    def ordered(n):
        keep, other = keep_ref[n], other_ref[n]
        return jnp.where(h == 0, keep, other), jnp.where(h == 0, other, keep)

    low, high = ordered(2)
    for n, ref in enumerate((fake_ref, gen_ref)):
        first, last = ordered(n)
        part = slice(n * NARROW, (n + 1) * NARROW)
        ref[:, :128] = first
        ref[:, 128:256] = jnp.concatenate([low[:, part], high[:, part]], axis=1)
        ref[:, 256:] = last


def exchange(value, axes):
    return lax.all_to_all(value, axes, 0, 0)


def shards(
    gen_noise,
    score_noise,
    gen_steps,
    score_steps,
    gen_embed,
    gen_modulation,
    gen_proj,
    gen_final,
    teacher_embed,
    teacher_modulation,
    teacher_proj,
    teacher_final,
    fake_embed,
    fake_modulation,
    fake_proj,
    fake_final,
):
    h = lax.axis_index("h")
    member = lax.axis_index(("g", "s"))
    start = member * 384
    place = jnp.stack([h, start + 256 * h, start + 128, start + 128 + 64 * h, member * OWNED]).astype(jnp.int32)

    gen_time, gen_cond = time_features(gen_steps, gen_modulation.shape[0])
    score_time, score_cond = time_features(score_steps, gen_modulation.shape[0])
    own_mods = jnp.concatenate(
        [
            dot(gen_cond, gen_modulation),
            dot(score_cond, teacher_modulation),
            dot(score_cond, fake_modulation),
        ],
        axis=0,
    ).astype(BF16)
    mods = lax.all_gather(own_mods, XHY, axis=1, tiled=True)
    mods = jnp.pad(mods.astype(F32).reshape(9, 5, D), ((0, 0), (0, 3), (0, 0)))

    projections = (gen_proj, teacher_proj, fake_proj)
    sent = [jnp.where(h == 0, w[:, 256:], w[:, :128]) for w in projections]
    parts = [jnp.where(h == 0, w[:, 192:256], w[:, 128:192]) for w in projections]
    sent.append(jnp.concatenate(parts[:2], axis=1))
    sent.append(jnp.concatenate([parts[2], parts[2]], axis=1))
    other_w = lax.ppermute(jnp.stack(sent), "h", SWAP_H)
    other_noise = lax.ppermute(jnp.stack([gen_noise, score_noise]), "h", SWAP_H)

    packed = pl.pallas_call(
        pack_kernel,
        grid=(16,),
        in_specs=[smem()] + [whole((96, 384))] * 3 + [whole((5, 96, 128))],
        out_specs=pl.BlockSpec((1, PACKED, 128), lambda i: (i, 0, 0)),
        out_shape=jax.ShapeDtypeStruct((16, PACKED, 128), BF16),
        compiler_params=params(),
        name="pack",
    )(place, *projections, other_w)
    packed = exchange(packed, XY)

    by_image = lambda *shape: pl.BlockSpec((1, *shape), lambda i: (i,) + (0,) * len(shape))
    mods_of = lambda net: pl.BlockSpec((1, 8, D), lambda i: (3 * net + i, 0, 0))
    local = jax.ShapeDtypeStruct((IMAGES, TOKENS, COLS), F32)
    wide = jax.ShapeDtypeStruct((IMAGES, TOKENS, D), BF16)

    part, g_shaped, g_pre, g_res = pl.pallas_call(
        generator_kernel,
        grid=(IMAGES,),
        in_specs=[
            smem(), by_image(HALF, C), by_image(HALF, C), whole((C, D)), mods_of(0), whole((D, C)),
            whole((16, PACKED, 128)),
        ],
        out_specs=[whole((OWNERS, 32, 128)), by_image(TOKENS, D), by_image(TOKENS, COLS), by_image(TOKENS, COLS)],
        out_shape=[jax.ShapeDtypeStruct((OWNERS, 32, 128), F32), wide, local, local],
        scratch_shapes=[pltpu.VMEM((D, COLS), BF16), pltpu.VMEM((TOKENS, D), F32)],
        compiler_params=params(),
        name="generator",
    )(place, gen_noise, other_noise[0], gen_embed, mods, gen_final, packed)
    part = exchange(part, COMBINE)

    net_mods = lambda net: pl.BlockSpec((IMAGES, 8, D), lambda *_: (net, 0, 0))
    pack1, keep, sums = pl.pallas_call(
        samples_kernel,
        grid=(1,),
        in_specs=[
            smem(), smem(), whole((OWNERS, 32, 128)), whole((IMAGES, HALF, C)), net_mods(0), whole((D, C)),
        ],
        out_specs=[whole((OWNERS, 24, 128)), whole((4, 48, C)), whole((8, C))],
        out_shape=[
            jax.ShapeDtypeStruct((OWNERS, 24, 128), F32),
            jax.ShapeDtypeStruct((4, 48, C), F32),
            jax.ShapeDtypeStruct((8, C), F32),
        ],
        compiler_params=params(),
        name="samples",
    )(place, gen_time, part, gen_noise, mods, gen_final)
    pack1 = exchange(pack1, COMBINE)

    part2, samples, f_shaped, f_pre, f_res = pl.pallas_call(
        score_kernel,
        grid=(IMAGES,),
        in_specs=[
            smem(), smem(), whole((OWNERS, 24, 128)), by_image(HALF, C), by_image(HALF, C),
            whole((C, D)), whole((C, D)), mods_of(1), mods_of(2), whole((D, C)), whole((D, C)),
            whole((16, PACKED, 128)),
        ],
        out_specs=[
            whole((OWNERS, 56, 128)), by_image(HALF, C), by_image(TOKENS, D), by_image(TOKENS, COLS),
            by_image(TOKENS, COLS),
        ],
        out_shape=[
            jax.ShapeDtypeStruct((OWNERS, 56, 128), F32),
            jax.ShapeDtypeStruct((IMAGES, HALF, C), F32),
            wide, local, local,
        ],
        scratch_shapes=[
            pltpu.VMEM((D, COLS), BF16), pltpu.VMEM((D, COLS), BF16), pltpu.VMEM((TOKENS, D), F32),
            pltpu.VMEM((TOKENS, D), BF16),
        ],
        compiler_params=params(),
        name="score",
    )(place, score_time, pack1, score_noise, other_noise[1], teacher_embed, fake_embed, mods, mods,
      teacher_final, fake_final, packed)
    part2 = exchange(part2, COMBINE)

    pack2 = pl.pallas_call(
        cotangent_kernel,
        grid=(1,),
        in_specs=[
            smem(), smem(), smem(), whole((OWNERS, 56, 128)), whole((IMAGES, HALF, C)), whole((4, 48, C)),
            whole((8, C)), net_mods(1), net_mods(2), whole((D, C)), whole((D, C)),
        ],
        out_specs=whole((OWNERS, 64, 128)),
        out_shape=jax.ShapeDtypeStruct((OWNERS, 64, 128), BF16),
        compiler_params=params(),
        name="cotangents",
    )(place, gen_time, score_time, part2, score_noise, keep, sums, mods, mods, teacher_final, fake_final)
    pack2 = exchange(pack2, COMBINE)

    gap = jnp.sum(pack2[:, 48:57, 96].astype(F32).reshape(OWNERS, 3, 3), axis=(0, 2))
    gap = jnp.broadcast_to(jnp.pad(gap, (0, 5))[None, :, None], (16, 8, 128))
    gap = exchange(gap, XY)

    by_columns = pl.BlockSpec((IMAGES, TOKENS, 768), lambda x: (0, 0, x))
    grads = pl.pallas_call(
        gradient_kernel,
        grid=(4,),
        in_specs=[
            smem(), whole((OWNERS, 64, 128)), whole((16, 8, 128)), net_mods(2), net_mods(0), whole((D, C)),
            whole((D, C)), *([whole((IMAGES, TOKENS, COLS))] * 4), by_columns, by_columns,
        ],
        out_specs=pl.BlockSpec((4, 3, 192, 128), lambda x: (x, 0, 0, 0)),
        out_shape=jax.ShapeDtypeStruct((16, 3, 192, 128), BF16),
        scratch_shapes=[pltpu.VMEM((COLS, IMAGES * TOKENS), BF16)] * 2,
        compiler_params=params(),
        name="gradients",
    )(place, pack2, gap, mods, mods, fake_final, gen_final, f_pre, f_res, g_pre, g_res, f_shaped, g_shaped)
    grads = exchange(grads, XY)

    tile = jax.ShapeDtypeStruct((3, ROWS, 128), F32)
    tile_spec = pl.BlockSpec((1, ROWS, 128), lambda n: (n, 0, 0))
    kept, sent = pl.pallas_call(
        sum_kernel,
        grid=(3,),
        in_specs=[smem(), pl.BlockSpec((16, 1, 192, 128), lambda n: (0, n, 0, 0))],
        out_specs=[tile_spec, tile_spec],
        out_shape=[tile, tile],
        compiler_params=params(),
        name="add",
    )(place, grads)
    other = lax.ppermute(sent, "h", SWAP_H)
    gen_grad, fake_grad = pl.pallas_call(
        place_kernel,
        grid=(1,),
        in_specs=[smem(), whole((3, ROWS, 128)), whole((3, ROWS, 128))],
        out_specs=[whole((ROWS, 384))] * 2,
        out_shape=[jax.ShapeDtypeStruct((ROWS, 384), F32)] * 2,
        compiler_params=params(),
        name="place",
    )(place, kept, other)
    return (samples, gen_grad, fake_grad)


def solution(mesh):
    split = Mesh(mesh.devices.reshape(4, 4, 2, 4, 2), ("g", "x", "h", "y", "s"))
    tokens = P(None, XHY, None)
    columns = P(None, XHY)
    block = P(XHY, ("g", "s"))
    net = (P(), columns, block, P())
    return jax.shard_map(
        shards,
        mesh=split,
        in_specs=(tokens, tokens, P(), P(), *net, *net, *net),
        out_specs=(tokens, block, block),
        check_vma=False,
    )
```

time: 991 us -> 352 us (0.36)
  waiting for transfers between devices: 490 us -> 18.1 us
  blocking collectives: 399 us -> 232 us
  Pallas kernels: 0 us -> 58.9 us
  matrix products: 38.7 us -> 0.52 us
  other arithmetic: 36 us -> 6.93 us
  starting transfers between devices: 0.54 us -> 24.2 us
  between operations: 14.7 us -> 0.87 us
    reduce_scatter x2 -> x0, waiting for transfers between devices: 419 us -> none  [net_backward(): lax.psum_scatter(lax.dot_general(shaped, preact_grad, (((0,), (0,)), ((),...]
    all_gather x3 -> x1, blocking collectives: 297 us -> 120 us  [shards(): mods = lax.all_gather(own_mods, XHY, axis=1, tiled=True)]
    all_to_all x0 -> x5, blocking collectives: none -> 112 us  [exchange(): return lax.all_to_all(value, axes, 0, 0)]
    psum x1 -> x0, blocking collectives: 102 us -> none  [shards(): gap_total = lax.psum(jnp.sum(distance, axis=(1, 2)), 'fsdp')]
    all_gather x6 -> x0, waiting for transfers between devices: 70 us -> none  [the longest x3 41 us: net_forward(): lax.all_gather(activated, ('group', 'seq'), axis=1, tiled=True)]
    pallas_call x0 -> x8, Pallas kernels: none -> 58.9 us  [the longest x1 18.8 us: shards(): pl.pallas_call(score_kernel, grid=(IMAGES,), in_specs=[smem(), smem(), wh...]
    dot_general x16 -> x3, matrix products: 38.7 us -> 0.52 us  [dot(): return jnp.dot(a, b, preferred_element_type=F32)]
    ppermute x0 -> x3, starting transfers between devices: none -> 13 us  [the longest x1 7.83 us: shards(): other_w = lax.ppermute(jnp.stack(sent), 'h', SWAP_H)]
  transfers between devices with their start and end apart: 8 -> 5, of which waited for: 5 -> 3; matrix products, arithmetic and copies ran while one was open for 8% -> 3% of each run, Pallas kernels for 0% -> 0%
where the time goes in v1:
time: 352 us; the launch traced here: 351 us
  blocking collectives  232 us (66%)
  Pallas kernels  58.9 us (17%)
  starting transfers between devices  24.2 us (7%)
  waiting for transfers between devices  18.1 us (5%)
  local copies, waits for them, and re-layouts  9.28 us (3%)
  other arithmetic  6.93 us (2%)
    all_gather x1, blocking collectives, shards(): mods = lax.all_gather(own_mods, XHY, axis=1, tiled=True)  120 us
    all_to_all x5, blocking collectives, exchange(): return lax.all_to_all(value, axes, 0, 0)  112 us
    pallas_call x1, Pallas kernels, shards(): pl.pallas_call(score_kernel, grid=(IMAGES,), in_specs=[smem(), smem(), wh...  18.8 us
    all_to_all x2, starting transfers between devices, exchange(): return lax.all_to_all(value, axes, 0, 0)  11.2 us
    pallas_call x1, Pallas kernels, shards(): pl.pallas_call(generator_kernel, grid=(IMAGES,), in_specs=[smem(), by_ima...  11 us
    pallas_call x1, Pallas kernels, shards(): pl.pallas_call(gradient_kernel, grid=(4,), in_specs=[smem(), whole((OWNER...  10.3 us
    ppermute x1, waiting for transfers between devices, shards(): other = lax.ppermute(sent, 'h', SWAP_H)  9.15 us
    pallas_call x1, Pallas kernels, shards(): pl.pallas_call(pack_kernel, grid=(16,), in_specs=[smem()] + [whole((96, 3...  8.28 us
  transfers between devices with their start and end apart: 5, of which 3 were waited for; matrix products, arithmetic and copies ran while one was open for 3% of the time, Pallas kernels for 0%

profile of v1, /device:TPU:1, one launch (start us, length us, event | category | flops | bytes accessed | tf_op | source)
XLA Modules:
  0.0 350.9 jit_solution(6280336386576583287)
XLA Ops:
  0.6 0.0 copy-start
  0.7 0.9 slice_select_fusion.2
  1.5 0.8 bitcast_dynamic-update-slice_fusion.2
  2.3 0.9 slice_select_fusion
  3.2 0.8 bitcast_dynamic-update-slice_fusion.1
  4.0 0.8 bitcast_dynamic-update-slice_fusion
  4.8 0.1 fusion
  4.9 0.1 fusion.1
  5.0 7.8 %collective-permute-start.1 = (bf16[5,96,128]{2,1,0:T(8,128)(2,1)S(1)}, bf16[5,96,128]{2,1,0:T(8,128)(2,1)S(1)}, u32[]{:S(2)}, u32[]{:S(2)}) collective-permute-start(bf16[5,96,128]{2,1,0:T(8,128)(2,1)S(1)} %fusion.1), channel_id=1, source_target_pairs={{0,8},{8,0},{1,9},{9,1},{2,10},{10,2},{3,11},{11,3},{4,12},{12,4},... | collective-permute-start | bytes 368648 | tf_op jit(solution)/shard_map/ppermute | solution.py:438
  12.8 0.7 stack.50.place_ref
  13.4 1.7 collective-permute-done.1.refs_3_
  15.2 0.6 copy-done.12
  15.8 8.3 %pack.1 = bf16[16,864,128]{2,1,0:T(8,128)(2,1)} custom-call(s32[5]{0:T(128)} %stack.50.place_ref, bf16[96,384]{1,0:T(8,128)(2,1)} %refs_0_.1, bf16[96,384]{1,0:T(8,128)(2,1)} %refs_1_.1, bf16[96,384]{1,0:T(8,128)(2,1)} %refs_2_.1, bf16[5,96,128]{2,1,0:T(8,128)(2,1)} %copy-done.12), custom_call_target="tpu_custom_call" | custom-call | tf_op jit(solution)/shard_map/pack/pallas_call | solution.py:441
  24.1 0.0 copy-start.16
  24.1 0.0 copy-start.8
  24.1 0.0 copy-start.9
  24.1 7.6 %all-to-all-start = ((bf16[16,864,128]{2,1,0:T(8,128)(2,1)}), bf16[16,864,128]{2,1,0:T(8,128)(2,1)}, u32[]{:S(2)}, u32[]{:S(2)}) async-start(bf16[16,864,128]{2,1,0:T(8,128)(2,1)} %pack.1), calls=%async_computation | async-start | bytes 7077888 | tf_op jit(solution)/shard_map/all_to_all | solution.py:394
  31.8 0.0 copy-start.5
  31.8 0.1 copy.53.own_ref.noise_ref
  31.9 0.0 copy-start.2
  31.9 0.1 copy.51.own_ref.noise_ref
  32.1 5.1 %collective-permute-start = (bf16[2,3,128,64]{3,2,1,0:T(8,128)(2,1)S(1)}, bf16[2,3,128,64]{3,2,1,0:T(8,128)(2,1)S(1)}, u32[]{:S(2)}, u32[]{:S(2)}) collective-permute-start(bf16[2,3,128,64]{3,2,1,0:T(8,128)(2,1)S(1)} %pad_maximum_fusion), channel_id=1, source_target_pairs={{0,8},{8,0},{1,9},{9,1},{2,10},{10,2},{3,11},{11,3},{4,12},{12,4},... | collective-permute-start | bytes 294920 | tf_op jit(solution)/shard_map/ppermute | solution.py:439
  37.3 0.5 fusion.8
  37.8 0.6 fusion.6
  38.4 0.1 multiply_cosine_fusion.1
  38.5 0.2 convolution_convert_fusion
  38.7 0.2 convolution_convert_fusion.1
  38.9 0.2 convolution_convert_fusion.2
  39.1 119.9 %all-gather = bf16[32,480,9]{1,2,0:T(8,128)(2,1)S(1)} all-gather(bf16[1,480,9]{1,2,0:T(8,128)(2,1)S(1)} %maximum_bitcast_fusion.2), channel_id=1, replica_groups=mesh['g'=4,'x'=4,'h'=2,'y'=4,'s'=2] {'x','h','y'}, dimensions={0}, use_global_device_ids=true | all-gather | bytes 285120 | tf_op jit(solution)/shard_map/all_gather | solution.py:430
  158.9 0.2 copy.52
  159.1 0.6 reshape.25
  159.7 0.4 reshape.23
  160.2 1.0 pad_convert_fusion.mods_ref.t_mods_ref.f_mods_ref.g_mods_ref
  161.2 1.2 copy.54.final_ref.g_final_ref
  162.3 0.0 collective-permute-done
  162.3 0.7 slice_bitcast_fusion
  163.0 0.0 all-to-all-done.packed_ref
  163.0 0.0 copy-start.6
  163.0 0.0 copy-start.7
  163.1 11.0 %generator.1 = (f32[16,32,128]{2,1,0:T(8,128)}, bf16[3,256,3072]{2,1,0:T(8,128)(2,1)}, f32[3,256,192]{2,1,0:T(8,128)}, f32[3,256,192]{2,1,0:T(8,128)}) custom-call(s32[5]{0:T(128)} %stack.50.place_ref, bf16[3,128,64]{2,1,0:T(8,128)(2,1)} %copy-done.2, bf16[3,128,64]{2,1,0:T(8,128)(2,1)} %get-tuple-element.45.other_ref, bf16[64,3072]{1,0:T(8,128)(2,1)} %embed_ref.1, ...), custom_call_target="tpu_custom_call" | custom-call | tf_op jit(solution)/shard_map/generator/pallas_call | solution.py:457
  174.0 33.3 %all_to_all.35.got_ref = f32[16,32,128]{2,1,0:T(8,128)} all-to-all(f32[16,32,128]{2,1,0:T(8,128)} %get-tuple-element.19), channel_id=1, replica_groups=mesh['g'=4,'x'=4,'h'=2,'y'=4,'s'=2] {'h','g','s'}, dimensions={0} | all-to-all | bytes 524288 | tf_op jit(solution)/shard_map/all_to_all | solution.py:394
  207.3 2.4 samples.1
  209.7 3.6 %all-to-all-start.2 = ((f32[16,24,128]{2,1,0:T(8,128)}), f32[16,24,128]{2,1,0:T(8,128)S(1)}, u32[]{:S(2)}, u32[]{:S(2)}) async-start(f32[16,24,128]{2,1,0:T(8,128)} %get-tuple-element.20), calls=%async_computation.2 | async-start | bytes 393216 | tf_op jit(solution)/shard_map/all_to_all | solution.py:394
  213.3 1.2 copy.59.f_final_ref
  214.5 1.2 copy.58.t_final_ref
  215.6 7.2 %all-to-all-done.2.got_ref = f32[16,24,128]{2,1,0:T(8,128)S(1)} async-done(((f32[16,24,128]{2,1,0:T(8,128)}), f32[16,24,128]{2,1,0:T(8,128)S(1)}, u32[]{:S(2)}, u32[]{:S(2)}) %all-to-all-start.2) | async-done | bytes 196640 | tf_op jit(solution)/shard_map/all_to_all | solution.py:394
  222.8 0.7 copy-done.4
  223.5 18.8 %score.1 = (f32[16,56,128]{2,1,0:T(8,128)}, f32[3,128,64]{2,1,0:T(8,128)}, bf16[3,256,3072]{2,1,0:T(8,128)(2,1)}, f32[3,256,192]{2,1,0:T(8,128)}, f32[3,256,192]{2,1,0:T(8,128)}) custom-call(s32[5]{0:T(128)} %stack.50.place_ref, f32[3]{0:T(128)} %get-tuple-element.55.time_ref, f32[16,24,128]{2,1,0:T(8,128)} %copy-done.4, bf16[3,128,64]{2,1,0:T(8,128)(2,1)} %copy-done.1, ...), custom_call_target="tpu_custom_call" | custom-call | tf_op jit(solution)/shard_map/score/pallas_call | solution.py:490
  242.3 19.9 %all_to_all.36.got_ref = f32[16,56,128]{2,1,0:T(8,128)} all-to-all(f32[16,56,128]{2,1,0:T(8,128)} %get-tuple-element.22), channel_id=1, replica_groups=mesh['g'=4,'x'=4,'h'=2,'y'=4,'s'=2] {'h','g','s'}, dimensions={0} | all-to-all | bytes 917504 | tf_op jit(solution)/shard_map/all_to_all | solution.py:394
  262.2 3.2 cotangents.1
  265.5 14.5 %all_to_all.37.got_ref = bf16[16,64,128]{2,1,0:T(8,128)(2,1)S(1)} all-to-all(bf16[16,64,128]{2,1,0:T(8,128)(2,1)} %cotangents.1), channel_id=1, replica_groups=mesh['g'=4,'x'=4,'h'=2,'y'=4,'s'=2] {'h','g','s'}, dimensions={0} | all-to-all | bytes 524288 | tf_op jit(solution)/shard_map/all_to_all | solution.py:394
  280.0 0.2 convert_reduce_fusion
  280.2 0.1 reduce_sum.14
  280.3 0.1 reduce_sum.18
  280.4 0.1 broadcast_in_dim.2
  280.5 10.0 %all_to_all.38.gap_ref = f32[16,8,128]{2,1,0:T(8,128)} all-to-all(f32[16,8,128]{2,1,0:T(8,128)S(1)} %broadcast_in_dim.2), channel_id=1, replica_groups=mesh['g'=4,'x'=4,'h'=2,'y'=4,'s'=2] {'x','y'}, dimensions={0} | all-to-all | bytes 131072 | tf_op jit(solution)/shard_map/all_to_all | solution.py:394
  290.5 10.3 %gradients.1 = bf16[16,3,192,128]{3,2,1,0:T(8,128)(2,1)} custom-call(s32[5]{0:T(128)} %stack.50.place_ref, bf16[16,64,128]{2,1,0:T(8,128)(2,1)} %copy-done.3, f32[16,8,128]{2,1,0:T(8,128)} %all_to_all.38.gap_ref, f32[9,8,3072]{2,1,0:T(8,128)} %pad_convert_fusion.mods_ref.t_mods_ref.f_mods_ref.g_mods_ref, ...), custom_call_target="tpu_custom_call" | custom-call | tf_op jit(solution)/shard_map/gradients/pallas_call | solution.py:536
  300.8 34.5 %all_to_all.39.got_ref = bf16[16,3,192,128]{3,2,1,0:T(8,128)(2,1)} all-to-all(bf16[16,3,192,128]{3,2,1,0:T(8,128)(2,1)} %gradients.1), channel_id=1, replica_groups=mesh['g'=4,'x'=4,'h'=2,'y'=4,'s'=2] {'x','y'}, dimensions={0} | all-to-all | bytes 4718592 | tf_op jit(solution)/shard_map/all_to_all | solution.py:394
  335.3 3.3 add.58
  338.5 0.0 collective-permute-start.2
  338.6 0.8 copy.65
  339.3 9.2 %collective-permute-done.2.other_ref = f32[3,96,128]{2,1,0:T(8,128)S(1)} collective-permute-done((f32[3,96,128]{2,1,0:T(8,128)}, f32[3,96,128]{2,1,0:T(8,128)S(1)}, u32[]{:S(2)}, u32[]{:S(2)}) %collective-permute-start.2) | collective-permute-done | bytes 147488 | tf_op jit(solution)/shard_map/ppermute | solution.py:562
  348.5 0.7 copy-done.11
  349.1 1.8 place.1
  (27 shorter events, 0.1 us)
Async XLA Ops:
  0.6 37.9 %copy-start = (bf16[256,480]{0,1:T(8,128)(2,1)S(1)}, bf16[256,480]{0,1:T(8,128)(2,1)}, u32[]{:S(2)}) copy-start(bf16[256,480]{0,1:T(8,128)(2,1)} %param.29) | copy-start | bytes 737284
  5.0 10.2 %collective-permute-start.1 = (bf16[5,96,128]{2,1,0:T(8,128)(2,1)S(1)}, bf16[5,96,128]{2,1,0:T(8,128)(2,1)S(1)}, u32[]{:S(2)}, u32[]{:S(2)}) collective-permute-start(bf16[5,96,128]{2,1,0:T(8,128)(2,1)S(1)} %fusion.1), channel_id=1, source_target_pairs={{0,8},{8,0},{1,9},{9,1},{2,10},{10,2},{3,11},{11,3},{4,12},{12,4},... | collective-permute-start | bytes 368648 | tf_op jit(solution)/shard_map/ppermute | solution.py:438
  15.2 0.6 copy-start.12
  24.1 7.7 %copy-start.13 = (bf16[3,128,64]{1,2,0:T(8,128)(2,1)S(1)}, bf16[3,128,64]{1,2,0:T(8,128)(2,1)}, u32[]{:S(2)}) copy-start(bf16[3,128,64]{1,2,0:T(8,128)(2,1)} %param.16) | copy-start | bytes 147460
  24.1 7.8 %copy-start.14 = (bf16[3,128,64]{1,2,0:T(8,128)(2,1)S(1)}, bf16[3,128,64]{1,2,0:T(8,128)(2,1)}, u32[]{:S(2)}) copy-start(bf16[3,128,64]{1,2,0:T(8,128)(2,1)} %param.17) | copy-start | bytes 147460
  24.1 13.2 %copy-start.15 = (s32[3]{0:T(128)S(1)}, s32[3]{0:T(128)}, u32[]{:S(2)}) copy-start(s32[3]{0:T(128)} %param.18) | copy-start | bytes 40
  24.1 13.7 %copy-start.16 = (s32[3]{0:T(128)S(1)}, s32[3]{0:T(128)}, u32[]{:S(2)}) copy-start(s32[3]{0:T(128)} %param.19) | copy-start | bytes 40
  24.1 14.6 %copy-start.8 = (bf16[256,480]{0,1:T(8,128)(2,1)S(1)}, bf16[256,480]{0,1:T(8,128)(2,1)}, u32[]{:S(2)}) copy-start(bf16[256,480]{0,1:T(8,128)(2,1)} %param.25) | copy-start | bytes 737284
  24.1 14.7 %copy-start.9 = (bf16[256,480]{0,1:T(8,128)(2,1)S(1)}, bf16[256,480]{0,1:T(8,128)(2,1)}, u32[]{:S(2)}) copy-start(bf16[256,480]{0,1:T(8,128)(2,1)} %param.21) | copy-start | bytes 737284
  24.1 138.9 %all-to-all-start = ((bf16[16,864,128]{2,1,0:T(8,128)(2,1)}), bf16[16,864,128]{2,1,0:T(8,128)(2,1)}, u32[]{:S(2)}, u32[]{:S(2)}) async-start(bf16[16,864,128]{2,1,0:T(8,128)(2,1)} %pack.1), calls=%async_computation | async-start | bytes 7077888 | tf_op jit(solution)/shard_map/all_to_all | solution.py:394
  31.8 129.4 %copy-start.5 = (bf16[3072,64]{0,1:T(8,128)(2,1)S(1)}, bf16[3072,64]{0,1:T(8,128)(2,1)}, u32[]{:S(2)}) copy-start(bf16[3072,64]{0,1:T(8,128)(2,1)} %param.23) | copy-start | bytes 1179652
  31.9 131.1 %copy-start.2 = (bf16[3,128,64]{2,1,0:T(8,128)(2,1)}, bf16[3,128,64]{2,1,0:T(8,128)(2,1)S(1)}, u32[]{:S(2)}) copy-start(bf16[3,128,64]{2,1,0:T(8,128)(2,1)S(1)} %copy.53.own_ref.noise_ref) | copy-start | bytes 147460
  32.1 131.0 %copy-start.1 = (bf16[3,128,64]{2,1,0:T(8,128)(2,1)}, bf16[3,128,64]{2,1,0:T(8,128)(2,1)S(1)}, u32[]{:S(2)}) copy-start(bf16[3,128,64]{2,1,0:T(8,128)(2,1)S(1)} %copy.51.own_ref.noise_ref) | copy-start | bytes 147460
  32.1 130.2 %collective-permute-start = (bf16[2,3,128,64]{3,2,1,0:T(8,128)(2,1)S(1)}, bf16[2,3,128,64]{3,2,1,0:T(8,128)(2,1)S(1)}, u32[]{:S(2)}, u32[]{:S(2)}) collective-permute-start(bf16[2,3,128,64]{3,2,1,0:T(8,128)(2,1)S(1)} %pad_maximum_fusion), channel_id=1, source_target_pairs={{0,8},{8,0},{1,9},{9,1},{2,10},{10,2},{3,11},{11,3},{4,12},{12,4},... | collective-permute-start | bytes 294920 | tf_op jit(solution)/shard_map/ppermute | solution.py:439
  163.0 50.3 %copy-start.6 = (bf16[3072,64]{0,1:T(8,128)(2,1)S(1)}, bf16[3072,64]{0,1:T(8,128)(2,1)}, u32[]{:S(2)}) copy-start(bf16[3072,64]{0,1:T(8,128)(2,1)} %param.31) | copy-start | bytes 1179652
  163.0 51.4 %copy-start.7 = (bf16[3072,64]{0,1:T(8,128)(2,1)S(1)}, bf16[3072,64]{0,1:T(8,128)(2,1)}, u32[]{:S(2)}) copy-start(bf16[3072,64]{0,1:T(8,128)(2,1)} %param.27) | copy-start | bytes 1179652
  209.7 13.2 %all-to-all-start.2 = ((f32[16,24,128]{2,1,0:T(8,128)}), f32[16,24,128]{2,1,0:T(8,128)S(1)}, u32[]{:S(2)}, u32[]{:S(2)}) async-start(f32[16,24,128]{2,1,0:T(8,128)} %get-tuple-element.20), calls=%async_computation.2 | async-start | bytes 393216 | tf_op jit(solution)/shard_map/all_to_all | solution.py:394
  222.8 0.7 copy-start.4
  280.0 10.5 %copy-start.3 = (bf16[16,64,128]{2,1,0:T(8,128)(2,1)}, bf16[16,64,128]{2,1,0:T(8,128)(2,1)S(1)}, u32[]{:S(2)}) copy-start(bf16[16,64,128]{2,1,0:T(8,128)(2,1)S(1)} %all_to_all.37.got_ref) | copy-start | bytes 786436
  300.8 37.8 %copy-start.10 = (f32[3,128,64]{2,1,0:T(8,128)S(1)}, f32[3,128,64]{2,1,0:T(8,128)}, u32[]{:S(2)}) copy-start(f32[3,128,64]{2,1,0:T(8,128)} %get-tuple-element.41) | copy-start | bytes 294916
  338.5 9.9 %collective-permute-start.2 = (f32[3,96,128]{2,1,0:T(8,128)}, f32[3,96,128]{2,1,0:T(8,128)S(1)}, u32[]{:S(2)}, u32[]{:S(2)}) collective-permute-start(f32[3,96,128]{2,1,0:T(8,128)} %get-tuple-element.32), channel_id=1, source_target_pairs={{0,8},{8,0},{1,9},{9,1},{2,10},{10,2},{3,11},{11,3},{4,12},{12,4},... | collective-permute-start | bytes 442376 | tf_op jit(solution)/shard_map/ppermute | solution.py:562
  348.5 0.7 copy-start.11

commit v2 on v1

v2 whole, which is shorter than its diff:
```python
import functools
import math

import jax
import jax.numpy as jnp
from jax import lax
from jax.experimental import pallas as pl
from jax.experimental.pallas import tpu as pltpu
from jax.sharding import Mesh
from jax.sharding import PartitionSpec as P

S = 4096
STEPS = 1000
D = 3072
C = 64
IMAGES = 3

norm_epsilon = 1e-06
gap_epsilon = 1e-05

F32 = jnp.float32
BF16 = jnp.bfloat16

GATHER = ("x", "w")
ROW_AXES = ("x", "h", "v", "w")
COMBINE = ("v", "h", "g")
TOKEN_AXES = ("x", "w", "s")
OWNERS = 16
TOKENS = 256
HALF = 128
OWNED = 16
ROWS = 96
WIDE = 128
NARROW = 64
COLS = WIDE + NARROW
GEN_ROWS = 288
NOISE_ROWS = 384
MODS_AT = 864
MODS_ROWS = 36
SENT_ROWS = 912
GEN_CHUNK = 368
SCORE_ROWS = 576
CHUNKS = 8
BLOCK = 512

PLACES = ("h", "v", "s")
SWAP = [(h * 4 + v * 2 + s, s * 4 + v * 2 + h) for h in range(2) for v in range(2) for s in range(2)]
SWAP_TURNED = [(h * 4 + v * 2 + s, s * 4 + (1 - v) * 2 + h) for h in range(2) for v in range(2) for s in range(2)]
SIBLING = [(0, 1), (1, 0)]


def params(mib):
    return pltpu.CompilerParams(vmem_limit_bytes=mib * 1024 * 1024)


def smem():
    return pl.BlockSpec(memory_space=pltpu.SMEM)


def whole(shape):
    zeros = (0,) * len(shape)
    return pl.BlockSpec(shape, lambda *_: zeros)


def dot(a, b):
    return jnp.dot(a, b, preferred_element_type=F32)


def dot_turned(a, b):
    return lax.dot_general(a, b, (((1,), (1,)), ((), ())), preferred_element_type=F32)


def time_features(steps, embed_width):
    times = (steps.astype(F32) + 1.0) / (STEPS + 1.0)
    half = embed_width // 2
    frequency = jnp.exp(-jnp.log(10000.0) * jnp.arange(half, dtype=F32) / half)
    angles = 1000.0 * times[:, None] * frequency[None, :]
    embedding = jnp.concatenate([jnp.cos(angles), jnp.sin(angles)], axis=1)
    return (times, jax.nn.silu(embedding).astype(BF16))


def to_row(numbers):
    shape = (numbers[0].shape[0], OWNED, 128)
    lane = lax.broadcasted_iota(jnp.int32, shape, 2)
    token = lax.broadcasted_iota(jnp.int32, shape, 1)
    total = jnp.zeros(shape, F32)
    for k, number in enumerate(numbers):
        total = jnp.where(lane == token + OWNED * k, number, total)
    return jnp.sum(total, axis=1, keepdims=True)


def from_row(row, k):
    shape = (row.shape[0], OWNED, 128)
    lane = lax.broadcasted_iota(jnp.int32, shape, 2)
    token = lax.broadcasted_iota(jnp.int32, shape, 1)
    return jnp.sum(jnp.where(lane == token + OWNED * k, row, 0.0), axis=2, keepdims=True)


def local_lanes(load, place_ref):
    tile = load(pl.ds(pl.multiple_of(place_ref[1], 128), 128))
    middle = load(pl.ds(pl.multiple_of(place_ref[2], 128), 128))
    part = jnp.where(place_ref[0] == 0, middle[:, :NARROW], middle[:, NARROW:])
    return jnp.concatenate([tile, part], axis=1)


def unpack_weights(place_ref, own_ref, other_ref, net, w_ref):
    s = place_ref[4]
    for packed_ref, side in ((own_ref, s), (other_ref, 1 - s)):
        for chunk in range(CHUNKS):
            x, w = chunk // 2, chunk % 2
            for v in range(2):
                k = pl.multiple_of((x * 8 + v * 2 + w) * ROWS + side * (4 * ROWS), 32)
                first = max(net - 1, 0) * 192 + v * ROWS
                w_ref[pl.ds(k, ROWS), :WIDE] = packed_ref[chunk, first : first + ROWS, :]
                if net == 0:
                    part = packed_ref[chunk, 192:288, v * NARROW : (v + 1) * NARROW]
                else:
                    part = packed_ref[chunk, 384 + v * ROWS : 384 + (v + 1) * ROWS, (net - 1) * NARROW : net * NARROW]
                w_ref[pl.ds(k, ROWS), WIDE:] = part


def forward(x, embed_ref, mods_ref, final_ref, w_ref, hidden_ref, shaped_ref, place_ref):
    sums = jnp.zeros((TOKENS, 128), F32)
    squares = jnp.zeros((TOKENS, 128), F32)
    for b in range(D // BLOCK):
        cut = slice(b * BLOCK, (b + 1) * BLOCK)
        hidden = dot(x, embed_ref[:, cut])
        hidden_ref[:, cut] = hidden
        for j in range(BLOCK // 128):
            piece = hidden[:, j * 128 : (j + 1) * 128]
            sums = sums + piece
            squares = squares + piece * piece
    average = jnp.sum(sums, axis=1, keepdims=True) / D
    square = jnp.sum(squares, axis=1, keepdims=True) / D
    inverse = lax.rsqrt(square - average * average + norm_epsilon)
    preactivation = jnp.zeros((TOKENS, COLS), F32)
    for b in range(D // BLOCK):
        cut = slice(b * BLOCK, (b + 1) * BLOCK)
        normed = (hidden_ref[:, cut] - average) * inverse
        shaped = (normed * (1.0 + mods_ref[0, 1:2, cut]) + mods_ref[0, 0:1, cut]).astype(BF16)
        shaped_ref[:, cut] = shaped
        preactivation = preactivation + dot(shaped, w_ref[cut, :])
    activated = jax.nn.gelu(preactivation, approximate=True).astype(BF16).astype(F32)
    own_hidden = dot(x, local_lanes(lambda at: embed_ref[:, at], place_ref))
    gate = local_lanes(lambda at: mods_ref[0, 2:3, at], place_ref)
    scale = local_lanes(lambda at: mods_ref[0, 4:5, at], place_ref)
    residual = own_hidden + gate * activated
    total = jnp.sum(residual, axis=1, keepdims=True)
    total_square = jnp.sum(residual * residual, axis=1, keepdims=True)
    own_mean = total / COLS
    final = local_lanes(lambda at: final_ref[:, at], place_ref)
    centred = ((residual - own_mean) * (1.0 + scale)).astype(BF16)
    ones = jnp.ones((8, COLS), BF16)
    column = dot_turned(jnp.concatenate([ones, jnp.broadcast_to(scale, (8, COLS)).astype(BF16)], axis=0), final)
    column = column[0:1] + column[8:9]
    partial = dot_turned(centred, final) + own_mean * column
    return preactivation, residual, partial, total, total_square


def owned(value):
    return value.reshape(OWNERS, OWNED, value.shape[-1])


def final_sums(mods_ref, final_ref):
    scales = [mods_ref[i, 4:5, :] for i in range(IMAGES)]
    shifts = [mods_ref[i, 3:4, :] for i in range(IMAGES)]
    left = jnp.concatenate(scales + shifts + [jnp.ones((2, D), F32)], axis=0).astype(BF16)
    sums = dot_turned(left, final_ref[...])
    return [sums[i : i + 1] + sums[6:7] for i in range(IMAGES)], [sums[3 + i : 4 + i] for i in range(IMAGES)]


def split_kernel(place_ref, cond_ref, gen_noise_ref, score_noise_ref, gen_ref, teacher_ref, fake_ref,
                 gen_mod_ref, teacher_mod_ref, fake_mod_ref, mine_ref, other_ref):
    for i in range(IMAGES):
        noise = jnp.concatenate([gen_noise_ref[i], score_noise_ref[i]], axis=0).astype(F32).T.astype(BF16)
        mine_ref[i * HALF : (i + 1) * HALF] = noise
        other_ref[i * HALF : (i + 1) * HALF] = noise
    cond = cond_ref[...]
    mods = [dot_turned(cond, ref[...]) for ref in (gen_mod_ref, teacher_mod_ref, fake_mod_ref)]
    mods = jnp.concatenate([mods[0][0:3], mods[1][3:6], mods[2][3:6]], axis=0)
    mods = jnp.concatenate([mods, jnp.zeros((9, 32), F32)], axis=1)
    mods = jnp.concatenate([mods[:, 128 * p : 128 * (p + 1)] for p in range(4)] + [jnp.zeros((12, 128), F32)], axis=0)
    mine_ref[MODS_AT:] = mods.astype(BF16)
    other_ref[MODS_AT:] = mods.astype(BF16)
    first = place_ref[0] == 0
    mine, other = [], []
    for n, ref in enumerate((gen_ref, teacher_ref, fake_ref)):
        rows = slice(NOISE_ROWS + n * ROWS, NOISE_ROWS + (n + 1) * ROWS)
        low, high = ref[:, :128], ref[:, 256:]
        mine_ref[rows] = jnp.where(first, low, high)
        other_ref[rows] = jnp.where(first, high, low)
        low, high = ref[:, 128:192], ref[:, 192:256]
        mine.append(jnp.where(first, low, high))
        other.append(jnp.where(first, high, low))
    for ref, parts in ((mine_ref, mine), (other_ref, other)):
        ref[NOISE_ROWS + 3 * ROWS : NOISE_ROWS + 4 * ROWS] = jnp.concatenate(parts[1:], axis=1)
        ref[NOISE_ROWS + 4 * ROWS : MODS_AT] = jnp.concatenate([parts[0], parts[0]], axis=1)


def in_order(v, mine, other):
    return jnp.where(v == 0, mine, other), jnp.where(v == 0, other, mine)


def pack_kernel(place_ref, mine_ref, other_ref, gen_ref, score_ref):
    v = place_ref[0]
    cuts = [slice(NOISE_ROWS + n * ROWS, NOISE_ROWS + (n + 1) * ROWS) for n in range(5)]
    ordered = [in_order(v, mine_ref[rows], other_ref[rows]) for rows in cuts]
    parts = jnp.concatenate([ordered[4][0][:, :NARROW], ordered[4][1][:, :NARROW]], axis=1)
    mods = in_order(v, mine_ref[MODS_AT:].astype(F32), other_ref[MODS_AT:].astype(F32))
    mods = jnp.concatenate([mods[0][:MODS_ROWS], mods[1][:MODS_ROWS], jnp.zeros((8, 128), F32)], axis=0)
    gen = jnp.concatenate([*ordered[0], parts, mods.astype(BF16)], axis=0)
    score = jnp.concatenate([*ordered[1], *ordered[2], *ordered[3]], axis=0)
    for k in range(CHUNKS):
        gen_ref[k] = gen
        score_ref[k] = score


def generator_kernel(place_ref, own_ref, other_ref, embed_ref, mods_ref, final_ref, own_w_ref, other_w_ref,
                     part_ref, shaped_ref, pre_ref, res_ref, w_ref, hidden_ref):
    i = pl.program_id(0)
    v = place_ref[0]

    @pl.when(i == 0)
    def _():
        unpack_weights(place_ref, own_w_ref, other_w_ref, 0, w_ref)
        part_ref[:, 24:32, :] = jnp.zeros((OWNERS, 8, 128), F32)

    x = jnp.concatenate(in_order(v, own_ref[:, :C], other_ref[:, :C]), axis=0)
    pre, res, partial, total, square = forward(
        x, embed_ref, mods_ref, final_ref, w_ref, hidden_ref, shaped_ref.at[0], place_ref
    )
    pre_ref[0] = pre
    res_ref[0] = res
    pieces = owned(partial)
    part_ref[:, pl.ds(pl.multiple_of(i * 8, 8), 8), :] = jnp.concatenate([pieces[:, :8], pieces[:, 8:]], axis=2)
    part_ref[:, pl.ds(24 + i, 1), :] = to_row([owned(total), owned(square)])


def samples_kernel(place_ref, time_ref, got_ref, noise_ref, mods_ref, final_ref,
                   out_ref, keep_ref, sums_ref):
    total = jnp.sum(got_ref[...], axis=0)
    scales, shifts = final_sums(mods_ref, final_ref)
    packed = []
    for i in range(IMAGES):
        block = total[8 * i : 8 * i + 8]
        partial = jnp.concatenate([block[:, :C], block[:, C:]], axis=0)
        row = total[24 + i : 25 + i][None]
        average = from_row(row, 0)[0] / D
        square = from_row(row, 1)[0] / D
        inverse = lax.rsqrt(square - average * average + norm_epsilon)
        inner = inverse * (partial - average * scales[i])
        velocity = inner + shifts[i]
        noise = noise_ref[pl.ds(pl.multiple_of(place_ref[3] + i * HALF, 16), OWNED), :][:, :C].astype(F32)
        samples = noise - time_ref[i] * velocity
        packed.append(jnp.concatenate([samples[:8], samples[8:]], axis=1))
        at = slice(i * OWNED, (i + 1) * OWNED)
        keep_ref[0, at, :] = samples
        keep_ref[1, at, :] = inner
        keep_ref[2, at, :] = jnp.broadcast_to(average, (OWNED, C))
        keep_ref[3, at, :] = jnp.broadcast_to(inverse, (OWNED, C))
    sums_ref[...] = jnp.concatenate(scales + [jnp.zeros((5, C), F32)], axis=0)
    out_ref[...] = jnp.broadcast_to(jnp.concatenate(packed, axis=0)[None], out_ref.shape)


def mix(samples, noise, t):
    return ((1.0 - t) * samples + t * noise).astype(BF16)


def score_kernel(place_ref, time_ref, got_ref, own_ref, other_ref,
                 t_embed_ref, f_embed_ref, t_mods_ref, f_mods_ref, t_final_ref, f_final_ref, own_w_ref, other_w_ref,
                 part_ref, samples_ref, shaped_ref, pre_ref, res_ref,
                 t_w_ref, f_w_ref, hidden_ref, t_shaped_ref):
    i = pl.program_id(0)
    v = place_ref[0]

    @pl.when(i == 0)
    def _():
        unpack_weights(place_ref, own_w_ref, other_w_ref, 1, t_w_ref)
        unpack_weights(place_ref, own_w_ref, other_w_ref, 2, f_w_ref)
        part_ref[:, 48:56, :] = jnp.zeros((OWNERS, 8, 128), F32)

    got = got_ref[:, pl.ds(pl.multiple_of(i * 8, 8), 8), :]
    samples = jnp.concatenate([got[:, :, :C], got[:, :, C:]], axis=1).reshape(TOKENS, C)
    turned = jnp.concatenate([samples[:HALF], samples[HALF:]], axis=1).T
    samples_ref[0] = jnp.where(v == 0, turned[:C], turned[C:])
    own, other = own_ref[:, C:].astype(F32), other_ref[:, C:].astype(F32)
    noise = jnp.concatenate(in_order(v, own, other), axis=0)
    noised = mix(samples, noise, time_ref[i])
    _, _, t_partial, t_total, t_square = forward(
        noised, t_embed_ref, t_mods_ref, t_final_ref, t_w_ref, hidden_ref, t_shaped_ref, place_ref
    )
    pre, res, f_partial, f_total, f_square = forward(
        noised, f_embed_ref, f_mods_ref, f_final_ref, f_w_ref, hidden_ref, shaped_ref.at[0], place_ref
    )
    pre_ref[0] = pre
    res_ref[0] = res
    part_ref[:, pl.ds(pl.multiple_of(i * 16, 16), 16), :] = owned(jnp.concatenate([t_partial, f_partial], axis=1))
    part_ref[:, pl.ds(48 + i, 1), :] = to_row([owned(v) for v in (t_total, t_square, f_total, f_square)])


def cotangent_kernel(place_ref, gen_time_ref, time_ref, got_ref, noise_ref, keep_ref, sums_ref,
                     t_mods_ref, f_mods_ref, t_final_ref, f_final_ref, out_ref):
    loss_scale = 1.0 / math.sqrt(IMAGES * S)
    total = jnp.sum(got_ref[...], axis=0)
    t_scales, t_shifts = final_sums(t_mods_ref, t_final_ref)
    f_scales, f_shifts = final_sums(f_mods_ref, f_final_ref)
    lane = lax.broadcasted_iota(jnp.int32, (1, 128), 1)
    cots, rows = [], []
    for i in range(IMAGES):
        block = total[16 * i : 16 * i + 16]
        row = total[48 + i : 49 + i][None]

        def inner(partial, k, scale):
            average = from_row(row, k)[0] / D
            square = from_row(row, k + 1)[0] / D
            inverse = lax.rsqrt(square - average * average + norm_epsilon)
            return inverse * (partial - average * scale), average, inverse

        t_inner, _, _ = inner(block[:, :C], 0, t_scales[i])
        f_inner, f_average, f_inverse = inner(block[:, C:], 2, f_scales[i])
        teacher, fake = t_inner + t_shifts[i], f_inner + f_shifts[i]
        at = slice(i * OWNED, (i + 1) * OWNED)
        samples, g_inner = keep_ref[0, at, :], keep_ref[1, at, :]
        g_average, g_inverse = keep_ref[2, at, 0:1], keep_ref[3, at, 0:1]
        noise = noise_ref[pl.ds(pl.multiple_of(place_ref[3] + i * HALF, 16), OWNED), :][:, C:].astype(F32)
        t = time_ref[i]
        noised = mix(samples, noise, t).astype(F32)
        distance = jnp.sum(jnp.abs(samples - noised + t * teacher))
        gen_cot = (-(gen_time_ref[i] * t * loss_scale) * (teacher - fake)).astype(BF16).astype(F32)
        fake_cot = (loss_scale * (fake - noise + samples)).astype(BF16).astype(F32)
        numbers = []
        for cot, column, value, average, inverse in (
            (fake_cot, f_scales[i], f_inner, f_average, f_inverse),
            (gen_cot, sums_ref[i : i + 1, :], g_inner, g_average, g_inverse),
        ):
            first = jnp.sum(cot * column, axis=1, keepdims=True) / D
            second = jnp.sum(cot * value, axis=1, keepdims=True) / D
            slope = inverse * inverse * second
            numbers += [inverse, slope, average * slope - inverse * first]
        cots.append(jnp.concatenate([fake_cot, gen_cot], axis=1))
        numbers_row = to_row([number[None] for number in numbers])[0]
        numbers_row = jnp.where(lane == 96, distance, numbers_row)
        for _ in range(3):
            rounded = numbers_row.astype(BF16).astype(F32)
            rows.append(rounded)
            numbers_row = numbers_row - rounded
    rows.append(jnp.zeros((7, 128), F32))
    packed = jnp.concatenate(cots + rows, axis=0).astype(BF16)
    out_ref[...] = jnp.broadcast_to(packed[None], out_ref.shape)


def gelu_slope(v):
    a, b = math.sqrt(2.0 / math.pi), 0.044715
    t = jnp.tanh(a * (v + b * (v * v * v)))
    return 0.5 * (1.0 + t) + 0.5 * v * (1.0 - t * t) * (a * (1.0 + 3.0 * b * (v * v)))


def gradient_kernel(net, place_ref, got_ref, *refs):
    gap_ref, refs = (refs[0], refs[1:]) if net == 1 else (None, refs)
    mods_ref, final_ref, pre_ref, res_ref, shaped_ref, keep_ref, send_ref, left_ref = refs

    @pl.when(pl.program_id(0) == 0)
    def _():
        final = local_lanes(lambda at: final_ref[:, at], place_ref)
        if net == 1:
            gaps = jnp.sum(gap_ref[...], axis=0)
        for i in range(IMAGES):
            row = got_ref[:, 48:64, :].astype(F32)
            row = row[:, 3 * i : 3 * i + 1] + row[:, 3 * i + 1 : 3 * i + 2] + row[:, 3 * i + 2 : 3 * i + 3]
            inverse, slope, offset = [from_row(row, 3 * net + k).reshape(TOKENS, 1) for k in range(3)]
            cot = got_ref[:, 16 * i : 16 * i + 16, :].reshape(TOKENS, 128)[:, net * C : (net + 1) * C]
            out_grad = dot(cot, final)
            scale = local_lanes(lambda at: mods_ref[i, 4:5, at], place_ref)
            gate = local_lanes(lambda at: mods_ref[i, 2:3, at], place_ref)
            res_grad = inverse * (out_grad * (1.0 + scale)) - slope * res_ref[i] + offset
            act_grad = res_grad * gate
            if net == 1:
                inverse_gap = 1.0 / (gaps[i : i + 1, :] / (S * C) + gap_epsilon)
                act_grad = act_grad * jnp.concatenate([inverse_gap, inverse_gap[:, :NARROW]], axis=1)
            grad = act_grad * gelu_slope(pre_ref[i])
            turned = jnp.concatenate([grad, jnp.zeros((TOKENS, NARROW), F32)], axis=1).T
            left_ref[:, i * TOKENS : (i + 1) * TOKENS] = turned[:COLS].astype(BF16)

    grad = dot(left_ref[...], shaped_ref[...].reshape(IMAGES * TOKENS, 768))
    tiles = grad[:WIDE].T.astype(BF16)
    parts = jnp.concatenate([grad[WIDE:, :384], grad[WIDE:, 384:]], axis=0).T.astype(BF16)
    first = place_ref[4] == 0
    for w in range(2):
        sides = []
        for h in range(2):
            at = [(v * 2 + w) * ROWS for v in range(2)]
            lanes = slice(h * NARROW, (h + 1) * NARROW)
            narrow = jnp.concatenate([parts[k : k + ROWS, lanes] for k in at], axis=1)
            sides.append([tiles[h * 384 + k : h * 384 + k + ROWS] for k in at] + [narrow])
        for n, (low, high) in enumerate(zip(*sides, strict=True)):
            keep_ref[w, n * ROWS : (n + 1) * ROWS, :] = jnp.where(first, low, high)
            send_ref[w, n * ROWS : (n + 1) * ROWS, :] = jnp.where(first, high, low)


def sum_kernel(place_ref, got_ref, keep_ref, send_ref):
    v = place_ref[0]
    for n in range(2):
        rows = slice(n * GEN_ROWS, (n + 1) * GEN_ROWS)
        total = got_ref[0, rows].astype(F32)
        for k in range(1, CHUNKS):
            total = total + got_ref[k, rows].astype(F32)
        low = jnp.concatenate([total[:ROWS], total[2 * ROWS :, :NARROW]], axis=1)
        high = jnp.concatenate([total[ROWS : 2 * ROWS], total[2 * ROWS :, NARROW:]], axis=1)
        keep_ref[n] = jnp.where(v == 0, low, high)
        send_ref[n] = jnp.where(v == 0, high, low)


def place_kernel(place_ref, keep_ref, other_ref, fake_ref, gen_ref):
    for n, ref in enumerate((fake_ref, gen_ref)):
        low, high = in_order(place_ref[0], keep_ref[n], other_ref[n])
        ref[:, :128] = low[:, :WIDE]
        ref[:, 128:256] = jnp.concatenate([low[:, WIDE:], high[:, WIDE:]], axis=1)
        ref[:, 256:] = high[:, :WIDE]


def in_hbm(*arrays):
    return [pltpu.with_memory_space_constraint(a, pltpu.HBM) for a in arrays]


def exchange(value, axes):
    return lax.all_to_all(value, axes, 0, 0)


def shards(
    gen_noise,
    score_noise,
    gen_steps,
    score_steps,
    gen_embed,
    gen_modulation,
    gen_proj,
    gen_final,
    teacher_embed,
    teacher_modulation,
    teacher_proj,
    teacher_final,
    fake_embed,
    fake_modulation,
    fake_proj,
    fake_final,
):
    v, s = lax.axis_index("v"), lax.axis_index("s")
    start = lax.axis_index(("g", "h")) * 384
    member = lax.axis_index(("h", "g"))
    place = jnp.stack([v, start + 256 * v, start + 128, member * OWNED, s]).astype(jnp.int32)
    gen_final, teacher_final, fake_final = gen_final.T, teacher_final.T, fake_final.T

    times, conds = time_features(jnp.concatenate([gen_steps, score_steps]), gen_modulation.shape[0])
    gen_time, score_time = times[:3], times[3:]
    halves = jax.ShapeDtypeStruct((SENT_ROWS, 128), BF16)
    mine, other = pl.pallas_call(
        split_kernel,
        grid=(1,),
        in_specs=[smem(), whole((6, 256))] + [whole((IMAGES, C, HALF))] * 2 + [whole((ROWS, 384))] * 3
        + [whole((480, 256))] * 3,
        out_specs=[whole((SENT_ROWS, 128))] * 2,
        out_shape=[halves, halves],
        compiler_params=params(60),
        name="split",
    )(place, conds, gen_noise.transpose(0, 2, 1), score_noise.transpose(0, 2, 1), gen_proj, teacher_proj, fake_proj,
      gen_modulation.T, teacher_modulation.T, fake_modulation.T)
    mine = lax.ppermute(mine, PLACES, SWAP)
    other = lax.ppermute(other, PLACES, SWAP_TURNED)

    g_packed, packed = pl.pallas_call(
        pack_kernel,
        grid=(1,),
        in_specs=[smem()] + [whole((SENT_ROWS, 128))] * 2,
        out_specs=[whole((CHUNKS, GEN_CHUNK, 128)), whole((CHUNKS, SCORE_ROWS, 128))],
        out_shape=[
            jax.ShapeDtypeStruct((CHUNKS, GEN_CHUNK, 128), BF16),
            jax.ShapeDtypeStruct((CHUNKS, SCORE_ROWS, 128), BF16),
        ],
        compiler_params=params(6),
        name="pack",
    )(place, mine, other)
    g_packed = exchange(g_packed, GATHER)
    g_other = lax.ppermute(g_packed, "s", SIBLING)
    packed, g_packed, g_other = lax.optimization_barrier((packed, g_packed, g_other))
    packed = exchange(packed, GATHER)
    low, high = (a[:, GEN_ROWS : GEN_ROWS + 2 * MODS_ROWS] for a in in_order(s, g_packed, g_other))
    mods = jnp.stack([low, high]).reshape(2, 4, 2, 2, 4, 9, 128).transpose(5, 1, 0, 3, 2, 4, 6)
    mods = mods.reshape(9, 32, 512)[:, :, :480].reshape(9, 5, D).astype(F32)
    mods = jnp.pad(mods, ((0, 0), (0, 3), (0, 0)))

    by_image = lambda *shape: pl.BlockSpec((1, *shape), lambda i: (i,) + (0,) * len(shape))
    noise_rows = pl.BlockSpec((HALF, 128), lambda i: (i, 0))
    mods_of = lambda net: pl.BlockSpec((1, 8, D), lambda i: (3 * net + i, 0, 0))
    local = pltpu.HBM((IMAGES, TOKENS, COLS), F32)
    wide = pltpu.HBM((IMAGES, TOKENS, D), BF16)
    gen_embed, teacher_embed, fake_embed = in_hbm(gen_embed, teacher_embed, fake_embed)
    gen_final, teacher_final, fake_final = in_hbm(gen_final, teacher_final, fake_final)

    part, g_shaped, g_pre, g_res = pl.pallas_call(
        generator_kernel,
        grid=(IMAGES,),
        in_specs=[
            smem(), noise_rows, noise_rows, whole((C, D)), mods_of(0), whole((C, D)),
            *([whole((CHUNKS, GEN_CHUNK, 128))] * 2),
        ],
        out_specs=[whole((OWNERS, 32, 128)), by_image(TOKENS, D), by_image(TOKENS, COLS), by_image(TOKENS, COLS)],
        out_shape=[jax.ShapeDtypeStruct((OWNERS, 32, 128), F32), wide, local, local],
        scratch_shapes=[pltpu.VMEM((D, COLS), BF16), pltpu.VMEM((TOKENS, D), F32)],
        compiler_params=params(16),
        cost_estimate=pl.CostEstimate(flops=12 * 10**9, bytes_accessed=30 * 10**6, transcendentals=0),
        name="generator",
    )(place, mine, other, gen_embed, mods, gen_final, g_packed, g_other)
    packed, part = lax.optimization_barrier((packed, part))
    other_packed = lax.ppermute(packed, "s", SIBLING)
    part = exchange(part, COMBINE)

    net_mods = lambda net: pl.BlockSpec((IMAGES, 8, D), lambda *_: (net, 0, 0))
    pack1, keep, sums = pl.pallas_call(
        samples_kernel,
        grid=(1,),
        in_specs=[
            smem(), smem(), whole((OWNERS, 32, 128)), whole((NOISE_ROWS, 128)), net_mods(0), whole((C, D)),
        ],
        out_specs=[whole((OWNERS, 24, 128)), whole((4, 48, C)), whole((8, C))],
        out_shape=[
            jax.ShapeDtypeStruct((OWNERS, 24, 128), F32),
            jax.ShapeDtypeStruct((4, 48, C), F32),
            jax.ShapeDtypeStruct((8, C), F32),
        ],
        compiler_params=params(5),
        name="samples",
    )(place, gen_time, part, mine, mods, gen_final)
    pack1 = exchange(pack1, COMBINE)

    part2, samples, f_shaped, f_pre, f_res = pl.pallas_call(
        score_kernel,
        grid=(IMAGES,),
        in_specs=[
            smem(), smem(), whole((OWNERS, 24, 128)), noise_rows, noise_rows,
            whole((C, D)), whole((C, D)), mods_of(1), mods_of(2), whole((C, D)), whole((C, D)),
            *([whole((CHUNKS, SCORE_ROWS, 128))] * 2),
        ],
        out_specs=[
            whole((OWNERS, 56, 128)), by_image(C, HALF), by_image(TOKENS, D), by_image(TOKENS, COLS),
            by_image(TOKENS, COLS),
        ],
        out_shape=[
            jax.ShapeDtypeStruct((OWNERS, 56, 128), F32),
            jax.ShapeDtypeStruct((IMAGES, C, HALF), F32),
            wide, local, local,
        ],
        scratch_shapes=[
            pltpu.VMEM((D, COLS), BF16), pltpu.VMEM((D, COLS), BF16), pltpu.VMEM((TOKENS, D), F32),
            pltpu.VMEM((TOKENS, D), BF16),
        ],
        compiler_params=params(22),
        cost_estimate=pl.CostEstimate(flops=24 * 10**9, bytes_accessed=50 * 10**6, transcendentals=0),
        name="score",
    )(place, score_time, pack1, mine, other, teacher_embed, fake_embed, mods, mods,
      teacher_final, fake_final, packed, other_packed)
    samples = lax.ppermute(samples, PLACES, SWAP).transpose(0, 2, 1)
    part2 = exchange(part2, COMBINE)

    pack2 = pl.pallas_call(
        cotangent_kernel,
        grid=(1,),
        in_specs=[
            smem(), smem(), smem(), whole((OWNERS, 56, 128)), whole((NOISE_ROWS, 128)), whole((4, 48, C)),
            whole((8, C)), net_mods(1), net_mods(2), whole((C, D)), whole((C, D)),
        ],
        out_specs=whole((OWNERS, 64, 128)),
        out_shape=jax.ShapeDtypeStruct((OWNERS, 64, 128), BF16),
        compiler_params=params(6),
        name="cotangents",
    )(place, gen_time, score_time, part2, mine, keep, sums, mods, mods, teacher_final, fake_final)
    pack2 = exchange(pack2, COMBINE)

    gap = jnp.sum(pack2[:, 48:57, 96].astype(F32).reshape(OWNERS, 3, 3), axis=(0, 2))
    gap = jnp.broadcast_to(jnp.pad(gap, (0, 5))[None, :, None], (16, 8, 128))
    gap = exchange(gap, TOKEN_AXES)

    by_columns = pl.BlockSpec((IMAGES, TOKENS, 768), lambda x: (0, 0, x))
    partial = jax.ShapeDtypeStruct((CHUNKS, GEN_ROWS, 128), BF16)
    partial_spec = pl.BlockSpec((2, GEN_ROWS, 128), lambda x: (x, 0, 0))

    def gradient(net, gaps, mods_net, final, pre, res, shaped):
        kept, sent = pl.pallas_call(
            functools.partial(gradient_kernel, net),
            grid=(4,),
            in_specs=[
                smem(), whole((OWNERS, 64, 128)), *([whole((16, 8, 128))] * len(gaps)), net_mods(mods_net),
                whole((C, D)), *([whole((IMAGES, TOKENS, COLS))] * 2), by_columns,
            ],
            out_specs=[partial_spec, partial_spec],
            out_shape=[partial, partial],
            scratch_shapes=[pltpu.VMEM((COLS, IMAGES * TOKENS), BF16)],
            compiler_params=params(13),
            cost_estimate=pl.CostEstimate(flops=7 * 10**9, bytes_accessed=20 * 10**6, transcendentals=0),
        name="gradient",
        )(place, pack2, *gaps, mods, final, *in_hbm(pre, res, shaped))
        return kept, lax.ppermute(sent, "s", SIBLING)

    pieces = gradient(0, (), 2, fake_final, f_pre, f_res, f_shaped)
    pieces += gradient(1, (gap,), 0, gen_final, g_pre, g_res, g_shaped)
    both = jnp.concatenate(
        [(pieces[n].astype(F32) + pieces[n + 1].astype(F32)).astype(BF16) for n in (0, 2)], axis=1
    )
    tiles = jax.ShapeDtypeStruct((2, ROWS, COLS), F32)
    kept, sent = pl.pallas_call(
        sum_kernel,
        grid=(1,),
        in_specs=[smem(), whole((CHUNKS, 2 * GEN_ROWS, 128))],
        out_specs=[whole((2, ROWS, COLS))] * 2,
        out_shape=[tiles, tiles],
        compiler_params=params(8),
        name="sum",
    )(place, exchange(both, GATHER))
    kept = lax.ppermute(kept, PLACES, SWAP)
    sent = lax.ppermute(sent, PLACES, SWAP_TURNED)
    fake_grad, gen_grad = pl.pallas_call(
        place_kernel,
        grid=(1,),
        in_specs=[smem(), whole((2, ROWS, COLS)), whole((2, ROWS, COLS))],
        out_specs=[whole((ROWS, 384))] * 2,
        out_shape=[jax.ShapeDtypeStruct((ROWS, 384), F32)] * 2,
        compiler_params=params(4),
        name="place",
    )(place, kept, sent)
    return (samples, gen_grad, fake_grad)


def solution(mesh):
    split = Mesh(mesh.devices.reshape(4, 4, 2, 2, 2, 2), ("g", "x", "h", "v", "w", "s"))
    tokens = P(None, ROW_AXES, None)
    columns = P(None, ROW_AXES)
    block = P(ROW_AXES, ("g", "s"))
    net = (P(), columns, block, P())
    return jax.shard_map(
        shards,
        mesh=split,
        in_specs=(tokens, tokens, P(), P(), *net, *net, *net),
        out_specs=(tokens, block, block),
        check_vma=False,
    )
```

time: 352 us -> 227 us (0.64)
  blocking collectives: 232 us -> 82.4 us
  starting transfers between devices: 24.2 us -> 47.5 us
  waiting for transfers between devices: 18.1 us -> 37.6 us
  Pallas kernels: 58.9 us -> 48.1 us
  local copies, waits for them, and re-layouts: 9.28 us -> 5.49 us
    all_gather x1 -> x0, blocking collectives: 120 us -> none  [shards(): mods = lax.all_gather(own_mods, XHY, axis=1, tiled=True)]
    all_to_all x5, blocking collectives: 112 us -> 82.4 us  [exchange(): return lax.all_to_all(value, axes, 0, 0)]
    ppermute x3 -> x9, starting transfers between devices: 13 us -> 28.3 us  [the longest x1 10.2 us: shards(): mine = lax.ppermute(mine, PLACES, SWAP)]
    ppermute x3 -> x9, waiting for transfers between devices: 10.9 us -> 22.2 us  [the longest x1 10.6 us: shards(): other = lax.ppermute(other, PLACES, SWAP_TURNED)]
    all_to_all x2 -> x3, waiting for transfers between devices: 7.21 us -> 15.4 us  [exchange(): return lax.all_to_all(value, axes, 0, 0)]
    all_to_all x2 -> x3, starting transfers between devices: 11.2 us -> 19.2 us  [exchange(): return lax.all_to_all(value, axes, 0, 0)]
    pallas_call x5 -> x7, Pallas kernels: 34.6 us -> 27.8 us  [the longest x2 12.2 us: gradient(): pl.pallas_call(functools.partial(gradient_kernel, net), grid=(4,), in_spe...]
    unnamed x41 -> x9, local copies, waits for them, and re-layouts: 7.14 us -> 2.33 us
  transfers between devices with their start and end apart: 5 -> 12, of which waited for: 3 -> 7; matrix products, arithmetic and copies ran while one was open for 3% -> 2% of each run, Pallas kernels for 0% -> 10%
where the time goes in v2:
time: 227 us; the launch traced here: 226 us
  blocking collectives  82.4 us (36%)
  Pallas kernels  48.1 us (21%)
  starting transfers between devices  47.5 us (21%)
  waiting for transfers between devices  37.6 us (17%)
  local copies, waits for them, and re-layouts  5.49 us (2%)
  other arithmetic  3.74 us (2%)
    all_to_all x5, blocking collectives, exchange(): return lax.all_to_all(value, axes, 0, 0)  82.4 us
    all_to_all x3, starting transfers between devices, exchange(): return lax.all_to_all(value, axes, 0, 0)  19.2 us
    pallas_call x1, Pallas kernels, shards(): pl.pallas_call(score_kernel, grid=(IMAGES,), in_specs=[smem(), smem(), wh...  17.2 us
    all_to_all x3, waiting for transfers between devices, exchange(): return lax.all_to_all(value, axes, 0, 0)  15.4 us
    pallas_call x2, Pallas kernels, gradient(): pl.pallas_call(functools.partial(gradient_kernel, net), grid=(4,), in_spe...  12.2 us
    ppermute x1, waiting for transfers between devices, shards(): other = lax.ppermute(other, PLACES, SWAP_TURNED)  10.6 us
    ppermute x1, starting transfers between devices, shards(): mine = lax.ppermute(mine, PLACES, SWAP)  10.2 us
    pallas_call x1, Pallas kernels, shards(): pl.pallas_call(generator_kernel, grid=(IMAGES,), in_specs=[smem(), noise_...  9.31 us
  transfers between devices with their start and end apart: 12, of which 7 were waited for; matrix products, arithmetic and copies ran while one was open for 2% of the time, Pallas kernels for 10%

profile of v2, /device:TPU:1, one launch (start us, length us, event | category | flops | bytes accessed | tf_op | source)
XLA Modules:
  0.0 225.8 jit_solution(13748847880813795802)
XLA Ops:
  0.7 0.8 broadcast_multiply_fusion
  1.4 0.1 multiply_cosine_fusion
  1.5 0.6 multiply_convert_fusion.cond_ref
  2.1 0.6 stack.32.place_ref
  2.7 2.4 %split.1 = (bf16[912,128]{1,0:T(8,128)(2,1)}, bf16[912,128]{1,0:T(8,128)(2,1)}) custom-call(s32[5]{0:T(128)} %stack.32.place_ref, bf16[6,256]{1,0:T(8,128)(2,1)} %multiply_convert_fusion.cond_ref, bf16[3,64,128]{2,1,0:T(8,128)(2,1)} %bitcast.34, bf16[3,64,128]{2,1,0:T(8,128)(2,1)} %bitcast.35, bf16[96,384]{1,0:T(8,128)(2,1)} %gen_ref.1, ...), custom_call_target="tpu_custom_call" | custom-call | tf_op jit(solution)/shard_map/split/pallas_call | solution.py:456
  5.1 10.2 %collective-permute-start = (bf16[912,128]{1,0:T(8,128)(2,1)}, bf16[912,128]{1,0:T(8,128)(2,1)S(1)}, u32[]{:S(2)}, u32[]{:S(2)}) collective-permute-start(bf16[912,128]{1,0:T(8,128)(2,1)} %get-tuple-element.32), channel_id=1, source_target_pairs={{0,0},{1,8},{4,4},{5,12},{8,1},{9,9},{12,5},{13,13},{2,2},{3,10},{... | collective-permute-start | bytes 700424 | tf_op jit(solution)/shard_map/ppermute | solution.py:467
  15.3 2.7 %collective-permute-start.1 = (bf16[912,128]{1,0:T(8,128)(2,1)}, bf16[912,128]{1,0:T(8,128)(2,1)S(1)}, u32[]{:S(2)}, u32[]{:S(2)}) collective-permute-start(bf16[912,128]{1,0:T(8,128)(2,1)} %get-tuple-element.33), channel_id=1, source_target_pairs={{0,4},{1,12},{4,0},{5,8},{8,5},{9,13},{12,1},{13,9},{2,6},{3,14},{... | collective-permute-start | bytes 700424 | tf_op jit(solution)/shard_map/ppermute | solution.py:468
  18.1 1.3 collective-permute-done.mine_ref.own_ref.noise_ref
  19.4 10.6 %collective-permute-done.1.other_ref = bf16[912,128]{1,0:T(8,128)(2,1)S(1)} collective-permute-done((bf16[912,128]{1,0:T(8,128)(2,1)}, bf16[912,128]{1,0:T(8,128)(2,1)S(1)}, u32[]{:S(2)}, u32[]{:S(2)}) %collective-permute-start.1) | collective-permute-done | bytes 233504 | tf_op jit(solution)/shard_map/ppermute | solution.py:468
  30.0 0.0 copy-start.2
  30.0 0.6 copy-done.2
  30.6 1.8 pack.1
  32.4 13.5 %all_to_all.40.own_w_ref = bf16[8,368,128]{2,1,0:T(8,128)(2,1)S(1)} all-to-all(bf16[8,368,128]{2,1,0:T(8,128)(2,1)S(1)} %get-tuple-element.35), channel_id=1, replica_groups=mesh['g'=4,'x'=4,'h'=2,'v'=2,'w'=2,'s'=2] {'x','w'}, dimensions={0} | all-to-all | bytes 1507328 | tf_op jit(solution)/shard_map/all_to_all | solution.py:426
  45.9 0.0 collective-permute-start.2
  45.9 2.2 collective-permute-done.2.other_w_ref
  48.1 3.6 %all-to-all-start.1 = ((bf16[8,576,128]{2,1,0:T(8,128)(2,1)}), bf16[8,576,128]{2,1,0:T(8,128)(2,1)S(1)}, u32[]{:S(2)}, u32[]{:S(2)}) async-start(bf16[8,576,128]{2,1,0:T(8,128)(2,1)} %get-tuple-element.36), calls=%async_computation.1 | async-start | bytes 2359296 | tf_op jit(solution)/shard_map/all_to_all | solution.py:426
  51.7 0.0 copy-done
  51.8 0.4 maximum_bitcast_fusion
  52.2 0.1 copy.24
  52.4 0.1 reshape.44
  52.5 0.0 copy-start.3
  52.5 1.4 convert_element_type.43
  53.9 1.1 pad_convert_fusion.mods_ref.t_mods_ref.f_mods_ref.refs_0_.refs_1_
  55.0 0.0 copy-done.3
  55.0 0.0 copy-start.1
  55.1 1.1 copy-done.1
  56.2 9.3 %generator.1 = (f32[16,32,128]{2,1,0:T(8,128)}, bf16[3,256,3072]{2,1,0:T(8,128)(2,1)}, f32[3,256,192]{2,1,0:T(8,128)}, f32[3,256,192]{2,1,0:T(8,128)}) custom-call(s32[5]{0:T(128)S(1)} %copy-done.3, bf16[912,128]{1,0:T(8,128)(2,1)S(1)} %collective-permute-done.mine_ref.own_ref.noise_ref, bf16[912,128]{1,0:T(8,128)(2,1)S(1)} %collective-permute-done.1.other_ref, ...), custom_call_target="tpu_custom_call" | custom-call | flops 12000000000 | bytes 30000000 | tf_op jit(solution)/shard_map/generator/pallas_call | solution.py:499
  65.5 5.0 %all-to-all-done.1.own_w_ref = bf16[8,576,128]{2,1,0:T(8,128)(2,1)S(1)} async-done(((bf16[8,576,128]{2,1,0:T(8,128)(2,1)}), bf16[8,576,128]{2,1,0:T(8,128)(2,1)S(1)}, u32[]{:S(2)}, u32[]{:S(2)}) %all-to-all-start.1) | async-done | bytes 1179680 | tf_op jit(solution)/shard_map/all_to_all | solution.py:426
  70.5 1.0 collective-permute-start.3
  71.4 8.9 %all-to-all-start.2 = ((f32[16,32,128]{2,1,0:T(8,128)}), f32[16,32,128]{2,1,0:T(8,128)S(1)}, u32[]{:S(2)}, u32[]{:S(2)}) async-start(f32[16,32,128]{2,1,0:T(8,128)} %get-tuple-element.40), calls=%async_computation.2 | async-start | bytes 524288 | tf_op jit(solution)/shard_map/all_to_all | solution.py:426
  80.3 0.1 fusion.2
  80.4 10.5 %all-to-all-done.2.got_ref = f32[16,32,128]{2,1,0:T(8,128)S(1)} async-done(((f32[16,32,128]{2,1,0:T(8,128)}), f32[16,32,128]{2,1,0:T(8,128)S(1)}, u32[]{:S(2)}, u32[]{:S(2)}) %all-to-all-start.2) | async-done | bytes 262176 | tf_op jit(solution)/shard_map/all_to_all | solution.py:426
  90.8 1.3 samples.1
  92.1 14.4 %all_to_all.41.got_ref = f32[16,24,128]{2,1,0:T(8,128)S(1)} all-to-all(f32[16,24,128]{2,1,0:T(8,128)S(1)} %get-tuple-element.41), channel_id=1, replica_groups=mesh['g'=4,'x'=4,'h'=2,'v'=2,'w'=2,'s'=2] {'v','h','g'}, dimensions={0} | all-to-all | bytes 393216 | tf_op jit(solution)/shard_map/all_to_all | solution.py:426
  106.5 0.0 collective-permute-done.3.other_w_ref
  106.5 17.2 %score.1 = (f32[16,56,128]{2,1,0:T(8,128)S(1)}, f32[3,64,128]{2,1,0:T(8,128)S(1)}, bf16[3,256,3072]{2,1,0:T(8,128)(2,1)}, f32[3,256,192]{2,1,0:T(8,128)}, f32[3,256,192]{2,1,0:T(8,128)}) custom-call(s32[5]{0:T(128)S(1)} %copy-done.3, f32[3]{0:T(128)S(1)} %get-tuple-element.68.time_ref, f32[16,24,128]{2,1,0:T(8,128)S(1)} %all_to_all.41.got_ref, ...), custom_call_target="tpu_custom_call" | custom-call | flops 24000000000 | bytes 50000000 | tf_op jit(solution)/shard_map/score/pallas_call | solution.py:535
  123.7 18.1 %all_to_all.42.got_ref = f32[16,56,128]{2,1,0:T(8,128)S(1)} all-to-all(f32[16,56,128]{2,1,0:T(8,128)S(1)} %get-tuple-element.44), channel_id=1, replica_groups=mesh['g'=4,'x'=4,'h'=2,'v'=2,'w'=2,'s'=2] {'v','h','g'}, dimensions={0} | all-to-all | bytes 917504 | tf_op jit(solution)/shard_map/all_to_all | solution.py:426
  141.8 1.8 cotangents.1
  143.6 15.2 %all_to_all.43.got_ref = bf16[16,64,128]{2,1,0:T(8,128)(2,1)S(1)} all-to-all(bf16[16,64,128]{2,1,0:T(8,128)(2,1)S(1)} %cotangents.1), channel_id=1, replica_groups=mesh['g'=4,'x'=4,'h'=2,'v'=2,'w'=2,'s'=2] {'v','h','g'}, dimensions={0} | all-to-all | bytes 524288 | tf_op jit(solution)/shard_map/all_to_all | solution.py:426
  158.8 0.2 convert_reduce_fusion
  159.0 0.1 reduce_sum.14
  159.1 0.1 reduce_sum.18
  159.2 0.7 broadcast_in_dim.2
  159.9 6.8 %all-to-all-start.6 = ((f32[16,8,128]{2,1,0:T(8,128)}), f32[16,8,128]{2,1,0:T(8,128)S(1)}, u32[]{:S(2)}, u32[]{:S(2)}) async-start(f32[16,8,128]{2,1,0:T(8,128)} %broadcast_in_dim.2), calls=%async_computation.6 | async-start | bytes 131072 | tf_op jit(solution)/shard_map/all_to_all | solution.py:426
  166.7 6.0 %gradient.2 = (bf16[8,288,128]{2,1,0:T(8,128)(2,1)S(1)}, bf16[8,288,128]{2,1,0:T(8,128)(2,1)S(1)}) custom-call(s32[5]{0:T(128)S(1)} %copy-done.3, bf16[16,64,128]{2,1,0:T(8,128)(2,1)S(1)} %all_to_all.43.got_ref, f32[9,8,3072]{2,1,0:T(8,128)S(1)} %pad_convert_fusion.mods_ref.t_mods_ref.f_mods_ref.refs_0_.refs_1_, bf16[64,3072]{1,0:T(8,128)(2,1)} %bitcast.29, ...), custom_call_target="tpu_custom_call" | custom-call | flops 7000000000 | bytes 20000000 | tf_op jit(solution)/shard_map/gradient/pallas_call | solution.py:587
  172.8 0.3 collective-permute-start.5
  173.1 0.0 all-to-all-done.6.refs_0_
  173.1 6.1 %gradient.3 = (bf16[8,288,128]{2,1,0:T(8,128)(2,1)S(1)}, bf16[8,288,128]{2,1,0:T(8,128)(2,1)S(1)}) custom-call(s32[5]{0:T(128)S(1)} %copy-done.3, bf16[16,64,128]{2,1,0:T(8,128)(2,1)S(1)} %all_to_all.43.got_ref, f32[16,8,128]{2,1,0:T(8,128)S(1)} %all-to-all-done.6.refs_0_, f32[9,8,3072]{2,1,0:T(8,128)S(1)} %pad_convert_fusion.mods_ref.t_mods_ref.f_mods_ref.refs_0_.refs_1_, ...), custom_call_target="tpu_custom_call" | custom-call | flops 7000000000 | bytes 20000000 | tf_op jit(solution)/shard_map/gradient/pallas_call | solution.py:587
  179.3 0.4 collective-permute-start.6
  179.6 0.0 collective-permute-done.5
  179.6 0.2 add_convert_fusion.1
  179.8 1.6 collective-permute-done.6
  181.3 0.2 add_convert_fusion
  181.5 0.1 pad_maximum_fusion
  181.6 21.3 %all_to_all.44.got_ref = bf16[8,576,128]{2,1,0:T(8,128)(2,1)S(1)} all-to-all(bf16[8,576,128]{2,1,0:T(8,128)(2,1)S(1)} %pad_maximum_fusion), channel_id=1, replica_groups=mesh['g'=4,'x'=4,'h'=2,'v'=2,'w'=2,'s'=2] {'x','w'}, dimensions={0} | all-to-all | bytes 2359296 | tf_op jit(solution)/shard_map/all_to_all | solution.py:426
  202.9 0.7 sum.1
  203.6 5.6 %collective-permute-start.7 = (f32[2,96,192]{2,1,0:T(8,128)S(1)}, f32[2,96,192]{2,1,0:T(8,128)S(1)}, u32[]{:S(2)}, u32[]{:S(2)}) collective-permute-start(f32[2,96,192]{2,1,0:T(8,128)S(1)} %get-tuple-element.57), channel_id=1, source_target_pairs={{0,0},{1,8},{4,4},{5,12},{8,1},{9,9},{12,5},{13,13},{2,2},{3,10},{... | collective-permute-start | bytes 442376 | tf_op jit(solution)/shard_map/ppermute | solution.py:618
  209.2 2.7 %collective-permute-start.8 = (f32[2,96,192]{2,1,0:T(8,128)S(1)}, f32[2,96,192]{2,1,0:T(8,128)S(1)}, u32[]{:S(2)}, u32[]{:S(2)}) collective-permute-start(f32[2,96,192]{2,1,0:T(8,128)S(1)} %get-tuple-element.58), channel_id=1, source_target_pairs={{0,4},{1,12},{4,0},{5,8},{8,5},{9,13},{12,1},{13,9},{2,6},{3,14},{... | collective-permute-start | bytes 442376 | tf_op jit(solution)/shard_map/ppermute | solution.py:619
  211.8 5.5 %collective-permute-start.4 = (f32[3,64,128]{2,1,0:T(8,128)S(1)}, f32[3,64,128]{2,1,0:T(8,128)S(1)}, u32[]{:S(2)}, u32[]{:S(2)}) collective-permute-start(f32[3,64,128]{2,1,0:T(8,128)S(1)} %get-tuple-element.43), channel_id=1, source_target_pairs={{0,0},{1,8},{4,4},{5,12},{8,1},{9,9},{12,5},{13,13},{2,2},{3,10},{... | collective-permute-start | bytes 294920 | tf_op jit(solution)/shard_map/ppermute | solution.py:561
  217.3 6.5 %collective-permute-done.4 = f32[3,64,128]{2,1,0:T(8,128)S(1)} collective-permute-done((f32[3,64,128]{2,1,0:T(8,128)S(1)}, f32[3,64,128]{2,1,0:T(8,128)S(1)}, u32[]{:S(2)}, u32[]{:S(2)}) %collective-permute-start.4) | collective-permute-done | bytes 98336 | tf_op jit(solution)/shard_map/ppermute | solution.py:561
  223.8 0.0 collective-permute-done.7.keep_ref
  223.8 0.0 collective-permute-done.8.other_ref
  223.8 1.3 place.1
  225.1 0.6 copy.26
  (7 shorter events, 0.1 us)
Async XLA Ops:
  5.1 14.2 %collective-permute-start = (bf16[912,128]{1,0:T(8,128)(2,1)}, bf16[912,128]{1,0:T(8,128)(2,1)S(1)}, u32[]{:S(2)}, u32[]{:S(2)}) collective-permute-start(bf16[912,128]{1,0:T(8,128)(2,1)} %get-tuple-element.32), channel_id=1, source_target_pairs={{0,0},{1,8},{4,4},{5,12},{8,1},{9,9},{12,5},{13,13},{2,2},{3,10},{... | collective-permute-start | bytes 700424 | tf_op jit(solution)/shard_map/ppermute | solution.py:467
  15.3 14.6 %collective-permute-start.1 = (bf16[912,128]{1,0:T(8,128)(2,1)}, bf16[912,128]{1,0:T(8,128)(2,1)S(1)}, u32[]{:S(2)}, u32[]{:S(2)}) collective-permute-start(bf16[912,128]{1,0:T(8,128)(2,1)} %get-tuple-element.33), channel_id=1, source_target_pairs={{0,4},{1,12},{4,0},{5,8},{8,5},{9,13},{12,1},{13,9},{2,6},{3,14},{... | collective-permute-start | bytes 700424 | tf_op jit(solution)/shard_map/ppermute | solution.py:468
  30.0 0.6 copy-start.2
  45.9 2.2 collective-permute-start.2
  48.1 3.6 %copy-start = (bf16[8,368,128]{2,1,0:T(8,128)(2,1)}, bf16[8,368,128]{2,1,0:T(8,128)(2,1)S(1)}, u32[]{:S(2)}) copy-start(bf16[8,368,128]{2,1,0:T(8,128)(2,1)S(1)} %collective-permute-done.2.other_w_ref) | copy-start | bytes 2260996
  48.1 22.3 %all-to-all-start.1 = ((bf16[8,576,128]{2,1,0:T(8,128)(2,1)}), bf16[8,576,128]{2,1,0:T(8,128)(2,1)S(1)}, u32[]{:S(2)}, u32[]{:S(2)}) async-start(bf16[8,576,128]{2,1,0:T(8,128)(2,1)} %get-tuple-element.36), calls=%async_computation.1 | async-start | bytes 2359296 | tf_op jit(solution)/shard_map/all_to_all | solution.py:426
  52.5 2.5 %copy-start.3 = (s32[5]{0:T(128)S(1)}, s32[5]{0:T(128)}, u32[]{:S(2)}) copy-start(s32[5]{0:T(128)} %stack.32.place_ref) | copy-start | bytes 64
  55.0 1.1 copy-start.1
  70.5 36.1 %collective-permute-start.3 = (bf16[8,576,128]{2,1,0:T(8,128)(2,1)S(1)}, bf16[8,576,128]{2,1,0:T(8,128)(2,1)}, u32[]{:S(2)}, u32[]{:S(2)}) collective-permute-start(bf16[8,576,128]{2,1,0:T(8,128)(2,1)S(1)} %all-to-all-done.1.own_w_ref), channel_id=1, source_target_pairs={{0,1},{1,0},{2,3},{3,2},{4,5},{5,4},{6,7},{7,6},{8,9},{9,8},{10,11... | collective-permute-start | bytes 3538952 | tf_op jit(solution)/shard_map/ppermute | solution.py:514
  71.4 19.4 %all-to-all-start.2 = ((f32[16,32,128]{2,1,0:T(8,128)}), f32[16,32,128]{2,1,0:T(8,128)S(1)}, u32[]{:S(2)}, u32[]{:S(2)}) async-start(f32[16,32,128]{2,1,0:T(8,128)} %get-tuple-element.40), calls=%async_computation.2 | async-start | bytes 524288 | tf_op jit(solution)/shard_map/all_to_all | solution.py:426
  159.9 13.2 %all-to-all-start.6 = ((f32[16,8,128]{2,1,0:T(8,128)}), f32[16,8,128]{2,1,0:T(8,128)S(1)}, u32[]{:S(2)}, u32[]{:S(2)}) async-start(f32[16,8,128]{2,1,0:T(8,128)} %broadcast_in_dim.2), calls=%async_computation.6 | async-start | bytes 131072 | tf_op jit(solution)/shard_map/all_to_all | solution.py:426
  172.8 6.8 %collective-permute-start.5 = (bf16[8,288,128]{2,1,0:T(8,128)(2,1)S(1)}, bf16[8,288,128]{2,1,0:T(8,128)(2,1)S(1)}, u32[]{:S(2)}, u32[]{:S(2)}) collective-permute-start(bf16[8,288,128]{2,1,0:T(8,128)(2,1)S(1)} %get-tuple-element.51), channel_id=1, source_target_pairs={{0,1},{1,0},{2,3},{3,2},{4,5},{5,4},{6,7},{7,6},{8,9},{9,8},{10,11... | collective-permute-start | bytes 1769480 | tf_op jit(solution)/shard_map/ppermute | solution.py:601
  179.3 2.1 collective-permute-start.6
  203.6 20.2 %collective-permute-start.7 = (f32[2,96,192]{2,1,0:T(8,128)S(1)}, f32[2,96,192]{2,1,0:T(8,128)S(1)}, u32[]{:S(2)}, u32[]{:S(2)}) collective-permute-start(f32[2,96,192]{2,1,0:T(8,128)S(1)} %get-tuple-element.57), channel_id=1, source_target_pairs={{0,0},{1,8},{4,4},{5,12},{8,1},{9,9},{12,5},{13,13},{2,2},{3,10},{... | collective-permute-start | bytes 442376 | tf_op jit(solution)/shard_map/ppermute | solution.py:618
  209.2 14.6 %collective-permute-start.8 = (f32[2,96,192]{2,1,0:T(8,128)S(1)}, f32[2,96,192]{2,1,0:T(8,128)S(1)}, u32[]{:S(2)}, u32[]{:S(2)}) collective-permute-start(f32[2,96,192]{2,1,0:T(8,128)S(1)} %get-tuple-element.58), channel_id=1, source_target_pairs={{0,4},{1,12},{4,0},{5,8},{8,5},{9,13},{12,1},{13,9},{2,6},{3,14},{... | collective-permute-start | bytes 442376 | tf_op jit(solution)/shard_map/ppermute | solution.py:619
  211.8 12.0 %collective-permute-start.4 = (f32[3,64,128]{2,1,0:T(8,128)S(1)}, f32[3,64,128]{2,1,0:T(8,128)S(1)}, u32[]{:S(2)}, u32[]{:S(2)}) collective-permute-start(f32[3,64,128]{2,1,0:T(8,128)S(1)} %get-tuple-element.43), channel_id=1, source_target_pairs={{0,0},{1,8},{4,4},{5,12},{8,1},{9,9},{12,5},{13,13},{2,2},{3,10},{... | collective-permute-start | bytes 294920 | tf_op jit(solution)/shard_map/ppermute | solution.py:561

commit v3 on v2

--- a/solution.py
+++ b/solution.py
@@ -119,25 +119,38 @@
                 w_ref[pl.ds(k, ROWS), WIDE:] = part
 
 
-def forward(x, embed_ref, mods_ref, final_ref, w_ref, hidden_ref, shaped_ref, place_ref):
-    sums = jnp.zeros((TOKENS, 128), F32)
-    squares = jnp.zeros((TOKENS, 128), F32)
-    for b in range(D // BLOCK):
-        cut = slice(b * BLOCK, (b + 1) * BLOCK)
-        hidden = dot(x, embed_ref[:, cut])
-        hidden_ref[:, cut] = hidden
-        for j in range(BLOCK // 128):
-            piece = hidden[:, j * 128 : (j + 1) * 128]
-            sums = sums + piece
-            squares = squares + piece * piece
-    average = jnp.sum(sums, axis=1, keepdims=True) / D
-    square = jnp.sum(squares, axis=1, keepdims=True) / D
-    inverse = lax.rsqrt(square - average * average + norm_epsilon)
+def split_bits(value, count):
+    pieces = []
+    for _ in range(count):
+        piece = value.astype(BF16)
+        pieces.append(piece)
+        value = value - piece.astype(F32)
+    return pieces
+
+
+def embed_moments(embed_ref, gram_ref, mean_ref):
+    embed = embed_ref[...]
+    ones = jnp.ones((8, D), BF16)
+    column = dot_turned(embed, ones)[:, 0:1] / D
+    row = dot_turned(ones, embed)[0:1] / D
+    gram = dot_turned(embed, embed) / D - column * row
+    gram_ref[...] = jnp.concatenate(split_bits(gram, 3), axis=1)
+    mean_ref[...] = jnp.broadcast_to(column, mean_ref.shape)
+
+
+def forward(x, embed_ref, mods_ref, final_ref, w_ref, gram_ref, mean_ref, shaped_ref, place_ref):
+    turned = dot(x, gram_ref[...])
+    turned = turned[:, :C] + turned[:, C : 2 * C] + turned[:, 2 * C :]
+    inverse = lax.rsqrt(jnp.sum(turned * x.astype(F32), axis=1, keepdims=True) + norm_epsilon)
+    inverse = jnp.broadcast_to(inverse, (TOKENS, BLOCK))
+    twice = jnp.concatenate([x, x], axis=1)
+    mean = mean_ref[:, 0:1]
     preactivation = jnp.zeros((TOKENS, COLS), F32)
     for b in range(D // BLOCK):
         cut = slice(b * BLOCK, (b + 1) * BLOCK)
-        normed = (hidden_ref[:, cut] - average) * inverse
-        shaped = (normed * (1.0 + mods_ref[0, 1:2, cut]) + mods_ref[0, 0:1, cut]).astype(BF16)
+        scaled = (embed_ref[:, cut].astype(F32) - mean) * (1.0 + mods_ref[0, 1:2, cut])
+        scaled = jnp.concatenate(split_bits(scaled, 2), axis=0)
+        shaped = (dot(twice, scaled) * inverse + mods_ref[0, 0:1, cut]).astype(BF16)
         shaped_ref[:, cut] = shaped
         preactivation = preactivation + dot(shaped, w_ref[cut, :])
     activated = jax.nn.gelu(preactivation, approximate=True).astype(BF16).astype(F32)
@@ -216,18 +229,19 @@
 
 
 def generator_kernel(place_ref, own_ref, other_ref, embed_ref, mods_ref, final_ref, own_w_ref, other_w_ref,
-                     part_ref, shaped_ref, pre_ref, res_ref, w_ref, hidden_ref):
+                     part_ref, shaped_ref, pre_ref, res_ref, w_ref, gram_ref, mean_ref):
     i = pl.program_id(0)
     v = place_ref[0]
 
     @pl.when(i == 0)
     def _():
+        embed_moments(embed_ref, gram_ref, mean_ref)
         unpack_weights(place_ref, own_w_ref, other_w_ref, 0, w_ref)
         part_ref[:, 24:32, :] = jnp.zeros((OWNERS, 8, 128), F32)
 
     x = jnp.concatenate(in_order(v, own_ref[:, :C], other_ref[:, :C]), axis=0)
     pre, res, partial, total, square = forward(
-        x, embed_ref, mods_ref, final_ref, w_ref, hidden_ref, shaped_ref.at[0], place_ref
+        x, embed_ref, mods_ref, final_ref, w_ref, gram_ref, mean_ref, shaped_ref.at[0], place_ref
     )
     pre_ref[0] = pre
     res_ref[0] = res
@@ -269,12 +283,14 @@
 def score_kernel(place_ref, time_ref, got_ref, own_ref, other_ref,
                  t_embed_ref, f_embed_ref, t_mods_ref, f_mods_ref, t_final_ref, f_final_ref, own_w_ref, other_w_ref,
                  part_ref, samples_ref, shaped_ref, pre_ref, res_ref,
-                 t_w_ref, f_w_ref, hidden_ref, t_shaped_ref):
+                 t_w_ref, f_w_ref, t_gram_ref, f_gram_ref, t_mean_ref, f_mean_ref, t_shaped_ref):
     i = pl.program_id(0)
     v = place_ref[0]
 
     @pl.when(i == 0)
     def _():
+        embed_moments(t_embed_ref, t_gram_ref, t_mean_ref)
+        embed_moments(f_embed_ref, f_gram_ref, f_mean_ref)
         unpack_weights(place_ref, own_w_ref, other_w_ref, 1, t_w_ref)
         unpack_weights(place_ref, own_w_ref, other_w_ref, 2, f_w_ref)
         part_ref[:, 48:56, :] = jnp.zeros((OWNERS, 8, 128), F32)
@@ -287,10 +303,10 @@
     noise = jnp.concatenate(in_order(v, own, other), axis=0)
     noised = mix(samples, noise, time_ref[i])
     _, _, t_partial, t_total, t_square = forward(
-        noised, t_embed_ref, t_mods_ref, t_final_ref, t_w_ref, hidden_ref, t_shaped_ref, place_ref
+        noised, t_embed_ref, t_mods_ref, t_final_ref, t_w_ref, t_gram_ref, t_mean_ref, t_shaped_ref, place_ref
     )
     pre, res, f_partial, f_total, f_square = forward(
-        noised, f_embed_ref, f_mods_ref, f_final_ref, f_w_ref, hidden_ref, shaped_ref.at[0], place_ref
+        noised, f_embed_ref, f_mods_ref, f_final_ref, f_w_ref, f_gram_ref, f_mean_ref, shaped_ref.at[0], place_ref
     )
     pre_ref[0] = pre
     res_ref[0] = res
@@ -404,8 +420,11 @@
         total = got_ref[0, rows].astype(F32)
         for k in range(1, CHUNKS):
             total = total + got_ref[k, rows].astype(F32)
-        low = jnp.concatenate([total[:ROWS], total[2 * ROWS :, :NARROW]], axis=1)
-        high = jnp.concatenate([total[ROWS : 2 * ROWS], total[2 * ROWS :, NARROW:]], axis=1)
+        def folded(rows, part):
+            return jnp.concatenate([rows, jnp.concatenate([part[:48], part[48:]], axis=1)], axis=0)
+
+        low = folded(total[:ROWS], total[2 * ROWS :, :NARROW])
+        high = folded(total[ROWS : 2 * ROWS], total[2 * ROWS :, NARROW:])
         keep_ref[n] = jnp.where(v == 0, low, high)
         send_ref[n] = jnp.where(v == 0, high, low)
 
@@ -413,9 +432,10 @@
 def place_kernel(place_ref, keep_ref, other_ref, fake_ref, gen_ref):
     for n, ref in enumerate((fake_ref, gen_ref)):
         low, high = in_order(place_ref[0], keep_ref[n], other_ref[n])
-        ref[:, :128] = low[:, :WIDE]
-        ref[:, 128:256] = jnp.concatenate([low[:, WIDE:], high[:, WIDE:]], axis=1)
-        ref[:, 256:] = high[:, :WIDE]
+        ref[:, :128] = low[:ROWS]
+        ref[:48, 128:256] = jnp.concatenate([low[ROWS:, :NARROW], high[ROWS:, :NARROW]], axis=1)
+        ref[48:, 128:256] = jnp.concatenate([low[ROWS:, NARROW:], high[ROWS:, NARROW:]], axis=1)
+        ref[:, 256:] = high[:ROWS]
 
 
 def in_hbm(*arrays):
@@ -505,13 +525,12 @@
         ],
         out_specs=[whole((OWNERS, 32, 128)), by_image(TOKENS, D), by_image(TOKENS, COLS), by_image(TOKENS, COLS)],
         out_shape=[jax.ShapeDtypeStruct((OWNERS, 32, 128), F32), wide, local, local],
-        scratch_shapes=[pltpu.VMEM((D, COLS), BF16), pltpu.VMEM((TOKENS, D), F32)],
+        scratch_shapes=[pltpu.VMEM((D, COLS), BF16), pltpu.VMEM((C, 3 * C), BF16), pltpu.VMEM((C, 128), F32)],
         compiler_params=params(16),
         cost_estimate=pl.CostEstimate(flops=12 * 10**9, bytes_accessed=30 * 10**6, transcendentals=0),
         name="generator",
     )(place, mine, other, gen_embed, mods, gen_final, g_packed, g_other)
     packed, part = lax.optimization_barrier((packed, part))
-    other_packed = lax.ppermute(packed, "s", SIBLING)
     part = exchange(part, COMBINE)
 
     net_mods = lambda net: pl.BlockSpec((IMAGES, 8, D), lambda *_: (net, 0, 0))
@@ -530,7 +549,9 @@
         compiler_params=params(5),
         name="samples",
     )(place, gen_time, part, mine, mods, gen_final)
+    packed, pack1 = lax.optimization_barrier((packed, pack1))
     pack1 = exchange(pack1, COMBINE)
+    other_packed = lax.ppermute(packed, "s", SIBLING)
 
     part2, samples, f_shaped, f_pre, f_res = pl.pallas_call(
         score_kernel,
@@ -550,15 +571,14 @@
             wide, local, local,
         ],
         scratch_shapes=[
-            pltpu.VMEM((D, COLS), BF16), pltpu.VMEM((D, COLS), BF16), pltpu.VMEM((TOKENS, D), F32),
-            pltpu.VMEM((TOKENS, D), BF16),
+            *([pltpu.VMEM((D, COLS), BF16)] * 2), *([pltpu.VMEM((C, 3 * C), BF16)] * 2),
+            *([pltpu.VMEM((C, 128), F32)] * 2), pltpu.VMEM((TOKENS, D), BF16),
         ],
         compiler_params=params(22),
         cost_estimate=pl.CostEstimate(flops=24 * 10**9, bytes_accessed=50 * 10**6, transcendentals=0),
         name="score",
     )(place, score_time, pack1, mine, other, teacher_embed, fake_embed, mods, mods,
       teacher_final, fake_final, packed, other_packed)
-    samples = lax.ppermute(samples, PLACES, SWAP).transpose(0, 2, 1)
     part2 = exchange(part2, COMBINE)
 
     pack2 = pl.pallas_call(
@@ -574,6 +594,8 @@
         name="cotangents",
     )(place, gen_time, score_time, part2, mine, keep, sums, mods, mods, teacher_final, fake_final)
     pack2 = exchange(pack2, COMBINE)
+    samples, pack2 = lax.optimization_barrier((samples, pack2))
+    samples = lax.ppermute(samples, PLACES, SWAP)
 
     gap = jnp.sum(pack2[:, 48:57, 96].astype(F32).reshape(OWNERS, 3, 3), axis=(0, 2))
     gap = jnp.broadcast_to(jnp.pad(gap, (0, 5))[None, :, None], (16, 8, 128))
@@ -605,12 +627,14 @@
     both = jnp.concatenate(
         [(pieces[n].astype(F32) + pieces[n + 1].astype(F32)).astype(BF16) for n in (0, 2)], axis=1
     )
-    tiles = jax.ShapeDtypeStruct((2, ROWS, COLS), F32)
+    samples, both = lax.optimization_barrier((samples, both))
+    samples = samples.transpose(0, 2, 1)
+    tiles = jax.ShapeDtypeStruct((2, 144, 128), F32)
     kept, sent = pl.pallas_call(
         sum_kernel,
         grid=(1,),
         in_specs=[smem(), whole((CHUNKS, 2 * GEN_ROWS, 128))],
-        out_specs=[whole((2, ROWS, COLS))] * 2,
+        out_specs=[whole((2, 144, 128))] * 2,
         out_shape=[tiles, tiles],
         compiler_params=params(8),
         name="sum",
@@ -620,7 +644,7 @@
     fake_grad, gen_grad = pl.pallas_call(
         place_kernel,
         grid=(1,),
-        in_specs=[smem(), whole((2, ROWS, COLS)), whole((2, ROWS, COLS))],
+        in_specs=[smem(), whole((2, 144, 128)), whole((2, 144, 128))],
         out_specs=[whole((ROWS, 384))] * 2,
         out_shape=[jax.ShapeDtypeStruct((ROWS, 384), F32)] * 2,
         compiler_params=params(4),

time: 227 us -> 223 us (0.982)
  waiting for transfers between devices: 37.6 us -> 44.5 us
  Pallas kernels: 48.1 us -> 42.6 us
  blocking collectives: 82.4 us -> 76.9 us
    ppermute x1, waiting for transfers between devices: 0.01 us -> 6.94 us  [shards(): sent = lax.ppermute(sent, PLACES, SWAP_TURNED)]
    all_to_all x5, blocking collectives: 82.4 us -> 76.9 us  [exchange(): return lax.all_to_all(value, axes, 0, 0)]
    pallas_call x1, Pallas kernels: 17.2 us -> 13.1 us  [shards(): pl.pallas_call(score_kernel, grid=(IMAGES,), in_specs=[smem(), smem(), wh...]
    ppermute x1, waiting for transfers between devices: 0.01 us -> 2.43 us  [shards(): kept = lax.ppermute(kept, PLACES, SWAP)]
    ppermute x1, starting transfers between devices: 0.95 us -> 3.29 us  [shards(): other_packed = lax.ppermute(packed, 's', SIBLING)]
  transfers between devices with their start and end apart: 12 -> 12, of which waited for: 7 -> 8; matrix products, arithmetic and copies ran while one was open for 2% -> 2% of each run, Pallas kernels for 10% -> 9%
where the time goes in v3:
time: 223 us; the launch traced here: 222 us
  blocking collectives  76.9 us (34%)
  starting transfers between devices  48.1 us (22%)
  waiting for transfers between devices  44.5 us (20%)
  Pallas kernels  42.6 us (19%)
  local copies, waits for them, and re-layouts  5.49 us (2%)
  other arithmetic  3.74 us (2%)
    all_to_all x5, blocking collectives, exchange(): return lax.all_to_all(value, axes, 0, 0)  76.9 us
    all_to_all x3, starting transfers between devices, exchange(): return lax.all_to_all(value, axes, 0, 0)  19 us
    all_to_all x3, waiting for transfers between devices, exchange(): return lax.all_to_all(value, axes, 0, 0)  15.7 us
    pallas_call x1, Pallas kernels, shards(): pl.pallas_call(score_kernel, grid=(IMAGES,), in_specs=[smem(), smem(), wh...  13.1 us
    pallas_call x2, Pallas kernels, gradient(): pl.pallas_call(functools.partial(gradient_kernel, net), grid=(4,), in_spe...  12.2 us
    ppermute x1, waiting for transfers between devices, shards(): other = lax.ppermute(other, PLACES, SWAP_TURNED)  10.6 us
    ppermute x1, starting transfers between devices, shards(): mine = lax.ppermute(mine, PLACES, SWAP)  10.2 us
    pallas_call x1, Pallas kernels, shards(): pl.pallas_call(generator_kernel, grid=(IMAGES,), in_specs=[smem(), noise_...  7.85 us
  transfers between devices with their start and end apart: 12, of which 8 were waited for; matrix products, arithmetic and copies ran while one was open for 2% of the time, Pallas kernels for 9%

profile of v3, /device:TPU:1, one launch (start us, length us, event | category | flops | bytes accessed | tf_op | source)
XLA Modules:
  0.0 222.2 jit_solution(9799747396783853582)
XLA Ops:
  0.7 0.8 broadcast_multiply_fusion
  1.4 0.1 multiply_cosine_fusion
  1.5 0.6 multiply_convert_fusion.cond_ref
  2.1 0.6 stack.32.place_ref
  2.7 2.4 %split.1 = (bf16[912,128]{1,0:T(8,128)(2,1)}, bf16[912,128]{1,0:T(8,128)(2,1)}) custom-call(s32[5]{0:T(128)} %stack.32.place_ref, bf16[6,256]{1,0:T(8,128)(2,1)} %multiply_convert_fusion.cond_ref, bf16[3,64,128]{2,1,0:T(8,128)(2,1)} %bitcast.34, bf16[3,64,128]{2,1,0:T(8,128)(2,1)} %bitcast.35, bf16[96,384]{1,0:T(8,128)(2,1)} %gen_ref.1, ...), custom_call_target="tpu_custom_call" | custom-call | tf_op jit(solution)/shard_map/split/pallas_call | solution.py:476
  5.1 10.2 %collective-permute-start = (bf16[912,128]{1,0:T(8,128)(2,1)}, bf16[912,128]{1,0:T(8,128)(2,1)S(1)}, u32[]{:S(2)}, u32[]{:S(2)}) collective-permute-start(bf16[912,128]{1,0:T(8,128)(2,1)} %get-tuple-element.38), channel_id=1, source_target_pairs={{0,0},{1,8},{4,4},{5,12},{8,1},{9,9},{12,5},{13,13},{2,2},{3,10},{... | collective-permute-start | bytes 700424 | tf_op jit(solution)/shard_map/ppermute | solution.py:487
  15.3 2.7 %collective-permute-start.1 = (bf16[912,128]{1,0:T(8,128)(2,1)}, bf16[912,128]{1,0:T(8,128)(2,1)S(1)}, u32[]{:S(2)}, u32[]{:S(2)}) collective-permute-start(bf16[912,128]{1,0:T(8,128)(2,1)} %get-tuple-element.39), channel_id=1, source_target_pairs={{0,4},{1,12},{4,0},{5,8},{8,5},{9,13},{12,1},{13,9},{2,6},{3,14},{... | collective-permute-start | bytes 700424 | tf_op jit(solution)/shard_map/ppermute | solution.py:488
  18.1 1.3 collective-permute-done.mine_ref.own_ref.noise_ref
  19.4 10.6 %collective-permute-done.1.other_ref = bf16[912,128]{1,0:T(8,128)(2,1)S(1)} collective-permute-done((bf16[912,128]{1,0:T(8,128)(2,1)}, bf16[912,128]{1,0:T(8,128)(2,1)S(1)}, u32[]{:S(2)}, u32[]{:S(2)}) %collective-permute-start.1) | collective-permute-done | bytes 233504 | tf_op jit(solution)/shard_map/ppermute | solution.py:488
  30.0 0.0 copy-start.2
  30.0 0.6 copy-done.2
  30.6 1.8 pack.1
  32.4 13.5 %all_to_all.40.own_w_ref = bf16[8,368,128]{2,1,0:T(8,128)(2,1)S(1)} all-to-all(bf16[8,368,128]{2,1,0:T(8,128)(2,1)S(1)} %get-tuple-element.41), channel_id=1, replica_groups=mesh['g'=4,'x'=4,'h'=2,'v'=2,'w'=2,'s'=2] {'x','w'}, dimensions={0} | all-to-all | bytes 1507328 | tf_op jit(solution)/shard_map/all_to_all | solution.py:446
  45.9 0.0 collective-permute-start.2
  45.9 2.2 %collective-permute-done.2.other_w_ref = bf16[8,368,128]{2,1,0:T(8,128)(2,1)S(1)} collective-permute-done((bf16[8,368,128]{2,1,0:T(8,128)(2,1)S(1)}, bf16[8,368,128]{2,1,0:T(8,128)(2,1)S(1)}, u32[]{:S(2)}, u32[]{:S(2)}) %collective-permute-start.2) | collective-permute-done | bytes 753696 | tf_op jit(solution)/shard_map/ppermute | solution.py:503
  48.1 3.6 %all-to-all-start.1 = ((bf16[8,576,128]{2,1,0:T(8,128)(2,1)}), bf16[8,576,128]{2,1,0:T(8,128)(2,1)S(1)}, u32[]{:S(2)}, u32[]{:S(2)}) async-start(bf16[8,576,128]{2,1,0:T(8,128)(2,1)} %get-tuple-element.42), calls=%async_computation.1 | async-start | bytes 2359296 | tf_op jit(solution)/shard_map/all_to_all | solution.py:446
  51.7 0.0 copy-done
  51.8 0.4 maximum_bitcast_fusion
  52.2 0.1 copy.24
  52.4 0.1 reshape.44
  52.5 0.0 copy-start.3
  52.5 1.4 convert_element_type.43
  53.9 1.1 pad_convert_fusion.mods_ref.t_mods_ref.f_mods_ref.refs_0_.refs_1_
  55.0 0.0 copy-done.3
  55.0 0.0 copy-start.1
  55.1 1.1 copy-done.1
  56.2 7.8 %generator.1 = (f32[16,32,128]{2,1,0:T(8,128)}, bf16[3,256,3072]{2,1,0:T(8,128)(2,1)}, f32[3,256,192]{2,1,0:T(8,128)}, f32[3,256,192]{2,1,0:T(8,128)}) custom-call(s32[5]{0:T(128)S(1)} %copy-done.3, bf16[912,128]{1,0:T(8,128)(2,1)S(1)} %collective-permute-done.mine_ref.own_ref.noise_ref, bf16[912,128]{1,0:T(8,128)(2,1)S(1)} %collective-permute-done.1.other_ref, ...), custom_call_target="tpu_custom_call" | custom-call | flops 12000000000 | bytes 30000000 | tf_op jit(solution)/shard_map/generator/pallas_call | solution.py:519
  64.0 6.4 %all-to-all-done.1.own_w_ref = bf16[8,576,128]{2,1,0:T(8,128)(2,1)S(1)} async-done(((bf16[8,576,128]{2,1,0:T(8,128)(2,1)}), bf16[8,576,128]{2,1,0:T(8,128)(2,1)S(1)}, u32[]{:S(2)}, u32[]{:S(2)}) %all-to-all-start.1) | async-done | bytes 1179680 | tf_op jit(solution)/shard_map/all_to_all | solution.py:446
  70.5 8.6 %all-to-all-start.2 = ((f32[16,32,128]{2,1,0:T(8,128)}), f32[16,32,128]{2,1,0:T(8,128)S(1)}, u32[]{:S(2)}, u32[]{:S(2)}) async-start(f32[16,32,128]{2,1,0:T(8,128)} %get-tuple-element.47), calls=%async_computation.2 | async-start | bytes 524288 | tf_op jit(solution)/shard_map/all_to_all | solution.py:446
  79.1 0.1 fusion.2
  79.2 9.3 %all-to-all-done.2.got_ref = f32[16,32,128]{2,1,0:T(8,128)S(1)} async-done(((f32[16,32,128]{2,1,0:T(8,128)}), f32[16,32,128]{2,1,0:T(8,128)S(1)}, u32[]{:S(2)}, u32[]{:S(2)}) %all-to-all-start.2) | async-done | bytes 262176 | tf_op jit(solution)/shard_map/all_to_all | solution.py:446
  88.4 1.3 samples.1
  89.7 3.3 %collective-permute-start.3 = (bf16[8,576,128]{2,1,0:T(8,128)(2,1)S(1)}, bf16[8,576,128]{2,1,0:T(8,128)(2,1)S(1)}, u32[]{:S(2)}, u32[]{:S(2)}) collective-permute-start(bf16[8,576,128]{2,1,0:T(8,128)(2,1)S(1)} %all-to-all-done.1.own_w_ref), channel_id=1, source_target_pairs={{0,1},{1,0},{2,3},{3,2},{4,5},{5,4},{6,7},{7,6},{8,9},{9,8},{10,11... | collective-permute-start | bytes 3538952 | tf_op jit(solution)/shard_map/ppermute | solution.py:554
  93.0 13.2 %all_to_all.41.got_ref = f32[16,24,128]{2,1,0:T(8,128)S(1)} all-to-all(f32[16,24,128]{2,1,0:T(8,128)S(1)} %get-tuple-element.49), channel_id=1, replica_groups=mesh['g'=4,'x'=4,'h'=2,'v'=2,'w'=2,'s'=2] {'v','h','g'}, dimensions={0} | all-to-all | bytes 393216 | tf_op jit(solution)/shard_map/all_to_all | solution.py:446
  106.3 0.0 collective-permute-done.3.other_w_ref
  106.3 13.1 %score.1 = (f32[16,56,128]{2,1,0:T(8,128)S(1)}, f32[3,64,128]{2,1,0:T(8,128)S(1)}, bf16[3,256,3072]{2,1,0:T(8,128)(2,1)}, f32[3,256,192]{2,1,0:T(8,128)}, f32[3,256,192]{2,1,0:T(8,128)}) custom-call(s32[5]{0:T(128)S(1)} %copy-done.3, f32[3]{0:T(128)S(1)} %get-tuple-element.80.time_ref, f32[16,24,128]{2,1,0:T(8,128)S(1)} %all_to_all.41.got_ref, ...), custom_call_target="tpu_custom_call" | custom-call | flops 24000000000 | bytes 50000000 | tf_op jit(solution)/shard_map/score/pallas_call | solution.py:556
  119.3 18.3 %all_to_all.42.got_ref = f32[16,56,128]{2,1,0:T(8,128)S(1)} all-to-all(f32[16,56,128]{2,1,0:T(8,128)S(1)} %get-tuple-element.52), channel_id=1, replica_groups=mesh['g'=4,'x'=4,'h'=2,'v'=2,'w'=2,'s'=2] {'v','h','g'}, dimensions={0} | all-to-all | bytes 917504 | tf_op jit(solution)/shard_map/all_to_all | solution.py:446
  137.6 1.8 cotangents.1
  139.5 15.8 %all_to_all.43.got_ref = bf16[16,64,128]{2,1,0:T(8,128)(2,1)S(1)} all-to-all(bf16[16,64,128]{2,1,0:T(8,128)(2,1)S(1)} %cotangents.1), channel_id=1, replica_groups=mesh['g'=4,'x'=4,'h'=2,'v'=2,'w'=2,'s'=2] {'v','h','g'}, dimensions={0} | all-to-all | bytes 524288 | tf_op jit(solution)/shard_map/all_to_all | solution.py:446
  155.3 0.2 convert_reduce_fusion
  155.5 0.1 reduce_sum.14
  155.5 0.1 reduce_sum.18
  155.7 0.7 broadcast_in_dim.2
  156.4 6.8 %all-to-all-start.6 = ((f32[16,8,128]{2,1,0:T(8,128)}), f32[16,8,128]{2,1,0:T(8,128)S(1)}, u32[]{:S(2)}, u32[]{:S(2)}) async-start(f32[16,8,128]{2,1,0:T(8,128)} %broadcast_in_dim.2), calls=%async_computation.6 | async-start | bytes 131072 | tf_op jit(solution)/shard_map/all_to_all | solution.py:446
  163.2 6.0 %gradient.2 = (bf16[8,288,128]{2,1,0:T(8,128)(2,1)S(1)}, bf16[8,288,128]{2,1,0:T(8,128)(2,1)S(1)}) custom-call(s32[5]{0:T(128)S(1)} %copy-done.3, bf16[16,64,128]{2,1,0:T(8,128)(2,1)S(1)} %all_to_all.43.got_ref, f32[9,8,3072]{2,1,0:T(8,128)S(1)} %pad_convert_fusion.mods_ref.t_mods_ref.f_mods_ref.refs_0_.refs_1_, bf16[64,3072]{1,0:T(8,128)(2,1)} %bitcast.29, ...), custom_call_target="tpu_custom_call" | custom-call | flops 7000000000 | bytes 20000000 | tf_op jit(solution)/shard_map/gradient/pallas_call | solution.py:609
  169.2 0.3 collective-permute-start.5
  169.6 0.0 all-to-all-done.6.refs_0_
  169.6 6.1 %gradient.3 = (bf16[8,288,128]{2,1,0:T(8,128)(2,1)S(1)}, bf16[8,288,128]{2,1,0:T(8,128)(2,1)S(1)}) custom-call(s32[5]{0:T(128)S(1)} %copy-done.3, bf16[16,64,128]{2,1,0:T(8,128)(2,1)S(1)} %all_to_all.43.got_ref, f32[16,8,128]{2,1,0:T(8,128)S(1)} %all-to-all-done.6.refs_0_, f32[9,8,3072]{2,1,0:T(8,128)S(1)} %pad_convert_fusion.mods_ref.t_mods_ref.f_mods_ref.refs_0_.refs_1_, ...), custom_call_target="tpu_custom_call" | custom-call | flops 7000000000 | bytes 20000000 | tf_op jit(solution)/shard_map/gradient/pallas_call | solution.py:609
  175.7 0.4 collective-permute-start.6
  176.1 4.2 %collective-permute-start.4 = (f32[3,64,128]{2,1,0:T(8,128)S(1)}, f32[3,64,128]{2,1,0:T(8,128)S(1)}, u32[]{:S(2)}, u32[]{:S(2)}) collective-permute-start(f32[3,64,128]{2,1,0:T(8,128)S(1)} %get-tuple-element.55), channel_id=1, source_target_pairs={{0,0},{1,8},{4,4},{5,12},{8,1},{9,9},{12,5},{13,13},{2,2},{3,10},{... | collective-permute-start | bytes 294920 | tf_op jit(solution)/shard_map/ppermute | solution.py:598
  180.3 0.0 collective-permute-done.5
  180.3 0.2 add_convert_fusion.1
  180.5 0.0 collective-permute-done.6
  180.5 0.2 add_convert_fusion
  180.6 0.1 pad_maximum_fusion
  180.7 5.3 %collective-permute-done.4 = f32[3,64,128]{2,1,0:T(8,128)S(1)} collective-permute-done((f32[3,64,128]{2,1,0:T(8,128)S(1)}, f32[3,64,128]{2,1,0:T(8,128)S(1)}, u32[]{:S(2)}, u32[]{:S(2)}) %collective-permute-start.4) | collective-permute-done | bytes 98336 | tf_op jit(solution)/shard_map/ppermute | solution.py:598
  186.0 16.1 %all_to_all.44.got_ref = bf16[8,576,128]{2,1,0:T(8,128)(2,1)S(1)} all-to-all(bf16[8,576,128]{2,1,0:T(8,128)(2,1)S(1)} %pad_maximum_fusion), channel_id=1, replica_groups=mesh['g'=4,'x'=4,'h'=2,'v'=2,'w'=2,'s'=2] {'x','w'}, dimensions={0} | all-to-all | bytes 2359296 | tf_op jit(solution)/shard_map/all_to_all | solution.py:446
  202.1 0.7 sum.1
  202.8 5.5 %collective-permute-start.7 = (f32[2,144,128]{2,1,0:T(8,128)S(1)}, f32[2,144,128]{2,1,0:T(8,128)S(1)}, u32[]{:S(2)}, u32[]{:S(2)}) collective-permute-start(f32[2,144,128]{2,1,0:T(8,128)S(1)} %get-tuple-element.69), channel_id=1, source_target_pairs={{0,0},{1,8},{4,4},{5,12},{8,1},{9,9},{12,5},{13,13},{2,2},{3,10},{... | collective-permute-start | bytes 442376 | tf_op jit(solution)/shard_map/ppermute | solution.py:642
  208.3 2.5 %collective-permute-start.8 = (f32[2,144,128]{2,1,0:T(8,128)S(1)}, f32[2,144,128]{2,1,0:T(8,128)S(1)}, u32[]{:S(2)}, u32[]{:S(2)}) collective-permute-start(f32[2,144,128]{2,1,0:T(8,128)S(1)} %get-tuple-element.70), channel_id=1, source_target_pairs={{0,4},{1,12},{4,0},{5,8},{8,5},{9,13},{12,1},{13,9},{2,6},{3,14},{... | collective-permute-start | bytes 442376 | tf_op jit(solution)/shard_map/ppermute | solution.py:643
  210.8 2.4 %collective-permute-done.7.keep_ref = f32[2,144,128]{2,1,0:T(8,128)S(1)} collective-permute-done((f32[2,144,128]{2,1,0:T(8,128)S(1)}, f32[2,144,128]{2,1,0:T(8,128)S(1)}, u32[]{:S(2)}, u32[]{:S(2)}) %collective-permute-start.7) | collective-permute-done | bytes 147488 | tf_op jit(solution)/shard_map/ppermute | solution.py:642
  213.3 6.9 %collective-permute-done.8.other_ref = f32[2,144,128]{2,1,0:T(8,128)S(1)} collective-permute-done((f32[2,144,128]{2,1,0:T(8,128)S(1)}, f32[2,144,128]{2,1,0:T(8,128)S(1)}, u32[]{:S(2)}, u32[]{:S(2)}) %collective-permute-start.8) | collective-permute-done | bytes 147488 | tf_op jit(solution)/shard_map/ppermute | solution.py:643
  220.2 1.3 place.1
  221.6 0.6 copy.26
  (7 shorter events, 0.1 us)
Async XLA Ops:
  5.1 14.2 %collective-permute-start = (bf16[912,128]{1,0:T(8,128)(2,1)}, bf16[912,128]{1,0:T(8,128)(2,1)S(1)}, u32[]{:S(2)}, u32[]{:S(2)}) collective-permute-start(bf16[912,128]{1,0:T(8,128)(2,1)} %get-tuple-element.38), channel_id=1, source_target_pairs={{0,0},{1,8},{4,4},{5,12},{8,1},{9,9},{12,5},{13,13},{2,2},{3,10},{... | collective-permute-start | bytes 700424 | tf_op jit(solution)/shard_map/ppermute | solution.py:487
  15.3 14.6 %collective-permute-start.1 = (bf16[912,128]{1,0:T(8,128)(2,1)}, bf16[912,128]{1,0:T(8,128)(2,1)S(1)}, u32[]{:S(2)}, u32[]{:S(2)}) collective-permute-start(bf16[912,128]{1,0:T(8,128)(2,1)} %get-tuple-element.39), channel_id=1, source_target_pairs={{0,4},{1,12},{4,0},{5,8},{8,5},{9,13},{12,1},{13,9},{2,6},{3,14},{... | collective-permute-start | bytes 700424 | tf_op jit(solution)/shard_map/ppermute | solution.py:488
  30.0 0.6 copy-start.2
  45.9 2.2 %collective-permute-start.2 = (bf16[8,368,128]{2,1,0:T(8,128)(2,1)S(1)}, bf16[8,368,128]{2,1,0:T(8,128)(2,1)S(1)}, u32[]{:S(2)}, u32[]{:S(2)}) collective-permute-start(bf16[8,368,128]{2,1,0:T(8,128)(2,1)S(1)} %all_to_all.40.own_w_ref), channel_id=1, source_target_pairs={{0,1},{1,0},{2,3},{3,2},{4,5},{5,4},{6,7},{7,6},{8,9},{9,8},{10,11... | collective-permute-start | bytes 2261000 | tf_op jit(solution)/shard_map/ppermute | solution.py:503
  48.1 3.6 %copy-start = (bf16[8,368,128]{2,1,0:T(8,128)(2,1)}, bf16[8,368,128]{2,1,0:T(8,128)(2,1)S(1)}, u32[]{:S(2)}) copy-start(bf16[8,368,128]{2,1,0:T(8,128)(2,1)S(1)} %collective-permute-done.2.other_w_ref) | copy-start | bytes 2260996
  48.1 22.3 %all-to-all-start.1 = ((bf16[8,576,128]{2,1,0:T(8,128)(2,1)}), bf16[8,576,128]{2,1,0:T(8,128)(2,1)S(1)}, u32[]{:S(2)}, u32[]{:S(2)}) async-start(bf16[8,576,128]{2,1,0:T(8,128)(2,1)} %get-tuple-element.42), calls=%async_computation.1 | async-start | bytes 2359296 | tf_op jit(solution)/shard_map/all_to_all | solution.py:446
  52.5 2.5 %copy-start.3 = (s32[5]{0:T(128)S(1)}, s32[5]{0:T(128)}, u32[]{:S(2)}) copy-start(s32[5]{0:T(128)} %stack.32.place_ref) | copy-start | bytes 64
  55.0 1.1 copy-start.1
  70.5 18.0 %all-to-all-start.2 = ((f32[16,32,128]{2,1,0:T(8,128)}), f32[16,32,128]{2,1,0:T(8,128)S(1)}, u32[]{:S(2)}, u32[]{:S(2)}) async-start(f32[16,32,128]{2,1,0:T(8,128)} %get-tuple-element.47), calls=%async_computation.2 | async-start | bytes 524288 | tf_op jit(solution)/shard_map/all_to_all | solution.py:446
  89.7 16.5 %collective-permute-start.3 = (bf16[8,576,128]{2,1,0:T(8,128)(2,1)S(1)}, bf16[8,576,128]{2,1,0:T(8,128)(2,1)S(1)}, u32[]{:S(2)}, u32[]{:S(2)}) collective-permute-start(bf16[8,576,128]{2,1,0:T(8,128)(2,1)S(1)} %all-to-all-done.1.own_w_ref), channel_id=1, source_target_pairs={{0,1},{1,0},{2,3},{3,2},{4,5},{5,4},{6,7},{7,6},{8,9},{9,8},{10,11... | collective-permute-start | bytes 3538952 | tf_op jit(solution)/shard_map/ppermute | solution.py:554
  156.4 13.2 %all-to-all-start.6 = ((f32[16,8,128]{2,1,0:T(8,128)}), f32[16,8,128]{2,1,0:T(8,128)S(1)}, u32[]{:S(2)}, u32[]{:S(2)}) async-start(f32[16,8,128]{2,1,0:T(8,128)} %broadcast_in_dim.2), calls=%async_computation.6 | async-start | bytes 131072 | tf_op jit(solution)/shard_map/all_to_all | solution.py:446
  169.2 11.1 %collective-permute-start.5 = (bf16[8,288,128]{2,1,0:T(8,128)(2,1)S(1)}, bf16[8,288,128]{2,1,0:T(8,128)(2,1)S(1)}, u32[]{:S(2)}, u32[]{:S(2)}) collective-permute-start(bf16[8,288,128]{2,1,0:T(8,128)(2,1)S(1)} %get-tuple-element.61), channel_id=1, source_target_pairs={{0,1},{1,0},{2,3},{3,2},{4,5},{5,4},{6,7},{7,6},{8,9},{9,8},{10,11... | collective-permute-start | bytes 1769480 | tf_op jit(solution)/shard_map/ppermute | solution.py:623
  175.7 4.8 %collective-permute-start.6 = (bf16[8,288,128]{2,1,0:T(8,128)(2,1)S(1)}, bf16[8,288,128]{2,1,0:T(8,128)(2,1)S(1)}, u32[]{:S(2)}, u32[]{:S(2)}) collective-permute-start(bf16[8,288,128]{2,1,0:T(8,128)(2,1)S(1)} %get-tuple-element.66), channel_id=1, source_target_pairs={{0,1},{1,0},{2,3},{3,2},{4,5},{5,4},{6,7},{7,6},{8,9},{9,8},{10,11... | collective-permute-start | bytes 1769480 | tf_op jit(solution)/shard_map/ppermute | solution.py:623
  176.1 9.9 %collective-permute-start.4 = (f32[3,64,128]{2,1,0:T(8,128)S(1)}, f32[3,64,128]{2,1,0:T(8,128)S(1)}, u32[]{:S(2)}, u32[]{:S(2)}) collective-permute-start(f32[3,64,128]{2,1,0:T(8,128)S(1)} %get-tuple-element.55), channel_id=1, source_target_pairs={{0,0},{1,8},{4,4},{5,12},{8,1},{9,9},{12,5},{13,13},{2,2},{3,10},{... | collective-permute-start | bytes 294920 | tf_op jit(solution)/shard_map/ppermute | solution.py:598
  202.8 10.5 %collective-permute-start.7 = (f32[2,144,128]{2,1,0:T(8,128)S(1)}, f32[2,144,128]{2,1,0:T(8,128)S(1)}, u32[]{:S(2)}, u32[]{:S(2)}) collective-permute-start(f32[2,144,128]{2,1,0:T(8,128)S(1)} %get-tuple-element.69), channel_id=1, source_target_pairs={{0,0},{1,8},{4,4},{5,12},{8,1},{9,9},{12,5},{13,13},{2,2},{3,10},{... | collective-permute-start | bytes 442376 | tf_op jit(solution)/shard_map/ppermute | solution.py:642
  208.3 11.9 %collective-permute-start.8 = (f32[2,144,128]{2,1,0:T(8,128)S(1)}, f32[2,144,128]{2,1,0:T(8,128)S(1)}, u32[]{:S(2)}, u32[]{:S(2)}) collective-permute-start(f32[2,144,128]{2,1,0:T(8,128)S(1)} %get-tuple-element.70), channel_id=1, source_target_pairs={{0,4},{1,12},{4,0},{5,8},{8,5},{9,13},{12,1},{13,9},{2,6},{3,14},{... | collective-permute-start | bytes 442376 | tf_op jit(solution)/shard_map/ppermute | solution.py:643

commit v4 on v3

--- a/solution.py
+++ b/solution.py
@@ -87,6 +87,21 @@
     for k, number in enumerate(numbers):
         total = jnp.where(lane == token + OWNED * k, number, total)
     return jnp.sum(total, axis=1, keepdims=True)
+
+
+def row_pieces(numbers, stride):
+    row = to_row(numbers)
+    per_row = 128 // stride
+    rows = [row.astype(BF16).astype(F32)]
+    row = row - rows[0]
+    rows.append(row.astype(BF16).astype(F32))
+    rows.append((row - rows[1]).astype(BF16).astype(F32))
+    packed = [jnp.concatenate([r[:, :, :stride] for r in rows[:per_row]], axis=2)]
+    if len(rows) > per_row:
+        packed.append(jnp.concatenate([rows[per_row][:, :, :stride], jnp.zeros_like(row)[:, :, : 128 - stride]], axis=2))
+    else:
+        packed[0] = jnp.concatenate([packed[0], jnp.zeros_like(row)[:, :, : 128 - 3 * stride]], axis=2)
+    return packed
 
 
 def from_row(row, k):
@@ -163,10 +178,7 @@
     own_mean = total / COLS
     final = local_lanes(lambda at: final_ref[:, at], place_ref)
     centred = ((residual - own_mean) * (1.0 + scale)).astype(BF16)
-    ones = jnp.ones((8, COLS), BF16)
-    column = dot_turned(jnp.concatenate([ones, jnp.broadcast_to(scale, (8, COLS)).astype(BF16)], axis=0), final)
-    column = column[0:1] + column[8:9]
-    partial = dot_turned(centred, final) + own_mean * column
+    partial = dot_turned(centred, final)
     return preactivation, residual, partial, total, total_square
 
 
@@ -177,9 +189,24 @@
 def final_sums(mods_ref, final_ref):
     scales = [mods_ref[i, 4:5, :] for i in range(IMAGES)]
     shifts = [mods_ref[i, 3:4, :] for i in range(IMAGES)]
-    left = jnp.concatenate(scales + shifts + [jnp.ones((2, D), F32)], axis=0).astype(BF16)
-    sums = dot_turned(left, final_ref[...])
-    return [sums[i : i + 1] + sums[6:7] for i in range(IMAGES)], [sums[3 + i : 4 + i] for i in range(IMAGES)]
+    run = lax.broadcasted_iota(jnp.int32, (OWNERS, D), 1) // COLS
+    own = run == lax.broadcasted_iota(jnp.int32, (OWNERS, D), 0)
+    left = [jnp.where(own, row, 0.0) for row in scales + [jnp.ones((1, D), F32)]]
+    sums = dot_turned(jnp.concatenate(left + shifts + [jnp.zeros((5, D), F32)], axis=0).astype(BF16), final_ref[...])
+    ones = sums[3 * OWNERS : 4 * OWNERS]
+    runs = [sums[i * OWNERS : (i + 1) * OWNERS] + ones for i in range(IMAGES)]
+    return runs, [jnp.sum(r, axis=0, keepdims=True) for r in runs], [sums[64 + i : 65 + i] for i in range(IMAGES)]
+
+
+def add_up(partials, totals, squares, runs):
+    means = totals * (1.0 / COLS)
+    ordered = jnp.concatenate(
+        [runs[(g * 2 + h) * 2 + v][None, None] for v in range(2) for h in range(2) for g in range(4)], axis=0
+    )
+    partial = jnp.sum(partials + means * ordered, axis=0)
+    average = jnp.sum(totals, axis=0) / D
+    inverse = lax.rsqrt(jnp.sum(squares, axis=0) / D - average * average + norm_epsilon)
+    return partial, average, inverse
 
 
 def split_kernel(place_ref, cond_ref, gen_noise_ref, score_noise_ref, gen_ref, teacher_ref, fake_ref,
@@ -229,7 +256,7 @@
 
 
 def generator_kernel(place_ref, own_ref, other_ref, embed_ref, mods_ref, final_ref, own_w_ref, other_w_ref,
-                     part_ref, shaped_ref, pre_ref, res_ref, w_ref, gram_ref, mean_ref):
+                     part_ref, shaped_ref, pre_ref, res_ref, w_ref, gram_ref, mean_ref, sum_ref):
     i = pl.program_id(0)
     v = place_ref[0]
 
@@ -237,7 +264,7 @@
     def _():
         embed_moments(embed_ref, gram_ref, mean_ref)
         unpack_weights(place_ref, own_w_ref, other_w_ref, 0, w_ref)
-        part_ref[:, 24:32, :] = jnp.zeros((OWNERS, 8, 128), F32)
+        sum_ref[:, 24:, :] = jnp.zeros((OWNERS, 8, 128), F32)
 
     x = jnp.concatenate(in_order(v, own_ref[:, :C], other_ref[:, :C]), axis=0)
     pre, res, partial, total, square = forward(
@@ -246,22 +273,28 @@
     pre_ref[0] = pre
     res_ref[0] = res
     pieces = owned(partial)
-    part_ref[:, pl.ds(pl.multiple_of(i * 8, 8), 8), :] = jnp.concatenate([pieces[:, :8], pieces[:, 8:]], axis=2)
-    part_ref[:, pl.ds(24 + i, 1), :] = to_row([owned(total), owned(square)])
+    pieces = jnp.concatenate([pieces[:, :8], pieces[:, 8:]], axis=2)
+    rows = row_pieces([owned(total), owned(square)], 32)
+    sum_ref[:, pl.ds(pl.multiple_of(i * 8, 8), 8), :] = pieces
+    sum_ref[:, pl.ds(24 + i, 1), :] = rows[0]
+
+    @pl.when(i == IMAGES - 1)
+    def _():
+        part_ref[...] = sum_ref[...].astype(BF16)
 
 
 def samples_kernel(place_ref, time_ref, got_ref, noise_ref, mods_ref, final_ref,
                    out_ref, keep_ref, sums_ref):
-    total = jnp.sum(got_ref[...], axis=0)
-    scales, shifts = final_sums(mods_ref, final_ref)
+    runs, scales, shifts = final_sums(mods_ref, final_ref)
+    got = got_ref[...].astype(F32)
     packed = []
     for i in range(IMAGES):
-        block = total[8 * i : 8 * i + 8]
-        partial = jnp.concatenate([block[:, :C], block[:, C:]], axis=0)
-        row = total[24 + i : 25 + i][None]
-        average = from_row(row, 0)[0] / D
-        square = from_row(row, 1)[0] / D
-        inverse = lax.rsqrt(square - average * average + norm_epsilon)
+        block = got[:, 8 * i : 8 * i + 8]
+        partials = jnp.concatenate([block[:, :, :C], block[:, :, C:]], axis=1)
+        row = got[:, 24 + i : 25 + i]
+        row = row[:, :, :32] + row[:, :, 32:64] + row[:, :, 64:96]
+        row = jnp.concatenate([row, jnp.zeros((OWNERS, 1, 96), F32)], axis=2)
+        partial, average, inverse = add_up(partials, from_row(row, 0), from_row(row, 1), runs[i])
         inner = inverse * (partial - average * scales[i])
         velocity = inner + shifts[i]
         noise = noise_ref[pl.ds(pl.multiple_of(place_ref[3] + i * HALF, 16), OWNED), :][:, :C].astype(F32)
@@ -283,7 +316,7 @@
 def score_kernel(place_ref, time_ref, got_ref, own_ref, other_ref,
                  t_embed_ref, f_embed_ref, t_mods_ref, f_mods_ref, t_final_ref, f_final_ref, own_w_ref, other_w_ref,
                  part_ref, samples_ref, shaped_ref, pre_ref, res_ref,
-                 t_w_ref, f_w_ref, t_gram_ref, f_gram_ref, t_mean_ref, f_mean_ref, t_shaped_ref):
+                 t_w_ref, f_w_ref, t_gram_ref, f_gram_ref, t_mean_ref, f_mean_ref, t_shaped_ref, sum_ref):
     i = pl.program_id(0)
     v = place_ref[0]
 
@@ -293,8 +326,7 @@
         embed_moments(f_embed_ref, f_gram_ref, f_mean_ref)
         unpack_weights(place_ref, own_w_ref, other_w_ref, 1, t_w_ref)
         unpack_weights(place_ref, own_w_ref, other_w_ref, 2, f_w_ref)
-        part_ref[:, 48:56, :] = jnp.zeros((OWNERS, 8, 128), F32)
-
+        sum_ref[:, 48:, :] = jnp.zeros((OWNERS, 16, 128), F32)
     got = got_ref[:, pl.ds(pl.multiple_of(i * 8, 8), 8), :]
     samples = jnp.concatenate([got[:, :, :C], got[:, :, C:]], axis=1).reshape(TOKENS, C)
     turned = jnp.concatenate([samples[:HALF], samples[HALF:]], axis=1).T
@@ -310,30 +342,36 @@
     )
     pre_ref[0] = pre
     res_ref[0] = res
-    part_ref[:, pl.ds(pl.multiple_of(i * 16, 16), 16), :] = owned(jnp.concatenate([t_partial, f_partial], axis=1))
-    part_ref[:, pl.ds(48 + i, 1), :] = to_row([owned(v) for v in (t_total, t_square, f_total, f_square)])
+    rows = row_pieces([owned(v) for v in (t_total, t_square, f_total, f_square)], 64)
+    sum_ref[:, pl.ds(pl.multiple_of(i * 16, 16), 16), :] = owned(jnp.concatenate([t_partial, f_partial], axis=1))
+    for n in range(2):
+        sum_ref[:, pl.ds(48 + 2 * i + n, 1), :] = rows[n]
+
+    @pl.when(i == IMAGES - 1)
+    def _():
+        part_ref[...] = sum_ref[...].astype(BF16)
 
 
 def cotangent_kernel(place_ref, gen_time_ref, time_ref, got_ref, noise_ref, keep_ref, sums_ref,
                      t_mods_ref, f_mods_ref, t_final_ref, f_final_ref, out_ref):
     loss_scale = 1.0 / math.sqrt(IMAGES * S)
-    total = jnp.sum(got_ref[...], axis=0)
-    t_scales, t_shifts = final_sums(t_mods_ref, t_final_ref)
-    f_scales, f_shifts = final_sums(f_mods_ref, f_final_ref)
+    t_runs, t_scales, t_shifts = final_sums(t_mods_ref, t_final_ref)
+    f_runs, f_scales, f_shifts = final_sums(f_mods_ref, f_final_ref)
+    got = got_ref[...].astype(F32)
     lane = lax.broadcasted_iota(jnp.int32, (1, 128), 1)
     cots, rows = [], []
     for i in range(IMAGES):
-        block = total[16 * i : 16 * i + 16]
-        row = total[48 + i : 49 + i][None]
-
-        def inner(partial, k, scale):
-            average = from_row(row, k)[0] / D
-            square = from_row(row, k + 1)[0] / D
-            inverse = lax.rsqrt(square - average * average + norm_epsilon)
+        block = got[:, 16 * i : 16 * i + 16]
+        row = got[:, 48 + 2 * i : 50 + 2 * i]
+        row = row[:, :1, :64] + row[:, :1, 64:] + row[:, 1:, :64]
+        row = jnp.concatenate([row, jnp.zeros((OWNERS, 1, 64), F32)], axis=2)
+
+        def inner(partials, k, runs, scale):
+            partial, average, inverse = add_up(partials, from_row(row, k), from_row(row, k + 1), runs)
             return inverse * (partial - average * scale), average, inverse
 
-        t_inner, _, _ = inner(block[:, :C], 0, t_scales[i])
-        f_inner, f_average, f_inverse = inner(block[:, C:], 2, f_scales[i])
+        t_inner, _, _ = inner(block[:, :, :C], 0, t_runs[i], t_scales[i])
+        f_inner, f_average, f_inverse = inner(block[:, :, C:], 2, f_runs[i], f_scales[i])
         teacher, fake = t_inner + t_shifts[i], f_inner + f_shifts[i]
         at = slice(i * OWNED, (i + 1) * OWNED)
         samples, g_inner = keep_ref[0, at, :], keep_ref[1, at, :]
@@ -524,8 +562,9 @@
             *([whole((CHUNKS, GEN_CHUNK, 128))] * 2),
         ],
         out_specs=[whole((OWNERS, 32, 128)), by_image(TOKENS, D), by_image(TOKENS, COLS), by_image(TOKENS, COLS)],
-        out_shape=[jax.ShapeDtypeStruct((OWNERS, 32, 128), F32), wide, local, local],
-        scratch_shapes=[pltpu.VMEM((D, COLS), BF16), pltpu.VMEM((C, 3 * C), BF16), pltpu.VMEM((C, 128), F32)],
+        out_shape=[jax.ShapeDtypeStruct((OWNERS, 32, 128), BF16), wide, local, local],
+        scratch_shapes=[pltpu.VMEM((D, COLS), BF16), pltpu.VMEM((C, 3 * C), BF16), pltpu.VMEM((C, 128), F32),
+                        pltpu.VMEM((OWNERS, 32, 128), F32)],
         compiler_params=params(16),
         cost_estimate=pl.CostEstimate(flops=12 * 10**9, bytes_accessed=30 * 10**6, transcendentals=0),
         name="generator",
@@ -562,17 +601,18 @@
             *([whole((CHUNKS, SCORE_ROWS, 128))] * 2),
         ],
         out_specs=[
-            whole((OWNERS, 56, 128)), by_image(C, HALF), by_image(TOKENS, D), by_image(TOKENS, COLS),
+            whole((OWNERS, 64, 128)), by_image(C, HALF), by_image(TOKENS, D), by_image(TOKENS, COLS),
             by_image(TOKENS, COLS),
         ],
         out_shape=[
-            jax.ShapeDtypeStruct((OWNERS, 56, 128), F32),
+            jax.ShapeDtypeStruct((OWNERS, 64, 128), BF16),
             jax.ShapeDtypeStruct((IMAGES, C, HALF), F32),
             wide, local, local,
         ],
         scratch_shapes=[
             *([pltpu.VMEM((D, COLS), BF16)] * 2), *([pltpu.VMEM((C, 3 * C), BF16)] * 2),
             *([pltpu.VMEM((C, 128), F32)] * 2), pltpu.VMEM((TOKENS, D), BF16),
+            pltpu.VMEM((OWNERS, 64, 128), F32),
         ],
         compiler_params=params(22),
         cost_estimate=pl.CostEstimate(flops=24 * 10**9, bytes_accessed=50 * 10**6, transcendentals=0),
@@ -585,7 +625,7 @@
         cotangent_kernel,
         grid=(1,),
         in_specs=[
-            smem(), smem(), smem(), whole((OWNERS, 56, 128)), whole((NOISE_ROWS, 128)), whole((4, 48, C)),
+            smem(), smem(), smem(), whole((OWNERS, 64, 128)), whole((NOISE_ROWS, 128)), whole((4, 48, C)),
             whole((8, C)), net_mods(1), net_mods(2), whole((C, D)), whole((C, D)),
         ],
         out_specs=whole((OWNERS, 64, 128)),

time: 223 us -> 218 us (0.978)
  blocking collectives: 76.9 us -> 71.6 us
    all_to_all x5, blocking collectives: 76.9 us -> 71.6 us  [exchange(): return lax.all_to_all(value, axes, 0, 0)]
where the time goes in v4:
time: 218 us; the launch traced here: 217 us
  blocking collectives  71.6 us (33%)
  starting transfers between devices  47.4 us (22%)
  Pallas kernels  44.4 us (20%)
  waiting for transfers between devices  43.7 us (20%)
  local copies, waits for them, and re-layouts  5.49 us (3%)
  other arithmetic  3.74 us (2%)
    all_to_all x5, blocking collectives, exchange(): return lax.all_to_all(value, axes, 0, 0)  71.6 us
    all_to_all x3, starting transfers between devices, exchange(): return lax.all_to_all(value, axes, 0, 0)  18.6 us
    all_to_all x3, waiting for transfers between devices, exchange(): return lax.all_to_all(value, axes, 0, 0)  15 us
    pallas_call x1, Pallas kernels, shards(): pl.pallas_call(score_kernel, grid=(IMAGES,), in_specs=[smem(), smem(), wh...  13.7 us
    pallas_call x2, Pallas kernels, gradient(): pl.pallas_call(functools.partial(gradient_kernel, net), grid=(4,), in_spe...  12.2 us
    ppermute x1, waiting for transfers between devices, shards(): other = lax.ppermute(other, PLACES, SWAP_TURNED)  10.6 us
    ppermute x1, starting transfers between devices, shards(): mine = lax.ppermute(mine, PLACES, SWAP)  10.2 us
    pallas_call x1, Pallas kernels, shards(): pl.pallas_call(generator_kernel, grid=(IMAGES,), in_specs=[smem(), noise_...  8.15 us
  transfers between devices with their start and end apart: 12, of which 8 were waited for; matrix products, arithmetic and copies ran while one was open for 2% of the time, Pallas kernels for 9%

profile of v4, /device:TPU:1, one launch (start us, length us, event | category | flops | bytes accessed | tf_op | source)
XLA Modules:
  0.0 217.2 jit_solution(10632552632744409815)
XLA Ops:
  0.7 0.8 broadcast_multiply_fusion
  1.4 0.1 multiply_cosine_fusion
  1.5 0.6 multiply_convert_fusion.cond_ref
  2.1 0.6 stack.32.place_ref
  2.7 2.4 %split.1 = (bf16[912,128]{1,0:T(8,128)(2,1)}, bf16[912,128]{1,0:T(8,128)(2,1)}) custom-call(s32[5]{0:T(128)} %stack.32.place_ref, bf16[6,256]{1,0:T(8,128)(2,1)} %multiply_convert_fusion.cond_ref, bf16[3,64,128]{2,1,0:T(8,128)(2,1)} %bitcast.34, bf16[3,64,128]{2,1,0:T(8,128)(2,1)} %bitcast.35, bf16[96,384]{1,0:T(8,128)(2,1)} %gen_ref.1, ...), custom_call_target="tpu_custom_call" | custom-call | tf_op jit(solution)/shard_map/split/pallas_call | solution.py:514
  5.1 10.2 %collective-permute-start = (bf16[912,128]{1,0:T(8,128)(2,1)}, bf16[912,128]{1,0:T(8,128)(2,1)S(1)}, u32[]{:S(2)}, u32[]{:S(2)}) collective-permute-start(bf16[912,128]{1,0:T(8,128)(2,1)} %get-tuple-element.38), channel_id=1, source_target_pairs={{0,0},{1,8},{4,4},{5,12},{8,1},{9,9},{12,5},{13,13},{2,2},{3,10},{... | collective-permute-start | bytes 700424 | tf_op jit(solution)/shard_map/ppermute | solution.py:525
  15.3 2.7 %collective-permute-start.1 = (bf16[912,128]{1,0:T(8,128)(2,1)}, bf16[912,128]{1,0:T(8,128)(2,1)S(1)}, u32[]{:S(2)}, u32[]{:S(2)}) collective-permute-start(bf16[912,128]{1,0:T(8,128)(2,1)} %get-tuple-element.39), channel_id=1, source_target_pairs={{0,4},{1,12},{4,0},{5,8},{8,5},{9,13},{12,1},{13,9},{2,6},{3,14},{... | collective-permute-start | bytes 700424 | tf_op jit(solution)/shard_map/ppermute | solution.py:526
  18.1 1.3 collective-permute-done.mine_ref.own_ref.noise_ref
  19.4 10.6 %collective-permute-done.1.other_ref = bf16[912,128]{1,0:T(8,128)(2,1)S(1)} collective-permute-done((bf16[912,128]{1,0:T(8,128)(2,1)}, bf16[912,128]{1,0:T(8,128)(2,1)S(1)}, u32[]{:S(2)}, u32[]{:S(2)}) %collective-permute-start.1) | collective-permute-done | bytes 233504 | tf_op jit(solution)/shard_map/ppermute | solution.py:526
  30.0 0.0 copy-start.2
  30.0 0.6 copy-done.2
  30.6 1.8 pack.1
  32.4 13.5 %all_to_all.40.own_w_ref = bf16[8,368,128]{2,1,0:T(8,128)(2,1)S(1)} all-to-all(bf16[8,368,128]{2,1,0:T(8,128)(2,1)S(1)} %get-tuple-element.41), channel_id=1, replica_groups=mesh['g'=4,'x'=4,'h'=2,'v'=2,'w'=2,'s'=2] {'x','w'}, dimensions={0} | all-to-all | bytes 1507328 | tf_op jit(solution)/shard_map/all_to_all | solution.py:484
  45.9 0.0 collective-permute-start.2
  45.9 2.2 %collective-permute-done.2.other_w_ref = bf16[8,368,128]{2,1,0:T(8,128)(2,1)S(1)} collective-permute-done((bf16[8,368,128]{2,1,0:T(8,128)(2,1)S(1)}, bf16[8,368,128]{2,1,0:T(8,128)(2,1)S(1)}, u32[]{:S(2)}, u32[]{:S(2)}) %collective-permute-start.2) | collective-permute-done | bytes 753696 | tf_op jit(solution)/shard_map/ppermute | solution.py:541
  48.1 3.6 %all-to-all-start.1 = ((bf16[8,576,128]{2,1,0:T(8,128)(2,1)}), bf16[8,576,128]{2,1,0:T(8,128)(2,1)S(1)}, u32[]{:S(2)}, u32[]{:S(2)}) async-start(bf16[8,576,128]{2,1,0:T(8,128)(2,1)} %get-tuple-element.42), calls=%async_computation.1 | async-start | bytes 2359296 | tf_op jit(solution)/shard_map/all_to_all | solution.py:484
  51.7 0.0 copy-done
  51.8 0.4 maximum_bitcast_fusion
  52.2 0.1 copy.24
  52.4 0.1 reshape.44
  52.5 0.0 copy-start.3
  52.5 1.4 convert_element_type.43
  53.9 1.1 pad_convert_fusion.mods_ref.t_mods_ref.f_mods_ref.refs_0_.refs_1_
  55.0 0.0 copy-done.3
  55.0 0.0 copy-start.1
  55.1 1.1 copy-done.1
  56.2 8.1 %generator.1 = (bf16[16,32,128]{2,1,0:T(8,128)(2,1)}, bf16[3,256,3072]{2,1,0:T(8,128)(2,1)}, f32[3,256,192]{2,1,0:T(8,128)}, f32[3,256,192]{2,1,0:T(8,128)}) custom-call(s32[5]{0:T(128)S(1)} %copy-done.3, bf16[912,128]{1,0:T(8,128)(2,1)S(1)} %collective-permute-done.mine_ref.own_ref.noise_ref, bf16[912,128]{1,0:T(8,128)(2,1)S(1)} %collective-permute-done.1.other_ref, ...), custom_call_target="tpu_custom_call" | custom-call | flops 12000000000 | bytes 30000000 | tf_op jit(solution)/shard_map/generator/pallas_call | solution.py:557
  64.3 6.1 %all-to-all-done.1.own_w_ref = bf16[8,576,128]{2,1,0:T(8,128)(2,1)S(1)} async-done(((bf16[8,576,128]{2,1,0:T(8,128)(2,1)}), bf16[8,576,128]{2,1,0:T(8,128)(2,1)S(1)}, u32[]{:S(2)}, u32[]{:S(2)}) %all-to-all-start.1) | async-done | bytes 1179680 | tf_op jit(solution)/shard_map/all_to_all | solution.py:484
  70.5 8.6 %all-to-all-start.2 = ((bf16[16,32,128]{2,1,0:T(8,128)(2,1)}), bf16[16,32,128]{2,1,0:T(8,128)(2,1)S(1)}, u32[]{:S(2)}, u32[]{:S(2)}) async-start(bf16[16,32,128]{2,1,0:T(8,128)(2,1)} %get-tuple-element.47), calls=%async_computation.2 | async-start | bytes 262144 | tf_op jit(solution)/shard_map/all_to_all | solution.py:484
  79.1 0.1 fusion.2
  79.2 8.8 %all-to-all-done.2.got_ref = bf16[16,32,128]{2,1,0:T(8,128)(2,1)S(1)} async-done(((bf16[16,32,128]{2,1,0:T(8,128)(2,1)}), bf16[16,32,128]{2,1,0:T(8,128)(2,1)S(1)}, u32[]{:S(2)}, u32[]{:S(2)}) %all-to-all-start.2) | async-done | bytes 131104 | tf_op jit(solution)/shard_map/all_to_all | solution.py:484
  88.0 1.6 samples.1
  89.6 2.7 %collective-permute-start.3 = (bf16[8,576,128]{2,1,0:T(8,128)(2,1)S(1)}, bf16[8,576,128]{2,1,0:T(8,128)(2,1)S(1)}, u32[]{:S(2)}, u32[]{:S(2)}) collective-permute-start(bf16[8,576,128]{2,1,0:T(8,128)(2,1)S(1)} %all-to-all-done.1.own_w_ref), channel_id=1, source_target_pairs={{0,1},{1,0},{2,3},{3,2},{4,5},{5,4},{6,7},{7,6},{8,9},{9,8},{10,11... | collective-permute-start | bytes 3538952 | tf_op jit(solution)/shard_map/ppermute | solution.py:593
  92.3 12.0 %all_to_all.41.got_ref = f32[16,24,128]{2,1,0:T(8,128)S(1)} all-to-all(f32[16,24,128]{2,1,0:T(8,128)S(1)} %get-tuple-element.49), channel_id=1, replica_groups=mesh['g'=4,'x'=4,'h'=2,'v'=2,'w'=2,'s'=2] {'v','h','g'}, dimensions={0} | all-to-all | bytes 393216 | tf_op jit(solution)/shard_map/all_to_all | solution.py:484
  104.3 0.0 collective-permute-done.3.other_w_ref
  104.3 13.7 %score.1 = (bf16[16,64,128]{2,1,0:T(8,128)(2,1)S(1)}, f32[3,64,128]{2,1,0:T(8,128)S(1)}, bf16[3,256,3072]{2,1,0:T(8,128)(2,1)}, f32[3,256,192]{2,1,0:T(8,128)}, f32[3,256,192]{2,1,0:T(8,128)}) custom-call(s32[5]{0:T(128)S(1)} %copy-done.3, f32[3]{0:T(128)S(1)} %get-tuple-element.80.time_ref, f32[16,24,128]{2,1,0:T(8,128)S(1)} %all_to_all.41.got_ref, ...), custom_call_target="tpu_custom_call" | custom-call | flops 24000000000 | bytes 50000000 | tf_op jit(solution)/shard_map/score/pallas_call | solution.py:595
  118.0 14.6 %all_to_all.42.got_ref = bf16[16,64,128]{2,1,0:T(8,128)(2,1)S(1)} all-to-all(bf16[16,64,128]{2,1,0:T(8,128)(2,1)S(1)} %get-tuple-element.52), channel_id=1, replica_groups=mesh['g'=4,'x'=4,'h'=2,'v'=2,'w'=2,'s'=2] {'v','h','g'}, dimensions={0} | all-to-all | bytes 524288 | tf_op jit(solution)/shard_map/all_to_all | solution.py:484
  132.7 2.4 %cotangents.1 = bf16[16,64,128]{2,1,0:T(8,128)(2,1)S(1)} custom-call(s32[5]{0:T(128)S(1)} %copy-done.3, f32[3]{0:T(128)S(1)} %get-tuple-element.79.time_ref.gen_time_ref, f32[3]{0:T(128)S(1)} %get-tuple-element.80.time_ref, bf16[16,64,128]{2,1,0:T(8,128)(2,1)S(1)} %all_to_all.42.got_ref, ...), custom_call_target="tpu_custom_call" | custom-call | tf_op jit(solution)/shard_map/cotangents/pallas_call | solution.py:624
  135.1 15.4 %all_to_all.43.got_ref = bf16[16,64,128]{2,1,0:T(8,128)(2,1)S(1)} all-to-all(bf16[16,64,128]{2,1,0:T(8,128)(2,1)S(1)} %cotangents.1), channel_id=1, replica_groups=mesh['g'=4,'x'=4,'h'=2,'v'=2,'w'=2,'s'=2] {'v','h','g'}, dimensions={0} | all-to-all | bytes 524288 | tf_op jit(solution)/shard_map/all_to_all | solution.py:484
  150.5 0.2 convert_reduce_fusion
  150.7 0.1 reduce_sum.14
  150.8 0.1 reduce_sum.18
  150.9 0.7 broadcast_in_dim.2
  151.6 6.4 %all-to-all-start.6 = ((f32[16,8,128]{2,1,0:T(8,128)}), f32[16,8,128]{2,1,0:T(8,128)S(1)}, u32[]{:S(2)}, u32[]{:S(2)}) async-start(f32[16,8,128]{2,1,0:T(8,128)} %broadcast_in_dim.2), calls=%async_computation.6 | async-start | bytes 131072 | tf_op jit(solution)/shard_map/all_to_all | solution.py:484
  158.0 6.0 %gradient.2 = (bf16[8,288,128]{2,1,0:T(8,128)(2,1)S(1)}, bf16[8,288,128]{2,1,0:T(8,128)(2,1)S(1)}) custom-call(s32[5]{0:T(128)S(1)} %copy-done.3, bf16[16,64,128]{2,1,0:T(8,128)(2,1)S(1)} %all_to_all.43.got_ref, f32[9,8,3072]{2,1,0:T(8,128)S(1)} %pad_convert_fusion.mods_ref.t_mods_ref.f_mods_ref.refs_0_.refs_1_, bf16[64,3072]{1,0:T(8,128)(2,1)} %bitcast.29, ...), custom_call_target="tpu_custom_call" | custom-call | flops 7000000000 | bytes 20000000 | tf_op jit(solution)/shard_map/gradient/pallas_call | solution.py:649
  164.1 0.3 collective-permute-start.5
  164.4 0.0 all-to-all-done.6.refs_0_
  164.4 6.1 %gradient.3 = (bf16[8,288,128]{2,1,0:T(8,128)(2,1)S(1)}, bf16[8,288,128]{2,1,0:T(8,128)(2,1)S(1)}) custom-call(s32[5]{0:T(128)S(1)} %copy-done.3, bf16[16,64,128]{2,1,0:T(8,128)(2,1)S(1)} %all_to_all.43.got_ref, f32[16,8,128]{2,1,0:T(8,128)S(1)} %all-to-all-done.6.refs_0_, f32[9,8,3072]{2,1,0:T(8,128)S(1)} %pad_convert_fusion.mods_ref.t_mods_ref.f_mods_ref.refs_0_.refs_1_, ...), custom_call_target="tpu_custom_call" | custom-call | flops 7000000000 | bytes 20000000 | tf_op jit(solution)/shard_map/gradient/pallas_call | solution.py:649
  170.5 0.4 collective-permute-start.6
  170.9 4.3 %collective-permute-start.4 = (f32[3,64,128]{2,1,0:T(8,128)S(1)}, f32[3,64,128]{2,1,0:T(8,128)S(1)}, u32[]{:S(2)}, u32[]{:S(2)}) collective-permute-start(f32[3,64,128]{2,1,0:T(8,128)S(1)} %get-tuple-element.55), channel_id=1, source_target_pairs={{0,0},{1,8},{4,4},{5,12},{8,1},{9,9},{12,5},{13,13},{2,2},{3,10},{... | collective-permute-start | bytes 294920 | tf_op jit(solution)/shard_map/ppermute | solution.py:638
  175.2 0.0 collective-permute-done.5
  175.2 0.2 add_convert_fusion.1
  175.4 0.0 collective-permute-done.6
  175.4 0.2 add_convert_fusion
  175.6 0.1 pad_maximum_fusion
  175.7 5.2 %collective-permute-done.4 = f32[3,64,128]{2,1,0:T(8,128)S(1)} collective-permute-done((f32[3,64,128]{2,1,0:T(8,128)S(1)}, f32[3,64,128]{2,1,0:T(8,128)S(1)}, u32[]{:S(2)}, u32[]{:S(2)}) %collective-permute-start.4) | collective-permute-done | bytes 98336 | tf_op jit(solution)/shard_map/ppermute | solution.py:638
  180.8 16.1 %all_to_all.44.got_ref = bf16[8,576,128]{2,1,0:T(8,128)(2,1)S(1)} all-to-all(bf16[8,576,128]{2,1,0:T(8,128)(2,1)S(1)} %pad_maximum_fusion), channel_id=1, replica_groups=mesh['g'=4,'x'=4,'h'=2,'v'=2,'w'=2,'s'=2] {'x','w'}, dimensions={0} | all-to-all | bytes 2359296 | tf_op jit(solution)/shard_map/all_to_all | solution.py:484
  196.9 0.7 sum.1
  197.7 5.6 %collective-permute-start.7 = (f32[2,144,128]{2,1,0:T(8,128)S(1)}, f32[2,144,128]{2,1,0:T(8,128)S(1)}, u32[]{:S(2)}, u32[]{:S(2)}) collective-permute-start(f32[2,144,128]{2,1,0:T(8,128)S(1)} %get-tuple-element.69), channel_id=1, source_target_pairs={{0,0},{1,8},{4,4},{5,12},{8,1},{9,9},{12,5},{13,13},{2,2},{3,10},{... | collective-permute-start | bytes 442376 | tf_op jit(solution)/shard_map/ppermute | solution.py:682
  203.3 2.6 %collective-permute-start.8 = (f32[2,144,128]{2,1,0:T(8,128)S(1)}, f32[2,144,128]{2,1,0:T(8,128)S(1)}, u32[]{:S(2)}, u32[]{:S(2)}) collective-permute-start(f32[2,144,128]{2,1,0:T(8,128)S(1)} %get-tuple-element.70), channel_id=1, source_target_pairs={{0,4},{1,12},{4,0},{5,8},{8,5},{9,13},{12,1},{13,9},{2,6},{3,14},{... | collective-permute-start | bytes 442376 | tf_op jit(solution)/shard_map/ppermute | solution.py:683
  205.8 2.3 %collective-permute-done.7.keep_ref = f32[2,144,128]{2,1,0:T(8,128)S(1)} collective-permute-done((f32[2,144,128]{2,1,0:T(8,128)S(1)}, f32[2,144,128]{2,1,0:T(8,128)S(1)}, u32[]{:S(2)}, u32[]{:S(2)}) %collective-permute-start.7) | collective-permute-done | bytes 147488 | tf_op jit(solution)/shard_map/ppermute | solution.py:682
  208.1 7.1 %collective-permute-done.8.other_ref = f32[2,144,128]{2,1,0:T(8,128)S(1)} collective-permute-done((f32[2,144,128]{2,1,0:T(8,128)S(1)}, f32[2,144,128]{2,1,0:T(8,128)S(1)}, u32[]{:S(2)}, u32[]{:S(2)}) %collective-permute-start.8) | collective-permute-done | bytes 147488 | tf_op jit(solution)/shard_map/ppermute | solution.py:683
  215.2 1.3 place.1
  216.6 0.6 copy.26
  (7 shorter events, 0.1 us)
Async XLA Ops:
  5.1 14.2 %collective-permute-start = (bf16[912,128]{1,0:T(8,128)(2,1)}, bf16[912,128]{1,0:T(8,128)(2,1)S(1)}, u32[]{:S(2)}, u32[]{:S(2)}) collective-permute-start(bf16[912,128]{1,0:T(8,128)(2,1)} %get-tuple-element.38), channel_id=1, source_target_pairs={{0,0},{1,8},{4,4},{5,12},{8,1},{9,9},{12,5},{13,13},{2,2},{3,10},{... | collective-permute-start | bytes 700424 | tf_op jit(solution)/shard_map/ppermute | solution.py:525
  15.3 14.6 %collective-permute-start.1 = (bf16[912,128]{1,0:T(8,128)(2,1)}, bf16[912,128]{1,0:T(8,128)(2,1)S(1)}, u32[]{:S(2)}, u32[]{:S(2)}) collective-permute-start(bf16[912,128]{1,0:T(8,128)(2,1)} %get-tuple-element.39), channel_id=1, source_target_pairs={{0,4},{1,12},{4,0},{5,8},{8,5},{9,13},{12,1},{13,9},{2,6},{3,14},{... | collective-permute-start | bytes 700424 | tf_op jit(solution)/shard_map/ppermute | solution.py:526
  30.0 0.6 copy-start.2
  45.9 2.2 %collective-permute-start.2 = (bf16[8,368,128]{2,1,0:T(8,128)(2,1)S(1)}, bf16[8,368,128]{2,1,0:T(8,128)(2,1)S(1)}, u32[]{:S(2)}, u32[]{:S(2)}) collective-permute-start(bf16[8,368,128]{2,1,0:T(8,128)(2,1)S(1)} %all_to_all.40.own_w_ref), channel_id=1, source_target_pairs={{0,1},{1,0},{2,3},{3,2},{4,5},{5,4},{6,7},{7,6},{8,9},{9,8},{10,11... | collective-permute-start | bytes 2261000 | tf_op jit(solution)/shard_map/ppermute | solution.py:541
  48.1 3.6 %copy-start = (bf16[8,368,128]{2,1,0:T(8,128)(2,1)}, bf16[8,368,128]{2,1,0:T(8,128)(2,1)S(1)}, u32[]{:S(2)}) copy-start(bf16[8,368,128]{2,1,0:T(8,128)(2,1)S(1)} %collective-permute-done.2.other_w_ref) | copy-start | bytes 2260996
  48.1 22.3 %all-to-all-start.1 = ((bf16[8,576,128]{2,1,0:T(8,128)(2,1)}), bf16[8,576,128]{2,1,0:T(8,128)(2,1)S(1)}, u32[]{:S(2)}, u32[]{:S(2)}) async-start(bf16[8,576,128]{2,1,0:T(8,128)(2,1)} %get-tuple-element.42), calls=%async_computation.1 | async-start | bytes 2359296 | tf_op jit(solution)/shard_map/all_to_all | solution.py:484
  52.5 2.5 %copy-start.3 = (s32[5]{0:T(128)S(1)}, s32[5]{0:T(128)}, u32[]{:S(2)}) copy-start(s32[5]{0:T(128)} %stack.32.place_ref) | copy-start | bytes 64
  55.0 1.1 copy-start.1
  70.5 17.5 %all-to-all-start.2 = ((bf16[16,32,128]{2,1,0:T(8,128)(2,1)}), bf16[16,32,128]{2,1,0:T(8,128)(2,1)S(1)}, u32[]{:S(2)}, u32[]{:S(2)}) async-start(bf16[16,32,128]{2,1,0:T(8,128)(2,1)} %get-tuple-element.47), calls=%async_computation.2 | async-start | bytes 262144 | tf_op jit(solution)/shard_map/all_to_all | solution.py:484
  89.6 14.7 %collective-permute-start.3 = (bf16[8,576,128]{2,1,0:T(8,128)(2,1)S(1)}, bf16[8,576,128]{2,1,0:T(8,128)(2,1)S(1)}, u32[]{:S(2)}, u32[]{:S(2)}) collective-permute-start(bf16[8,576,128]{2,1,0:T(8,128)(2,1)S(1)} %all-to-all-done.1.own_w_ref), channel_id=1, source_target_pairs={{0,1},{1,0},{2,3},{3,2},{4,5},{5,4},{6,7},{7,6},{8,9},{9,8},{10,11... | collective-permute-start | bytes 3538952 | tf_op jit(solution)/shard_map/ppermute | solution.py:593
  151.6 12.8 %all-to-all-start.6 = ((f32[16,8,128]{2,1,0:T(8,128)}), f32[16,8,128]{2,1,0:T(8,128)S(1)}, u32[]{:S(2)}, u32[]{:S(2)}) async-start(f32[16,8,128]{2,1,0:T(8,128)} %broadcast_in_dim.2), calls=%async_computation.6 | async-start | bytes 131072 | tf_op jit(solution)/shard_map/all_to_all | solution.py:484
  164.1 11.1 %collective-permute-start.5 = (bf16[8,288,128]{2,1,0:T(8,128)(2,1)S(1)}, bf16[8,288,128]{2,1,0:T(8,128)(2,1)S(1)}, u32[]{:S(2)}, u32[]{:S(2)}) collective-permute-start(bf16[8,288,128]{2,1,0:T(8,128)(2,1)S(1)} %get-tuple-element.61), channel_id=1, source_target_pairs={{0,1},{1,0},{2,3},{3,2},{4,5},{5,4},{6,7},{7,6},{8,9},{9,8},{10,11... | collective-permute-start | bytes 1769480 | tf_op jit(solution)/shard_map/ppermute | solution.py:663
  170.5 4.9 %collective-permute-start.6 = (bf16[8,288,128]{2,1,0:T(8,128)(2,1)S(1)}, bf16[8,288,128]{2,1,0:T(8,128)(2,1)S(1)}, u32[]{:S(2)}, u32[]{:S(2)}) collective-permute-start(bf16[8,288,128]{2,1,0:T(8,128)(2,1)S(1)} %get-tuple-element.66), channel_id=1, source_target_pairs={{0,1},{1,0},{2,3},{3,2},{4,5},{5,4},{6,7},{7,6},{8,9},{9,8},{10,11... | collective-permute-start | bytes 1769480 | tf_op jit(solution)/shard_map/ppermute | solution.py:663
  170.9 9.9 %collective-permute-start.4 = (f32[3,64,128]{2,1,0:T(8,128)S(1)}, f32[3,64,128]{2,1,0:T(8,128)S(1)}, u32[]{:S(2)}, u32[]{:S(2)}) collective-permute-start(f32[3,64,128]{2,1,0:T(8,128)S(1)} %get-tuple-element.55), channel_id=1, source_target_pairs={{0,0},{1,8},{4,4},{5,12},{8,1},{9,9},{12,5},{13,13},{2,2},{3,10},{... | collective-permute-start | bytes 294920 | tf_op jit(solution)/shard_map/ppermute | solution.py:638
  197.7 10.5 %collective-permute-start.7 = (f32[2,144,128]{2,1,0:T(8,128)S(1)}, f32[2,144,128]{2,1,0:T(8,128)S(1)}, u32[]{:S(2)}, u32[]{:S(2)}) collective-permute-start(f32[2,144,128]{2,1,0:T(8,128)S(1)} %get-tuple-element.69), channel_id=1, source_target_pairs={{0,0},{1,8},{4,4},{5,12},{8,1},{9,9},{12,5},{13,13},{2,2},{3,10},{... | collective-permute-start | bytes 442376 | tf_op jit(solution)/shard_map/ppermute | solution.py:682
  203.3 12.0 %collective-permute-start.8 = (f32[2,144,128]{2,1,0:T(8,128)S(1)}, f32[2,144,128]{2,1,0:T(8,128)S(1)}, u32[]{:S(2)}, u32[]{:S(2)}) collective-permute-start(f32[2,144,128]{2,1,0:T(8,128)S(1)} %get-tuple-element.70), channel_id=1, source_target_pairs={{0,4},{1,12},{4,0},{5,8},{8,5},{9,13},{12,1},{13,9},{2,6},{3,14},{... | collective-permute-start | bytes 442376 | tf_op jit(solution)/shard_map/ppermute | solution.py:683

commit v5 on v4

--- a/solution.py
+++ b/solution.py
@@ -22,7 +22,7 @@
 BF16 = jnp.bfloat16
 
 GATHER = ("x", "w")
-ROW_AXES = ("x", "h", "v", "w")
+ROW_AXES = ("x", "h", "w", "v")
 COMBINE = ("v", "h", "g")
 TOKEN_AXES = ("x", "w", "s")
 OWNERS = 16
@@ -35,17 +35,28 @@
 COLS = WIDE + NARROW
 GEN_ROWS = 288
 NOISE_ROWS = 384
-MODS_AT = 864
+MODS_AT = 480
 MODS_ROWS = 36
-SENT_ROWS = 912
+SENT_ROWS = 528
 GEN_CHUNK = 368
 SCORE_ROWS = 576
 CHUNKS = 8
 BLOCK = 512
 
-PLACES = ("h", "v", "s")
-SWAP = [(h * 4 + v * 2 + s, s * 4 + v * 2 + h) for h in range(2) for v in range(2) for s in range(2)]
-SWAP_TURNED = [(h * 4 + v * 2 + s, s * 4 + (1 - v) * 2 + h) for h in range(2) for v in range(2) for s in range(2)]
+PLACES = ("g", "h", "v", "s")
+
+
+def number(g, h, v, s):
+    return g * 8 + h * 4 + v * 2 + s
+
+
+EVERY = [(g, h, v, s) for g in range(4) for h in range(2) for v in range(2) for s in range(2)]
+SWAP, SWAP_TURNED = [
+    [(number(g, h, v, s), number((g + 2) % 4, s, v ^ turn, h)) for g, h, v, s in EVERY] for turn in range(2)
+]
+NEAR, NEAR_TURNED = [
+    [(number(g, h, v, s), number(g if h == s else 3 - g, s, v ^ turn, h)) for g, h, v, s in EVERY] for turn in range(2)
+]
 SIBLING = [(0, 1), (1, 0)]
 
 
@@ -124,7 +135,7 @@
         for chunk in range(CHUNKS):
             x, w = chunk // 2, chunk % 2
             for v in range(2):
-                k = pl.multiple_of((x * 8 + v * 2 + w) * ROWS + side * (4 * ROWS), 32)
+                k = pl.multiple_of((x * 8 + w * 2 + v) * ROWS + side * (4 * ROWS), 32)
                 first = max(net - 1, 0) * 192 + v * ROWS
                 w_ref[pl.ds(k, ROWS), :WIDE] = packed_ref[chunk, first : first + ROWS, :]
                 if net == 0:
@@ -186,23 +197,30 @@
     return value.reshape(OWNERS, OWNED, value.shape[-1])
 
 
-def final_sums(mods_ref, final_ref):
-    scales = [mods_ref[i, 4:5, :] for i in range(IMAGES)]
-    shifts = [mods_ref[i, 3:4, :] for i in range(IMAGES)]
+def sums_kernel(g_final_ref, t_final_ref, f_final_ref, mods_ref, out_ref):
     run = lax.broadcasted_iota(jnp.int32, (OWNERS, D), 1) // COLS
     own = run == lax.broadcasted_iota(jnp.int32, (OWNERS, D), 0)
-    left = [jnp.where(own, row, 0.0) for row in scales + [jnp.ones((1, D), F32)]]
-    sums = dot_turned(jnp.concatenate(left + shifts + [jnp.zeros((5, D), F32)], axis=0).astype(BF16), final_ref[...])
-    ones = sums[3 * OWNERS : 4 * OWNERS]
-    runs = [sums[i * OWNERS : (i + 1) * OWNERS] + ones for i in range(IMAGES)]
-    return runs, [jnp.sum(r, axis=0, keepdims=True) for r in runs], [sums[64 + i : 65 + i] for i in range(IMAGES)]
+    for net, final_ref in enumerate((g_final_ref, t_final_ref, f_final_ref)):
+        scales = [mods_ref[3 * net + i, 4:5, :] for i in range(IMAGES)]
+        shifts = [mods_ref[3 * net + i, 3:4, :] for i in range(IMAGES)]
+        left = [jnp.where(own, row, 0.0) for row in scales + [jnp.ones((1, D), F32)]]
+        left = jnp.concatenate(left + shifts + [jnp.zeros((5, D), F32)], axis=0).astype(BF16)
+        sums = dot_turned(left, final_ref[...])
+        ones = sums[3 * OWNERS : 4 * OWNERS]
+        runs = [sums[i * OWNERS : (i + 1) * OWNERS] + ones for i in range(IMAGES)]
+        totals = [jnp.sum(r, axis=0, keepdims=True) for r in runs]
+        out_ref[net] = jnp.concatenate(runs + totals + [sums[64:67], jnp.zeros((2, C), F32)], axis=0)
+
+
+def read_sums(sums_ref, net):
+    runs = [sums_ref[net, i * OWNERS : (i + 1) * OWNERS] for i in range(IMAGES)]
+    return runs, [sums_ref[net, 48 + i : 49 + i] for i in range(IMAGES)], [sums_ref[net, 51 + i : 52 + i] for i in range(IMAGES)]
 
 
 def add_up(partials, totals, squares, runs):
     means = totals * (1.0 / COLS)
-    ordered = jnp.concatenate(
-        [runs[(g * 2 + h) * 2 + v][None, None] for v in range(2) for h in range(2) for g in range(4)], axis=0
-    )
+    ordered = [((g + 2) % 4 * 2 + h) * 2 + v for v in range(2) for h in range(2) for g in range(4)]
+    ordered = jnp.concatenate([runs[run : run + 1][None] for run in ordered], axis=0)
     partial = jnp.sum(partials + means * ordered, axis=0)
     average = jnp.sum(totals, axis=0) / D
     inverse = lax.rsqrt(jnp.sum(squares, axis=0) / D - average * average + norm_epsilon)
@@ -210,11 +228,10 @@
 
 
 def split_kernel(place_ref, cond_ref, gen_noise_ref, score_noise_ref, gen_ref, teacher_ref, fake_ref,
-                 gen_mod_ref, teacher_mod_ref, fake_mod_ref, mine_ref, other_ref):
+                 gen_mod_ref, teacher_mod_ref, fake_mod_ref, mine_ref, other_ref, noise_ref):
     for i in range(IMAGES):
         noise = jnp.concatenate([gen_noise_ref[i], score_noise_ref[i]], axis=0).astype(F32).T.astype(BF16)
-        mine_ref[i * HALF : (i + 1) * HALF] = noise
-        other_ref[i * HALF : (i + 1) * HALF] = noise
+        noise_ref[i * HALF : (i + 1) * HALF] = noise
     cond = cond_ref[...]
     mods = [dot_turned(cond, ref[...]) for ref in (gen_mod_ref, teacher_mod_ref, fake_mod_ref)]
     mods = jnp.concatenate([mods[0][0:3], mods[1][3:6], mods[2][3:6]], axis=0)
@@ -225,7 +242,7 @@
     first = place_ref[0] == 0
     mine, other = [], []
     for n, ref in enumerate((gen_ref, teacher_ref, fake_ref)):
-        rows = slice(NOISE_ROWS + n * ROWS, NOISE_ROWS + (n + 1) * ROWS)
+        rows = slice(n * ROWS, (n + 1) * ROWS)
         low, high = ref[:, :128], ref[:, 256:]
         mine_ref[rows] = jnp.where(first, low, high)
         other_ref[rows] = jnp.where(first, high, low)
@@ -233,8 +250,8 @@
         mine.append(jnp.where(first, low, high))
         other.append(jnp.where(first, high, low))
     for ref, parts in ((mine_ref, mine), (other_ref, other)):
-        ref[NOISE_ROWS + 3 * ROWS : NOISE_ROWS + 4 * ROWS] = jnp.concatenate(parts[1:], axis=1)
-        ref[NOISE_ROWS + 4 * ROWS : MODS_AT] = jnp.concatenate([parts[0], parts[0]], axis=1)
+        ref[3 * ROWS : 4 * ROWS] = jnp.concatenate(parts[1:], axis=1)
+        ref[4 * ROWS : MODS_AT] = jnp.concatenate([parts[0], parts[0]], axis=1)
 
 
 def in_order(v, mine, other):
@@ -243,7 +260,7 @@
 
 def pack_kernel(place_ref, mine_ref, other_ref, gen_ref, score_ref):
     v = place_ref[0]
-    cuts = [slice(NOISE_ROWS + n * ROWS, NOISE_ROWS + (n + 1) * ROWS) for n in range(5)]
+    cuts = [slice(n * ROWS, (n + 1) * ROWS) for n in range(5)]
     ordered = [in_order(v, mine_ref[rows], other_ref[rows]) for rows in cuts]
     parts = jnp.concatenate([ordered[4][0][:, :NARROW], ordered[4][1][:, :NARROW]], axis=1)
     mods = in_order(v, mine_ref[MODS_AT:].astype(F32), other_ref[MODS_AT:].astype(F32))
@@ -283,9 +300,8 @@
         part_ref[...] = sum_ref[...].astype(BF16)
 
 
-def samples_kernel(place_ref, time_ref, got_ref, noise_ref, mods_ref, final_ref,
-                   out_ref, keep_ref, sums_ref):
-    runs, scales, shifts = final_sums(mods_ref, final_ref)
+def samples_kernel(place_ref, time_ref, got_ref, noise_ref, sums_ref, out_ref, keep_ref):
+    runs, scales, shifts = read_sums(sums_ref, 0)
     got = got_ref[...].astype(F32)
     packed = []
     for i in range(IMAGES):
@@ -305,7 +321,6 @@
         keep_ref[1, at, :] = inner
         keep_ref[2, at, :] = jnp.broadcast_to(average, (OWNED, C))
         keep_ref[3, at, :] = jnp.broadcast_to(inverse, (OWNED, C))
-    sums_ref[...] = jnp.concatenate(scales + [jnp.zeros((5, C), F32)], axis=0)
     out_ref[...] = jnp.broadcast_to(jnp.concatenate(packed, axis=0)[None], out_ref.shape)
 
 
@@ -352,11 +367,10 @@
         part_ref[...] = sum_ref[...].astype(BF16)
 
 
-def cotangent_kernel(place_ref, gen_time_ref, time_ref, got_ref, noise_ref, keep_ref, sums_ref,
-                     t_mods_ref, f_mods_ref, t_final_ref, f_final_ref, out_ref):
+def cotangent_kernel(place_ref, gen_time_ref, time_ref, got_ref, noise_ref, keep_ref, sums_ref, out_ref):
     loss_scale = 1.0 / math.sqrt(IMAGES * S)
-    t_runs, t_scales, t_shifts = final_sums(t_mods_ref, t_final_ref)
-    f_runs, f_scales, f_shifts = final_sums(f_mods_ref, f_final_ref)
+    t_runs, t_scales, t_shifts = read_sums(sums_ref, 1)
+    f_runs, f_scales, f_shifts = read_sums(sums_ref, 2)
     got = got_ref[...].astype(F32)
     lane = lax.broadcasted_iota(jnp.int32, (1, 128), 1)
     cots, rows = [], []
@@ -385,7 +399,7 @@
         numbers = []
         for cot, column, value, average, inverse in (
             (fake_cot, f_scales[i], f_inner, f_average, f_inverse),
-            (gen_cot, sums_ref[i : i + 1, :], g_inner, g_average, g_inverse),
+            (gen_cot, sums_ref[0, 48 + i : 49 + i], g_inner, g_average, g_inverse),
         ):
             first = jnp.sum(cot * column, axis=1, keepdims=True) / D
             second = jnp.sum(cot * value, axis=1, keepdims=True) / D
@@ -442,7 +456,7 @@
     for w in range(2):
         sides = []
         for h in range(2):
-            at = [(v * 2 + w) * ROWS for v in range(2)]
+            at = [(w * 2 + v) * ROWS for v in range(2)]
             lanes = slice(h * NARROW, (h + 1) * NARROW)
             narrow = jnp.concatenate([parts[k : k + ROWS, lanes] for k in at], axis=1)
             sides.append([tiles[h * 384 + k : h * 384 + k + ROWS] for k in at] + [narrow])
@@ -463,13 +477,13 @@
 
         low = folded(total[:ROWS], total[2 * ROWS :, :NARROW])
         high = folded(total[ROWS : 2 * ROWS], total[2 * ROWS :, NARROW:])
-        keep_ref[n] = jnp.where(v == 0, low, high)
-        send_ref[n] = jnp.where(v == 0, high, low)
+        keep_ref[n] = jnp.where(v == 0, low, high).astype(BF16)
+        send_ref[n] = jnp.where(v == 0, high, low).astype(BF16)
 
 
 def place_kernel(place_ref, keep_ref, other_ref, fake_ref, gen_ref):
     for n, ref in enumerate((fake_ref, gen_ref)):
-        low, high = in_order(place_ref[0], keep_ref[n], other_ref[n])
+        low, high = in_order(place_ref[0], keep_ref[n].astype(F32), other_ref[n].astype(F32))
         ref[:, :128] = low[:ROWS]
         ref[:48, 128:256] = jnp.concatenate([low[ROWS:, :NARROW], high[ROWS:, :NARROW]], axis=1)
         ref[48:, 128:256] = jnp.concatenate([low[ROWS:, NARROW:], high[ROWS:, NARROW:]], axis=1)
@@ -503,7 +517,7 @@
     fake_final,
 ):
     v, s = lax.axis_index("v"), lax.axis_index("s")
-    start = lax.axis_index(("g", "h")) * 384
+    start = (lax.rem(lax.axis_index("g") + 2, 4) * 2 + lax.axis_index("h")) * 384
     member = lax.axis_index(("h", "g"))
     place = jnp.stack([v, start + 256 * v, start + 128, member * OWNED, s]).astype(jnp.int32)
     gen_final, teacher_final, fake_final = gen_final.T, teacher_final.T, fake_final.T
@@ -511,19 +525,22 @@
     times, conds = time_features(jnp.concatenate([gen_steps, score_steps]), gen_modulation.shape[0])
     gen_time, score_time = times[:3], times[3:]
     halves = jax.ShapeDtypeStruct((SENT_ROWS, 128), BF16)
-    mine, other = pl.pallas_call(
+    mine, other, noise = pl.pallas_call(
         split_kernel,
         grid=(1,),
         in_specs=[smem(), whole((6, 256))] + [whole((IMAGES, C, HALF))] * 2 + [whole((ROWS, 384))] * 3
         + [whole((480, 256))] * 3,
-        out_specs=[whole((SENT_ROWS, 128))] * 2,
-        out_shape=[halves, halves],
+        out_specs=[whole((SENT_ROWS, 128))] * 2 + [whole((NOISE_ROWS, 128))],
+        out_shape=[halves, halves, jax.ShapeDtypeStruct((NOISE_ROWS, 128), BF16)],
         compiler_params=params(60),
         name="split",
     )(place, conds, gen_noise.transpose(0, 2, 1), score_noise.transpose(0, 2, 1), gen_proj, teacher_proj, fake_proj,
       gen_modulation.T, teacher_modulation.T, fake_modulation.T)
     mine = lax.ppermute(mine, PLACES, SWAP)
     other = lax.ppermute(other, PLACES, SWAP_TURNED)
+    mine, other, noise = lax.optimization_barrier((mine, other, noise))
+    own_noise = lax.ppermute(noise, PLACES, NEAR)
+    other_noise = lax.ppermute(noise, PLACES, NEAR_TURNED)
 
     g_packed, packed = pl.pallas_call(
         pack_kernel,
@@ -538,11 +555,12 @@
         name="pack",
     )(place, mine, other)
     g_packed = exchange(g_packed, GATHER)
+    g_packed, own_noise, other_noise = lax.optimization_barrier((g_packed, own_noise, other_noise))
     g_other = lax.ppermute(g_packed, "s", SIBLING)
     packed, g_packed, g_other = lax.optimization_barrier((packed, g_packed, g_other))
     packed = exchange(packed, GATHER)
     low, high = (a[:, GEN_ROWS : GEN_ROWS + 2 * MODS_ROWS] for a in in_order(s, g_packed, g_other))
-    mods = jnp.stack([low, high]).reshape(2, 4, 2, 2, 4, 9, 128).transpose(5, 1, 0, 3, 2, 4, 6)
+    mods = jnp.stack([low, high]).reshape(2, 4, 2, 2, 4, 9, 128).transpose(5, 1, 0, 2, 3, 4, 6)
     mods = mods.reshape(9, 32, 512)[:, :, :480].reshape(9, 5, D).astype(F32)
     mods = jnp.pad(mods, ((0, 0), (0, 3), (0, 0)))
 
@@ -554,6 +572,16 @@
     gen_embed, teacher_embed, fake_embed = in_hbm(gen_embed, teacher_embed, fake_embed)
     gen_final, teacher_final, fake_final = in_hbm(gen_final, teacher_final, fake_final)
 
+    sums = pl.pallas_call(
+        sums_kernel,
+        grid=(1,),
+        in_specs=[whole((C, D))] * 3 + [whole((9, 8, D))],
+        out_specs=whole((3, 56, C)),
+        out_shape=jax.ShapeDtypeStruct((3, 56, C), F32),
+        compiler_params=params(16),
+        name="sums",
+    )(gen_final, teacher_final, fake_final, mods)
+
     part, g_shaped, g_pre, g_res = pl.pallas_call(
         generator_kernel,
         grid=(IMAGES,),
@@ -568,26 +596,25 @@
         compiler_params=params(16),
         cost_estimate=pl.CostEstimate(flops=12 * 10**9, bytes_accessed=30 * 10**6, transcendentals=0),
         name="generator",
-    )(place, mine, other, gen_embed, mods, gen_final, g_packed, g_other)
-    packed, part = lax.optimization_barrier((packed, part))
+    )(place, own_noise, other_noise, gen_embed, mods, gen_final, g_packed, g_other)
+    packed, part, sums = lax.optimization_barrier((packed, part, sums))
     part = exchange(part, COMBINE)
 
     net_mods = lambda net: pl.BlockSpec((IMAGES, 8, D), lambda *_: (net, 0, 0))
-    pack1, keep, sums = pl.pallas_call(
+    pack1, keep = pl.pallas_call(
         samples_kernel,
         grid=(1,),
         in_specs=[
-            smem(), smem(), whole((OWNERS, 32, 128)), whole((NOISE_ROWS, 128)), net_mods(0), whole((C, D)),
-        ],
-        out_specs=[whole((OWNERS, 24, 128)), whole((4, 48, C)), whole((8, C))],
+            smem(), smem(), whole((OWNERS, 32, 128)), whole((NOISE_ROWS, 128)), whole((3, 56, C)),
+        ],
+        out_specs=[whole((OWNERS, 24, 128)), whole((4, 48, C))],
         out_shape=[
             jax.ShapeDtypeStruct((OWNERS, 24, 128), F32),
             jax.ShapeDtypeStruct((4, 48, C), F32),
-            jax.ShapeDtypeStruct((8, C), F32),
         ],
         compiler_params=params(5),
         name="samples",
-    )(place, gen_time, part, mine, mods, gen_final)
+    )(place, gen_time, part, own_noise, sums)
     packed, pack1 = lax.optimization_barrier((packed, pack1))
     pack1 = exchange(pack1, COMBINE)
     other_packed = lax.ppermute(packed, "s", SIBLING)
@@ -617,7 +644,7 @@
         compiler_params=params(22),
         cost_estimate=pl.CostEstimate(flops=24 * 10**9, bytes_accessed=50 * 10**6, transcendentals=0),
         name="score",
-    )(place, score_time, pack1, mine, other, teacher_embed, fake_embed, mods, mods,
+    )(place, score_time, pack1, own_noise, other_noise, teacher_embed, fake_embed, mods, mods,
       teacher_final, fake_final, packed, other_packed)
     part2 = exchange(part2, COMBINE)
 
@@ -626,20 +653,23 @@
         grid=(1,),
         in_specs=[
             smem(), smem(), smem(), whole((OWNERS, 64, 128)), whole((NOISE_ROWS, 128)), whole((4, 48, C)),
-            whole((8, C)), net_mods(1), net_mods(2), whole((C, D)), whole((C, D)),
+            whole((3, 56, C)),
         ],
         out_specs=whole((OWNERS, 64, 128)),
         out_shape=jax.ShapeDtypeStruct((OWNERS, 64, 128), BF16),
         compiler_params=params(6),
         name="cotangents",
-    )(place, gen_time, score_time, part2, mine, keep, sums, mods, mods, teacher_final, fake_final)
+    )(place, gen_time, score_time, part2, own_noise, keep, sums)
     pack2 = exchange(pack2, COMBINE)
     samples, pack2 = lax.optimization_barrier((samples, pack2))
-    samples = lax.ppermute(samples, PLACES, SWAP)
+    own_samples = samples
+    samples = lax.ppermute(samples, "s", SIBLING)
 
     gap = jnp.sum(pack2[:, 48:57, 96].astype(F32).reshape(OWNERS, 3, 3), axis=(0, 2))
     gap = jnp.broadcast_to(jnp.pad(gap, (0, 5))[None, :, None], (16, 8, 128))
     gap = exchange(gap, TOKEN_AXES)
+    samples, gap = lax.optimization_barrier((samples, gap))
+    samples = jnp.where(lax.axis_index("h") == s, own_samples, samples).transpose(0, 2, 1)
 
     by_columns = pl.BlockSpec((IMAGES, TOKENS, 768), lambda x: (0, 0, x))
     partial = jax.ShapeDtypeStruct((CHUNKS, GEN_ROWS, 128), BF16)
@@ -667,9 +697,7 @@
     both = jnp.concatenate(
         [(pieces[n].astype(F32) + pieces[n + 1].astype(F32)).astype(BF16) for n in (0, 2)], axis=1
     )
-    samples, both = lax.optimization_barrier((samples, both))
-    samples = samples.transpose(0, 2, 1)
-    tiles = jax.ShapeDtypeStruct((2, 144, 128), F32)
+    tiles = jax.ShapeDtypeStruct((2, 144, 128), BF16)
     kept, sent = pl.pallas_call(
         sum_kernel,
         grid=(1,),
@@ -694,7 +722,7 @@
 
 
 def solution(mesh):
-    split = Mesh(mesh.devices.reshape(4, 4, 2, 2, 2, 2), ("g", "x", "h", "v", "w", "s"))
+    split = Mesh(mesh.devices.reshape(4, 4, 2, 2, 2, 2), ("g", "x", "h", "w", "v", "s"))
     tokens = P(None, ROW_AXES, None)
     columns = P(None, ROW_AXES)
     block = P(ROW_AXES, ("g", "s"))

time: 218 us -> 200 us (0.917)
  blocking collectives: 71.6 us -> 37.4 us
  waiting for transfers between devices: 43.7 us -> 55.1 us
  starting transfers between devices: 47.4 us -> 51.1 us
    all_to_all x5 -> x3, blocking collectives: 71.6 us -> 37.4 us  [exchange(): return lax.all_to_all(value, axes, 0, 0)]
    all_to_all x3 -> x5, waiting for transfers between devices: 15 us -> 32.7 us  [exchange(): return lax.all_to_all(value, axes, 0, 0)]
    all_to_all x3 -> x5, starting transfers between devices: 18.6 us -> 30.3 us  [exchange(): return lax.all_to_all(value, axes, 0, 0)]
    ppermute x1, waiting for transfers between devices: 10.6 us -> 6.28 us  [shards(): other = lax.ppermute(other, PLACES, SWAP_TURNED)]
    ppermute x1, starting transfers between devices: 10.2 us -> 7.41 us  [shards(): mine = lax.ppermute(mine, PLACES, SWAP)]
    ppermute x1, waiting for transfers between devices: 7.13 us -> 4.48 us  [shards(): sent = lax.ppermute(sent, PLACES, SWAP_TURNED)]
    ppermute x1 -> x3, waiting for transfers between devices: 5.17 us -> 3.99 us  [the longest x1 3.57 us: shards(): other_noise = lax.ppermute(noise, PLACES, NEAR_TURNED)]
    ppermute x1 -> x3, starting transfers between devices: 4.31 us -> 4.69 us  [the longest x1 3.14 us: shards(): own_noise = lax.ppermute(noise, PLACES, NEAR)]
  transfers between devices with their start and end apart: 12 -> 16, of which waited for: 8 -> 13; matrix products, arithmetic and copies ran while one was open for 2% -> 2% of each run, Pallas kernels for 9% -> 11%
where the time goes in v5:
time: 200 us; the launch traced here: 199 us
  waiting for transfers between devices  55.1 us (28%)
  starting transfers between devices  51.1 us (26%)
  Pallas kernels  45.6 us (23%)
  blocking collectives  37.4 us (19%)
  other arithmetic  5.42 us (3%)
  local copies, waits for them, and re-layouts  3.74 us (2%)
    all_to_all x3, blocking collectives, exchange(): return lax.all_to_all(value, axes, 0, 0)  37.4 us
    all_to_all x5, waiting for transfers between devices, exchange(): return lax.all_to_all(value, axes, 0, 0)  32.7 us
    all_to_all x5, starting transfers between devices, exchange(): return lax.all_to_all(value, axes, 0, 0)  30.3 us
    pallas_call x1, Pallas kernels, shards(): pl.pallas_call(score_kernel, grid=(IMAGES,), in_specs=[smem(), smem(), wh...  13.7 us
    pallas_call x2, Pallas kernels, gradient(): pl.pallas_call(functools.partial(gradient_kernel, net), grid=(4,), in_spe...  12.2 us
    pallas_call x1, Pallas kernels, shards(): pl.pallas_call(generator_kernel, grid=(IMAGES,), in_specs=[smem(), noise_...  8.2 us
    ppermute x1, starting transfers between devices, shards(): mine = lax.ppermute(mine, PLACES, SWAP)  7.41 us
    ppermute x1, waiting for transfers between devices, shards(): other = lax.ppermute(other, PLACES, SWAP_TURNED)  6.28 us
  transfers between devices with their start and end apart: 16, of which 13 were waited for; matrix products, arithmetic and copies ran while one was open for 2% of the time, Pallas kernels for 11%

profile of v5, /device:TPU:1, one launch (start us, length us, event | category | flops | bytes accessed | tf_op | source)
XLA Modules:
  0.0 199.3 jit_solution(11783144380262091462)
XLA Ops:
  0.7 0.8 broadcast_multiply_fusion
  1.4 0.1 multiply_cosine_fusion
  1.5 0.6 multiply_convert_fusion.cond_ref
  2.1 0.6 stack.32.place_ref
  2.7 2.4 %split.1 = (bf16[528,128]{1,0:T(8,128)(2,1)}, bf16[528,128]{1,0:T(8,128)(2,1)}, bf16[384,128]{1,0:T(8,128)(2,1)}) custom-call(s32[5]{0:T(128)} %stack.32.place_ref, bf16[6,256]{1,0:T(8,128)(2,1)} %multiply_convert_fusion.cond_ref, bf16[3,64,128]{2,1,0:T(8,128)(2,1)} %bitcast.34, bf16[3,64,128]{2,1,0:T(8,128)(2,1)} %bitcast.35, bf16[96,384]{1,0:T(8,128)(2,1)} %gen_ref.1, ...), custom_call_target="tpu_custom_call" | custom-call | tf_op jit(solution)/shard_map/split/pallas_call | solution.py:528
  5.1 7.4 %collective-permute-start = (bf16[528,128]{1,0:T(8,128)(2,1)}, bf16[528,128]{1,0:T(8,128)(2,1)S(1)}, u32[]{:S(2)}, u32[]{:S(2)}) collective-permute-start(bf16[528,128]{1,0:T(8,128)(2,1)} %get-tuple-element.45), channel_id=1, source_target_pairs={{0,128},{1,136},{2,130},{3,138},{8,129},{9,137},{10,131},{11,139},... | collective-permute-start | bytes 405512 | tf_op jit(solution)/shard_map/ppermute | solution.py:539
  12.5 1.1 collective-permute-start.1
  13.6 2.5 %collective-permute-done.mine_ref = bf16[528,128]{1,0:T(8,128)(2,1)S(1)} collective-permute-done((bf16[528,128]{1,0:T(8,128)(2,1)}, bf16[528,128]{1,0:T(8,128)(2,1)S(1)}, u32[]{:S(2)}, u32[]{:S(2)}) %collective-permute-start) | collective-permute-done | bytes 135200 | tf_op jit(solution)/shard_map/ppermute | solution.py:539
  16.1 6.3 %collective-permute-done.1.other_ref = bf16[528,128]{1,0:T(8,128)(2,1)S(1)} collective-permute-done((bf16[528,128]{1,0:T(8,128)(2,1)}, bf16[528,128]{1,0:T(8,128)(2,1)S(1)}, u32[]{:S(2)}, u32[]{:S(2)}) %collective-permute-start.1) | collective-permute-done | bytes 135200 | tf_op jit(solution)/shard_map/ppermute | solution.py:540
  22.4 0.6 copy-done.2
  22.9 2.1 %pack.1 = (bf16[8,368,128]{2,1,0:T(8,128)(2,1)}, bf16[8,576,128]{2,1,0:T(8,128)(2,1)}) custom-call(s32[5]{0:T(128)S(1)} %copy-done.2, bf16[528,128]{1,0:T(8,128)(2,1)S(1)} %collective-permute-done.mine_ref, bf16[528,128]{1,0:T(8,128)(2,1)S(1)} %collective-permute-done.1.other_ref), custom_call_target="tpu_custom_call" | custom-call | tf_op jit(solution)/shard_map/pack/pallas_call | solution.py:545
  25.0 6.4 %all-to-all-start = ((bf16[8,368,128]{2,1,0:T(8,128)(2,1)}), bf16[8,368,128]{2,1,0:T(8,128)(2,1)S(1)}, u32[]{:S(2)}, u32[]{:S(2)}) async-start(bf16[8,368,128]{2,1,0:T(8,128)(2,1)} %get-tuple-element.51), calls=%async_computation | async-start | bytes 1507328 | tf_op jit(solution)/shard_map/all_to_all | solution.py:498
  31.4 1.4 collective-permute-start.3
  32.8 3.1 %collective-permute-start.2 = (bf16[384,128]{1,0:T(8,128)(2,1)S(1)}, bf16[384,128]{1,0:T(8,128)(2,1)S(1)}, u32[]{:S(2)}, u32[]{:S(2)}) collective-permute-start(bf16[384,128]{1,0:T(8,128)(2,1)S(1)} %copy-done.4), channel_id=1, source_target_pairs={{0,0},{1,200},{2,2},{3,202},{8,193},{9,9},{10,195},{11,11},{64,64}... | collective-permute-start | bytes 294920 | tf_op jit(solution)/shard_map/ppermute | solution.py:542
  35.9 3.6 %collective-permute-done.3.other_ref = bf16[384,128]{1,0:T(8,128)(2,1)S(1)} collective-permute-done((bf16[384,128]{1,0:T(8,128)(2,1)S(1)}, bf16[384,128]{1,0:T(8,128)(2,1)S(1)}, u32[]{:S(2)}, u32[]{:S(2)}) %collective-permute-start.3) | collective-permute-done | bytes 98336 | tf_op jit(solution)/shard_map/ppermute | solution.py:543
  39.5 0.4 collective-permute-done.2.own_ref.noise_ref
  39.9 2.1 %all-to-all-done.own_w_ref = bf16[8,368,128]{2,1,0:T(8,128)(2,1)S(1)} async-done(((bf16[8,368,128]{2,1,0:T(8,128)(2,1)}), bf16[8,368,128]{2,1,0:T(8,128)(2,1)S(1)}, u32[]{:S(2)}, u32[]{:S(2)}) %all-to-all-start) | async-done | bytes 753696 | tf_op jit(solution)/shard_map/all_to_all | solution.py:498
  42.1 0.0 collective-permute-start.4
  42.1 2.2 %collective-permute-done.4.other_w_ref = bf16[8,368,128]{2,1,0:T(8,128)(2,1)S(1)} collective-permute-done((bf16[8,368,128]{2,1,0:T(8,128)(2,1)S(1)}, bf16[8,368,128]{2,1,0:T(8,128)(2,1)S(1)}, u32[]{:S(2)}, u32[]{:S(2)}) %collective-permute-start.4) | collective-permute-done | bytes 753696 | tf_op jit(solution)/shard_map/ppermute | solution.py:559
  44.3 5.3 %all-to-all-start.1 = ((bf16[8,576,128]{2,1,0:T(8,128)(2,1)}), bf16[8,576,128]{2,1,0:T(8,128)(2,1)S(1)}, u32[]{:S(2)}, u32[]{:S(2)}) async-start(bf16[8,576,128]{2,1,0:T(8,128)(2,1)} %get-tuple-element.54), calls=%async_computation.1 | async-start | bytes 2359296 | tf_op jit(solution)/shard_map/all_to_all | solution.py:498
  49.7 0.4 maximum_bitcast_fusion
  50.1 0.1 copy.24
  50.2 0.1 reshape.44
  50.4 1.4 convert_element_type.43
  51.8 1.1 pad_convert_fusion.mods_ref.t_mods_ref.f_mods_ref.refs_0_.refs_1_
  52.9 1.8 sums.1.sums_ref
  54.8 8.2 %generator.1 = (bf16[16,32,128]{2,1,0:T(8,128)(2,1)}, bf16[3,256,3072]{2,1,0:T(8,128)(2,1)}, f32[3,256,192]{2,1,0:T(8,128)}, f32[3,256,192]{2,1,0:T(8,128)}) custom-call(s32[5]{0:T(128)S(1)} %copy-done.3, bf16[384,128]{1,0:T(8,128)(2,1)S(1)} %collective-permute-done.2.own_ref.noise_ref, bf16[384,128]{1,0:T(8,128)(2,1)S(1)} %collective-permute-done.3.other_ref, ...), custom_call_target="tpu_custom_call" | custom-call | flops 12000000000 | bytes 30000000 | tf_op jit(solution)/shard_map/generator/pallas_call | solution.py:585
  63.0 4.8 %all-to-all-done.1.own_w_ref = bf16[8,576,128]{2,1,0:T(8,128)(2,1)S(1)} async-done(((bf16[8,576,128]{2,1,0:T(8,128)(2,1)}), bf16[8,576,128]{2,1,0:T(8,128)(2,1)S(1)}, u32[]{:S(2)}, u32[]{:S(2)}) %all-to-all-start.1) | async-done | bytes 1179680 | tf_op jit(solution)/shard_map/all_to_all | solution.py:498
  67.7 5.3 %all-to-all-start.2 = ((bf16[16,32,128]{2,1,0:T(8,128)(2,1)}), bf16[16,32,128]{2,1,0:T(8,128)(2,1)S(1)}, u32[]{:S(2)}, u32[]{:S(2)}) async-start(bf16[16,32,128]{2,1,0:T(8,128)(2,1)} %get-tuple-element.61), calls=%async_computation.2 | async-start | bytes 262144 | tf_op jit(solution)/shard_map/all_to_all | solution.py:498
  73.1 0.1 fusion.2
  73.1 7.3 %all-to-all-done.2.got_ref = bf16[16,32,128]{2,1,0:T(8,128)(2,1)S(1)} async-done(((bf16[16,32,128]{2,1,0:T(8,128)(2,1)}), bf16[16,32,128]{2,1,0:T(8,128)(2,1)S(1)}, u32[]{:S(2)}, u32[]{:S(2)}) %all-to-all-start.2) | async-done | bytes 131104 | tf_op jit(solution)/shard_map/all_to_all | solution.py:498
  80.5 1.2 samples.1
  81.6 2.8 %collective-permute-start.5 = (bf16[8,576,128]{2,1,0:T(8,128)(2,1)S(1)}, bf16[8,576,128]{2,1,0:T(8,128)(2,1)S(1)}, u32[]{:S(2)}, u32[]{:S(2)}) collective-permute-start(bf16[8,576,128]{2,1,0:T(8,128)(2,1)S(1)} %all-to-all-done.1.own_w_ref), channel_id=1, source_target_pairs={{0,1},{1,0},{2,3},{3,2},{4,5},{5,4},{6,7},{7,6},{8,9},{9,8},{10,11... | collective-permute-start | bytes 3538952 | tf_op jit(solution)/shard_map/ppermute | solution.py:620
  84.4 10.5 %all_to_all.40.got_ref = f32[16,24,128]{2,1,0:T(8,128)S(1)} all-to-all(f32[16,24,128]{2,1,0:T(8,128)S(1)} %get-tuple-element.64), channel_id=1, replica_groups=mesh['g'=4,'x'=4,'h'=2,'w'=2,'v'=2,'s'=2] {'v','h','g'}, dimensions={0} | all-to-all | bytes 393216 | tf_op jit(solution)/shard_map/all_to_all | solution.py:498
  94.9 0.0 collective-permute-done.5.other_w_ref
  94.9 13.7 %score.1 = (bf16[16,64,128]{2,1,0:T(8,128)(2,1)S(1)}, f32[3,64,128]{2,1,0:T(8,128)S(1)}, bf16[3,256,3072]{2,1,0:T(8,128)(2,1)}, f32[3,256,192]{2,1,0:T(8,128)}, f32[3,256,192]{2,1,0:T(8,128)}) custom-call(s32[5]{0:T(128)S(1)} %copy-done.3, f32[3]{0:T(128)S(1)} %get-tuple-element.94.time_ref, f32[16,24,128]{2,1,0:T(8,128)S(1)} %all_to_all.40.got_ref, ...), custom_call_target="tpu_custom_call" | custom-call | flops 24000000000 | bytes 50000000 | tf_op jit(solution)/shard_map/score/pallas_call | solution.py:622
  108.6 13.1 %all_to_all.41.got_ref = bf16[16,64,128]{2,1,0:T(8,128)(2,1)S(1)} all-to-all(bf16[16,64,128]{2,1,0:T(8,128)(2,1)S(1)} %get-tuple-element.67), channel_id=1, replica_groups=mesh['g'=4,'x'=4,'h'=2,'w'=2,'v'=2,'s'=2] {'v','h','g'}, dimensions={0} | all-to-all | bytes 524288 | tf_op jit(solution)/shard_map/all_to_all | solution.py:498
  121.6 2.1 %cotangents.1 = bf16[16,64,128]{2,1,0:T(8,128)(2,1)S(1)} custom-call(s32[5]{0:T(128)S(1)} %copy-done.3, f32[3]{0:T(128)S(1)} %get-tuple-element.93.time_ref.gen_time_ref, f32[3]{0:T(128)S(1)} %get-tuple-element.94.time_ref, bf16[16,64,128]{2,1,0:T(8,128)(2,1)S(1)} %all_to_all.41.got_ref, bf16[384,128]{1,0:T(8,128)(2,1)S(1)} %collective-permute-done.2.own_ref.noise_ref, ...), custom_call_target="tpu_custom_call" | custom-call | tf_op jit(solution)/shard_map/cotangents/pallas_call | solution.py:651
  123.7 13.9 %all_to_all.42.got_ref = bf16[16,64,128]{2,1,0:T(8,128)(2,1)S(1)} all-to-all(bf16[16,64,128]{2,1,0:T(8,128)(2,1)S(1)} %cotangents.1), channel_id=1, replica_groups=mesh['g'=4,'x'=4,'h'=2,'w'=2,'v'=2,'s'=2] {'v','h','g'}, dimensions={0} | all-to-all | bytes 524288 | tf_op jit(solution)/shard_map/all_to_all | solution.py:498
  137.6 0.2 convert_reduce_fusion
  137.8 0.1 reduce_sum.14
  137.9 0.1 reduce_sum.18
  138.0 0.7 broadcast_in_dim.2
  138.7 7.5 %all-to-all-start.6 = ((f32[16,8,128]{2,1,0:T(8,128)}), f32[16,8,128]{2,1,0:T(8,128)S(1)}, u32[]{:S(2)}, u32[]{:S(2)}) async-start(f32[16,8,128]{2,1,0:T(8,128)} %broadcast_in_dim.2), calls=%async_computation.6 | async-start | bytes 131072 | tf_op jit(solution)/shard_map/all_to_all | solution.py:498
  146.2 0.2 collective-permute-start.6
  146.4 6.0 %gradient.2 = (bf16[8,288,128]{2,1,0:T(8,128)(2,1)S(1)}, bf16[8,288,128]{2,1,0:T(8,128)(2,1)S(1)}) custom-call(s32[5]{0:T(128)S(1)} %copy-done.3, bf16[16,64,128]{2,1,0:T(8,128)(2,1)S(1)} %all_to_all.42.got_ref, f32[9,8,3072]{2,1,0:T(8,128)S(1)} %pad_convert_fusion.mods_ref.t_mods_ref.f_mods_ref.refs_0_.refs_1_, bf16[64,3072]{1,0:T(8,128)(2,1)} %bitcast.27, ...), custom_call_target="tpu_custom_call" | custom-call | flops 7000000000 | bytes 20000000 | tf_op jit(solution)/shard_map/gradient/pallas_call | solution.py:679
  152.4 0.4 collective-permute-start.7
  152.8 0.7 all-to-all-done.6.refs_0_
  153.6 0.0 collective-permute-done.6
  153.6 6.1 %gradient.3 = (bf16[8,288,128]{2,1,0:T(8,128)(2,1)S(1)}, bf16[8,288,128]{2,1,0:T(8,128)(2,1)S(1)}) custom-call(s32[5]{0:T(128)S(1)} %copy-done.3, bf16[16,64,128]{2,1,0:T(8,128)(2,1)S(1)} %all_to_all.42.got_ref, f32[16,8,128]{2,1,0:T(8,128)S(1)} %all-to-all-done.6.refs_0_, f32[9,8,3072]{2,1,0:T(8,128)S(1)} %pad_convert_fusion.mods_ref.t_mods_ref.f_mods_ref.refs_0_.refs_1_, ...), custom_call_target="tpu_custom_call" | custom-call | flops 7000000000 | bytes 20000000 | tf_op jit(solution)/shard_map/gradient/pallas_call | solution.py:679
  159.7 0.5 collective-permute-start.8
  160.2 0.2 add_convert_fusion.1
  160.3 1.5 collective-permute-done.8
  161.8 0.2 add_convert_fusion
  162.0 1.1 pad_maximum_fusion
  163.1 5.8 %all-to-all-start.7 = ((bf16[8,576,128]{2,1,0:T(8,128)(2,1)}), bf16[8,576,128]{2,1,0:T(8,128)(2,1)S(1)}, u32[]{:S(2)}, u32[]{:S(2)}) async-start(bf16[8,576,128]{2,1,0:T(8,128)(2,1)} %pad_maximum_fusion), calls=%async_computation.7 | async-start | bytes 2359296 | tf_op jit(solution)/shard_map/all_to_all | solution.py:498
  168.9 17.7 %all-to-all-done.7.got_ref = bf16[8,576,128]{2,1,0:T(8,128)(2,1)S(1)} async-done(((bf16[8,576,128]{2,1,0:T(8,128)(2,1)}), bf16[8,576,128]{2,1,0:T(8,128)(2,1)S(1)}, u32[]{:S(2)}, u32[]{:S(2)}) %all-to-all-start.7) | async-done | bytes 1179680 | tf_op jit(solution)/shard_map/all_to_all | solution.py:498
  186.7 0.7 sum.1
  187.4 3.5 %collective-permute-start.9 = (bf16[2,144,128]{2,1,0:T(8,128)(2,1)S(1)}, bf16[2,144,128]{2,1,0:T(8,128)(2,1)S(1)}, u32[]{:S(2)}, u32[]{:S(2)}) collective-permute-start(bf16[2,144,128]{2,1,0:T(8,128)(2,1)S(1)} %get-tuple-element.83), channel_id=1, source_target_pairs={{0,128},{1,136},{2,130},{3,138},{8,129},{9,137},{10,131},{11,139},... | collective-permute-start | bytes 221192 | tf_op jit(solution)/shard_map/ppermute | solution.py:710
  190.9 0.5 collective-permute-start.10
  191.4 0.7 select_bitcast_fusion
  192.1 1.4 collective-permute-done.9.keep_ref
  193.5 4.5 %collective-permute-done.10.other_ref = bf16[2,144,128]{2,1,0:T(8,128)(2,1)S(1)} collective-permute-done((bf16[2,144,128]{2,1,0:T(8,128)(2,1)S(1)}, bf16[2,144,128]{2,1,0:T(8,128)(2,1)S(1)}, u32[]{:S(2)}, u32[]{:S(2)}) %collective-permute-start.10) | collective-permute-done | bytes 73760 | tf_op jit(solution)/shard_map/ppermute | solution.py:711
  198.0 1.3 place.1
  (16 shorter events, 0.1 us)
Async XLA Ops:
  5.1 11.0 %collective-permute-start = (bf16[528,128]{1,0:T(8,128)(2,1)}, bf16[528,128]{1,0:T(8,128)(2,1)S(1)}, u32[]{:S(2)}, u32[]{:S(2)}) collective-permute-start(bf16[528,128]{1,0:T(8,128)(2,1)} %get-tuple-element.45), channel_id=1, source_target_pairs={{0,128},{1,136},{2,130},{3,138},{8,129},{9,137},{10,131},{11,139},... | collective-permute-start | bytes 405512 | tf_op jit(solution)/shard_map/ppermute | solution.py:539
  12.5 9.9 %collective-permute-start.1 = (bf16[528,128]{1,0:T(8,128)(2,1)}, bf16[528,128]{1,0:T(8,128)(2,1)S(1)}, u32[]{:S(2)}, u32[]{:S(2)}) collective-permute-start(bf16[528,128]{1,0:T(8,128)(2,1)} %get-tuple-element.46), channel_id=1, source_target_pairs={{0,130},{1,138},{2,128},{3,136},{8,131},{9,139},{10,129},{11,137},... | collective-permute-start | bytes 405512 | tf_op jit(solution)/shard_map/ppermute | solution.py:540
  22.3 0.6 copy-start.2
  22.9 8.5 %copy-start.4 = (bf16[384,128]{1,0:T(8,128)(2,1)S(1)}, bf16[384,128]{1,0:T(8,128)(2,1)}, u32[]{:S(2)}) copy-start(bf16[384,128]{1,0:T(8,128)(2,1)} %get-tuple-element.52) | copy-start | bytes 294916
  25.0 17.0 %all-to-all-start = ((bf16[8,368,128]{2,1,0:T(8,128)(2,1)}), bf16[8,368,128]{2,1,0:T(8,128)(2,1)S(1)}, u32[]{:S(2)}, u32[]{:S(2)}) async-start(bf16[8,368,128]{2,1,0:T(8,128)(2,1)} %get-tuple-element.51), calls=%async_computation | async-start | bytes 1507328 | tf_op jit(solution)/shard_map/all_to_all | solution.py:498
  31.4 8.1 %collective-permute-start.3 = (bf16[384,128]{1,0:T(8,128)(2,1)S(1)}, bf16[384,128]{1,0:T(8,128)(2,1)S(1)}, u32[]{:S(2)}, u32[]{:S(2)}) collective-permute-start(bf16[384,128]{1,0:T(8,128)(2,1)S(1)} %copy-done.4), channel_id=1, source_target_pairs={{0,2},{1,202},{2,0},{3,200},{8,195},{9,11},{10,193},{11,9},{64,66}... | collective-permute-start | bytes 294920 | tf_op jit(solution)/shard_map/ppermute | solution.py:543
  32.8 7.1 %collective-permute-start.2 = (bf16[384,128]{1,0:T(8,128)(2,1)S(1)}, bf16[384,128]{1,0:T(8,128)(2,1)S(1)}, u32[]{:S(2)}, u32[]{:S(2)}) collective-permute-start(bf16[384,128]{1,0:T(8,128)(2,1)S(1)} %copy-done.4), channel_id=1, source_target_pairs={{0,0},{1,200},{2,2},{3,202},{8,193},{9,9},{10,195},{11,11},{64,64}... | collective-permute-start | bytes 294920 | tf_op jit(solution)/shard_map/ppermute | solution.py:542
  42.1 2.2 %collective-permute-start.4 = (bf16[8,368,128]{2,1,0:T(8,128)(2,1)S(1)}, bf16[8,368,128]{2,1,0:T(8,128)(2,1)S(1)}, u32[]{:S(2)}, u32[]{:S(2)}) collective-permute-start(bf16[8,368,128]{2,1,0:T(8,128)(2,1)S(1)} %all-to-all-done.own_w_ref), channel_id=1, source_target_pairs={{0,1},{1,0},{2,3},{3,2},{4,5},{5,4},{6,7},{7,6},{8,9},{9,8},{10,11... | collective-permute-start | bytes 2261000 | tf_op jit(solution)/shard_map/ppermute | solution.py:559
  44.3 5.3 %copy-start = (bf16[8,368,128]{2,1,0:T(8,128)(2,1)}, bf16[8,368,128]{2,1,0:T(8,128)(2,1)S(1)}, u32[]{:S(2)}) copy-start(bf16[8,368,128]{2,1,0:T(8,128)(2,1)S(1)} %collective-permute-done.4.other_w_ref) | copy-start | bytes 2260996
  44.3 23.4 %all-to-all-start.1 = ((bf16[8,576,128]{2,1,0:T(8,128)(2,1)}), bf16[8,576,128]{2,1,0:T(8,128)(2,1)S(1)}, u32[]{:S(2)}, u32[]{:S(2)}) async-start(bf16[8,576,128]{2,1,0:T(8,128)(2,1)} %get-tuple-element.54), calls=%async_computation.1 | async-start | bytes 2359296 | tf_op jit(solution)/shard_map/all_to_all | solution.py:498
  52.9 1.9 copy-start.1
  52.9 1.9 copy-start.3
  67.7 12.7 %all-to-all-start.2 = ((bf16[16,32,128]{2,1,0:T(8,128)(2,1)}), bf16[16,32,128]{2,1,0:T(8,128)(2,1)S(1)}, u32[]{:S(2)}, u32[]{:S(2)}) async-start(bf16[16,32,128]{2,1,0:T(8,128)(2,1)} %get-tuple-element.61), calls=%async_computation.2 | async-start | bytes 262144 | tf_op jit(solution)/shard_map/all_to_all | solution.py:498
  81.6 13.2 %collective-permute-start.5 = (bf16[8,576,128]{2,1,0:T(8,128)(2,1)S(1)}, bf16[8,576,128]{2,1,0:T(8,128)(2,1)S(1)}, u32[]{:S(2)}, u32[]{:S(2)}) collective-permute-start(bf16[8,576,128]{2,1,0:T(8,128)(2,1)S(1)} %all-to-all-done.1.own_w_ref), channel_id=1, source_target_pairs={{0,1},{1,0},{2,3},{3,2},{4,5},{5,4},{6,7},{7,6},{8,9},{9,8},{10,11... | collective-permute-start | bytes 3538952 | tf_op jit(solution)/shard_map/ppermute | solution.py:620
  138.7 14.8 %all-to-all-start.6 = ((f32[16,8,128]{2,1,0:T(8,128)}), f32[16,8,128]{2,1,0:T(8,128)S(1)}, u32[]{:S(2)}, u32[]{:S(2)}) async-start(f32[16,8,128]{2,1,0:T(8,128)} %broadcast_in_dim.2), calls=%async_computation.6 | async-start | bytes 131072 | tf_op jit(solution)/shard_map/all_to_all | solution.py:498
  146.2 7.4 %collective-permute-start.6 = (f32[3,64,128]{2,1,0:T(8,128)S(1)}, f32[3,64,128]{2,1,0:T(8,128)S(1)}, u32[]{:S(2)}, u32[]{:S(2)}) collective-permute-start(f32[3,64,128]{2,1,0:T(8,128)S(1)} %get-tuple-element.69), channel_id=1, source_target_pairs={{0,1},{1,0},{2,3},{3,2},{4,5},{5,4},{6,7},{7,6},{8,9},{9,8},{10,11... | collective-permute-start | bytes 294920 | tf_op jit(solution)/shard_map/ppermute | solution.py:666
  152.4 7.8 %collective-permute-start.7 = (bf16[8,288,128]{2,1,0:T(8,128)(2,1)S(1)}, bf16[8,288,128]{2,1,0:T(8,128)(2,1)S(1)}, u32[]{:S(2)}, u32[]{:S(2)}) collective-permute-start(bf16[8,288,128]{2,1,0:T(8,128)(2,1)S(1)} %get-tuple-element.76), channel_id=1, source_target_pairs={{0,1},{1,0},{2,3},{3,2},{4,5},{5,4},{6,7},{7,6},{8,9},{9,8},{10,11... | collective-permute-start | bytes 1769480 | tf_op jit(solution)/shard_map/ppermute | solution.py:693
  159.7 2.1 %collective-permute-start.8 = (bf16[8,288,128]{2,1,0:T(8,128)(2,1)S(1)}, bf16[8,288,128]{2,1,0:T(8,128)(2,1)S(1)}, u32[]{:S(2)}, u32[]{:S(2)}) collective-permute-start(bf16[8,288,128]{2,1,0:T(8,128)(2,1)S(1)} %get-tuple-element.82), channel_id=1, source_target_pairs={{0,1},{1,0},{2,3},{3,2},{4,5},{5,4},{6,7},{7,6},{8,9},{9,8},{10,11... | collective-permute-start | bytes 1769480 | tf_op jit(solution)/shard_map/ppermute | solution.py:693
  163.1 23.6 %all-to-all-start.7 = ((bf16[8,576,128]{2,1,0:T(8,128)(2,1)}), bf16[8,576,128]{2,1,0:T(8,128)(2,1)S(1)}, u32[]{:S(2)}, u32[]{:S(2)}) async-start(bf16[8,576,128]{2,1,0:T(8,128)(2,1)} %pad_maximum_fusion), calls=%async_computation.7 | async-start | bytes 2359296 | tf_op jit(solution)/shard_map/all_to_all | solution.py:498
  187.4 6.1 %collective-permute-start.9 = (bf16[2,144,128]{2,1,0:T(8,128)(2,1)S(1)}, bf16[2,144,128]{2,1,0:T(8,128)(2,1)S(1)}, u32[]{:S(2)}, u32[]{:S(2)}) collective-permute-start(bf16[2,144,128]{2,1,0:T(8,128)(2,1)S(1)} %get-tuple-element.83), channel_id=1, source_target_pairs={{0,128},{1,136},{2,130},{3,138},{8,129},{9,137},{10,131},{11,139},... | collective-permute-start | bytes 221192 | tf_op jit(solution)/shard_map/ppermute | solution.py:710
  190.9 7.1 %collective-permute-start.10 = (bf16[2,144,128]{2,1,0:T(8,128)(2,1)S(1)}, bf16[2,144,128]{2,1,0:T(8,128)(2,1)S(1)}, u32[]{:S(2)}, u32[]{:S(2)}) collective-permute-start(bf16[2,144,128]{2,1,0:T(8,128)(2,1)S(1)} %get-tuple-element.84), channel_id=1, source_target_pairs={{0,130},{1,138},{2,128},{3,136},{8,131},{9,139},{10,129},{11,137},... | collective-permute-start | bytes 221192 | tf_op jit(solution)/shard_map/ppermute | solution.py:711

commit v6 on v5

--- a/solution.py
+++ b/solution.py
@@ -164,25 +164,25 @@
     mean_ref[...] = jnp.broadcast_to(column, mean_ref.shape)
 
 
-def forward(x, embed_ref, mods_ref, final_ref, w_ref, gram_ref, mean_ref, shaped_ref, place_ref):
+def shape_tokens(x, embed_ref, mods_ref, image, gram_ref, mean_ref, store):
     turned = dot(x, gram_ref[...])
     turned = turned[:, :C] + turned[:, C : 2 * C] + turned[:, 2 * C :]
     inverse = lax.rsqrt(jnp.sum(turned * x.astype(F32), axis=1, keepdims=True) + norm_epsilon)
     inverse = jnp.broadcast_to(inverse, (TOKENS, BLOCK))
     twice = jnp.concatenate([x, x], axis=1)
     mean = mean_ref[:, 0:1]
-    preactivation = jnp.zeros((TOKENS, COLS), F32)
     for b in range(D // BLOCK):
         cut = slice(b * BLOCK, (b + 1) * BLOCK)
-        scaled = (embed_ref[:, cut].astype(F32) - mean) * (1.0 + mods_ref[0, 1:2, cut])
+        scaled = (embed_ref[:, cut].astype(F32) - mean) * (1.0 + mods_ref[image, 1:2, cut])
         scaled = jnp.concatenate(split_bits(scaled, 2), axis=0)
-        shaped = (dot(twice, scaled) * inverse + mods_ref[0, 0:1, cut]).astype(BF16)
-        shaped_ref[:, cut] = shaped
-        preactivation = preactivation + dot(shaped, w_ref[cut, :])
+        store(cut, (dot(twice, scaled) * inverse + mods_ref[image, 0:1, cut]).astype(BF16))
+
+
+def finish(preactivation, x, embed_ref, mods_ref, image, final_ref, place_ref):
     activated = jax.nn.gelu(preactivation, approximate=True).astype(BF16).astype(F32)
     own_hidden = dot(x, local_lanes(lambda at: embed_ref[:, at], place_ref))
-    gate = local_lanes(lambda at: mods_ref[0, 2:3, at], place_ref)
-    scale = local_lanes(lambda at: mods_ref[0, 4:5, at], place_ref)
+    gate = local_lanes(lambda at: mods_ref[image, 2:3, at], place_ref)
+    scale = local_lanes(lambda at: mods_ref[image, 4:5, at], place_ref)
     residual = own_hidden + gate * activated
     total = jnp.sum(residual, axis=1, keepdims=True)
     total_square = jnp.sum(residual * residual, axis=1, keepdims=True)
@@ -190,7 +190,7 @@
     final = local_lanes(lambda at: final_ref[:, at], place_ref)
     centred = ((residual - own_mean) * (1.0 + scale)).astype(BF16)
     partial = dot_turned(centred, final)
-    return preactivation, residual, partial, total, total_square
+    return residual, partial, total, total_square
 
 
 def owned(value):
@@ -258,18 +258,24 @@
     return jnp.where(v == 0, mine, other), jnp.where(v == 0, other, mine)
 
 
-def pack_kernel(place_ref, mine_ref, other_ref, gen_ref, score_ref):
+def pack_kernel(place_ref, mine_ref, other_ref, out_ref):
     v = place_ref[0]
-    cuts = [slice(n * ROWS, (n + 1) * ROWS) for n in range(5)]
-    ordered = [in_order(v, mine_ref[rows], other_ref[rows]) for rows in cuts]
-    parts = jnp.concatenate([ordered[4][0][:, :NARROW], ordered[4][1][:, :NARROW]], axis=1)
+    tiles = in_order(v, mine_ref[:ROWS], other_ref[:ROWS])
+    parts = in_order(v, mine_ref[4 * ROWS : MODS_AT], other_ref[4 * ROWS : MODS_AT])
+    parts = jnp.concatenate([part[:, :NARROW] for part in parts], axis=1)
     mods = in_order(v, mine_ref[MODS_AT:].astype(F32), other_ref[MODS_AT:].astype(F32))
     mods = jnp.concatenate([mods[0][:MODS_ROWS], mods[1][:MODS_ROWS], jnp.zeros((8, 128), F32)], axis=0)
-    gen = jnp.concatenate([*ordered[0], parts, mods.astype(BF16)], axis=0)
-    score = jnp.concatenate([*ordered[1], *ordered[2], *ordered[3]], axis=0)
+    gen = jnp.concatenate([*tiles, parts, mods.astype(BF16)], axis=0)
     for k in range(CHUNKS):
-        gen_ref[k] = gen
-        score_ref[k] = score
+        out_ref[k] = gen
+
+
+def pack_score_kernel(place_ref, mine_ref, other_ref, out_ref):
+    cuts = [slice(n * ROWS, (n + 1) * ROWS) for n in (1, 2, 3)]
+    ordered = [in_order(place_ref[0], mine_ref[rows], other_ref[rows]) for rows in cuts]
+    score = jnp.concatenate([block for pair in ordered for block in pair], axis=0)
+    for k in range(CHUNKS):
+        out_ref[k] = score
 
 
 def generator_kernel(place_ref, own_ref, other_ref, embed_ref, mods_ref, final_ref, own_w_ref, other_w_ref,
@@ -284,9 +290,13 @@
         sum_ref[:, 24:, :] = jnp.zeros((OWNERS, 8, 128), F32)
 
     x = jnp.concatenate(in_order(v, own_ref[:, :C], other_ref[:, :C]), axis=0)
-    pre, res, partial, total, square = forward(
-        x, embed_ref, mods_ref, final_ref, w_ref, gram_ref, mean_ref, shaped_ref.at[0], place_ref
-    )
+
+    def store(cut, shaped):
+        shaped_ref[0, :, cut] = shaped
+
+    shape_tokens(x, embed_ref, mods_ref, 0, gram_ref, mean_ref, store)
+    pre = dot(shaped_ref[0], w_ref[...])
+    res, partial, total, square = finish(pre, x, embed_ref, mods_ref, 0, final_ref, place_ref)
     pre_ref[0] = pre
     res_ref[0] = res
     pieces = owned(partial)
@@ -331,7 +341,7 @@
 def score_kernel(place_ref, time_ref, got_ref, own_ref, other_ref,
                  t_embed_ref, f_embed_ref, t_mods_ref, f_mods_ref, t_final_ref, f_final_ref, own_w_ref, other_w_ref,
                  part_ref, samples_ref, shaped_ref, pre_ref, res_ref,
-                 t_w_ref, f_w_ref, t_gram_ref, f_gram_ref, t_mean_ref, f_mean_ref, t_shaped_ref, sum_ref):
+                 t_w_ref, f_w_ref, t_gram_ref, f_gram_ref, t_mean_ref, f_mean_ref, t_shaped_ref, f_shaped_ref, x_ref, sum_ref):
     i = pl.program_id(0)
     v = place_ref[0]
 
@@ -349,21 +359,34 @@
     own, other = own_ref[:, C:].astype(F32), other_ref[:, C:].astype(F32)
     noise = jnp.concatenate(in_order(v, own, other), axis=0)
     noised = mix(samples, noise, time_ref[i])
-    _, _, t_partial, t_total, t_square = forward(
-        noised, t_embed_ref, t_mods_ref, t_final_ref, t_w_ref, t_gram_ref, t_mean_ref, t_shaped_ref, place_ref
-    )
-    pre, res, f_partial, f_total, f_square = forward(
-        noised, f_embed_ref, f_mods_ref, f_final_ref, f_w_ref, f_gram_ref, f_mean_ref, shaped_ref.at[0], place_ref
-    )
-    pre_ref[0] = pre
-    res_ref[0] = res
-    rows = row_pieces([owned(v) for v in (t_total, t_square, f_total, f_square)], 64)
-    sum_ref[:, pl.ds(pl.multiple_of(i * 16, 16), 16), :] = owned(jnp.concatenate([t_partial, f_partial], axis=1))
-    for n in range(2):
-        sum_ref[:, pl.ds(48 + 2 * i + n, 1), :] = rows[n]
+    x_ref[i] = noised
+    tokens = pl.ds(pl.multiple_of(i * TOKENS, TOKENS), TOKENS)
+
+    def t_store(cut, shaped):
+        t_shaped_ref[tokens, cut] = shaped
+
+    def f_store(cut, shaped):
+        f_shaped_ref[tokens, cut] = shaped
+        shaped_ref[0, :, cut] = shaped
+
+    shape_tokens(noised, t_embed_ref, t_mods_ref, i, t_gram_ref, t_mean_ref, t_store)
+    shape_tokens(noised, f_embed_ref, f_mods_ref, i, f_gram_ref, f_mean_ref, f_store)
 
     @pl.when(i == IMAGES - 1)
     def _():
+        t_pre = dot(t_shaped_ref[...], t_w_ref[...])
+        f_pre = dot(f_shaped_ref[...], f_w_ref[...])
+        for n in range(IMAGES):
+            x = x_ref[n]
+            rows = slice(n * TOKENS, (n + 1) * TOKENS)
+            _, t_partial, t_total, t_square = finish(t_pre[rows], x, t_embed_ref, t_mods_ref, n, t_final_ref, place_ref)
+            res, f_partial, f_total, f_square = finish(f_pre[rows], x, f_embed_ref, f_mods_ref, n, f_final_ref, place_ref)
+            pre_ref[n] = f_pre[rows]
+            res_ref[n] = res
+            sum_ref[:, 16 * n : 16 * n + 16, :] = owned(jnp.concatenate([t_partial, f_partial], axis=1))
+            pieces = row_pieces([owned(v) for v in (t_total, t_square, f_total, f_square)], 64)
+            for k in range(2):
+                sum_ref[:, 48 + 2 * n + k : 49 + 2 * n + k, :] = pieces[k]
         part_ref[...] = sum_ref[...].astype(BF16)
 
 
@@ -443,8 +466,9 @@
             res_grad = inverse * (out_grad * (1.0 + scale)) - slope * res_ref[i] + offset
             act_grad = res_grad * gate
             if net == 1:
-                inverse_gap = 1.0 / (gaps[i : i + 1, :] / (S * C) + gap_epsilon)
-                act_grad = act_grad * jnp.concatenate([inverse_gap, inverse_gap[:, :NARROW]], axis=1)
+                lane = lax.broadcasted_iota(jnp.int32, gaps.shape, 1)
+                total = jnp.sum(jnp.where(lane == i, gaps, 0.0), axis=1, keepdims=True)
+                act_grad = act_grad * (1.0 / (total / (S * C) + gap_epsilon))
             grad = act_grad * gelu_slope(pre_ref[i])
             turned = jnp.concatenate([grad, jnp.zeros((TOKENS, NARROW), F32)], axis=1).T
             left_ref[:, i * TOKENS : (i + 1) * TOKENS] = turned[:COLS].astype(BF16)
@@ -463,6 +487,13 @@
         for n, (low, high) in enumerate(zip(*sides, strict=True)):
             keep_ref[w, n * ROWS : (n + 1) * ROWS, :] = jnp.where(first, low, high)
             send_ref[w, n * ROWS : (n + 1) * ROWS, :] = jnp.where(first, high, low)
+
+
+def add_kernel(f_keep_ref, f_got_ref, g_keep_ref, g_got_ref, out_ref):
+    for n, (keep_ref, got_ref) in enumerate(((f_keep_ref, f_got_ref), (g_keep_ref, g_got_ref))):
+        for k in range(CHUNKS):
+            total = keep_ref[k].astype(F32) + got_ref[k].astype(F32)
+            out_ref[k, n * GEN_ROWS : (n + 1) * GEN_ROWS] = total.astype(BF16)
 
 
 def sum_kernel(place_ref, got_ref, keep_ref, send_ref):
@@ -542,19 +573,21 @@
     own_noise = lax.ppermute(noise, PLACES, NEAR)
     other_noise = lax.ppermute(noise, PLACES, NEAR_TURNED)
 
-    g_packed, packed = pl.pallas_call(
-        pack_kernel,
-        grid=(1,),
-        in_specs=[smem()] + [whole((SENT_ROWS, 128))] * 2,
-        out_specs=[whole((CHUNKS, GEN_CHUNK, 128)), whole((CHUNKS, SCORE_ROWS, 128))],
-        out_shape=[
-            jax.ShapeDtypeStruct((CHUNKS, GEN_CHUNK, 128), BF16),
-            jax.ShapeDtypeStruct((CHUNKS, SCORE_ROWS, 128), BF16),
-        ],
-        compiler_params=params(6),
-        name="pack",
-    )(place, mine, other)
+    def pack(kernel, rows):
+        return pl.pallas_call(
+            kernel,
+            grid=(1,),
+            in_specs=[smem()] + [whole((SENT_ROWS, 128))] * 2,
+            out_specs=whole((CHUNKS, rows, 128)),
+            out_shape=jax.ShapeDtypeStruct((CHUNKS, rows, 128), BF16),
+            compiler_params=params(6),
+            name="pack",
+        )(place, mine, other)
+
+    g_packed = pack(pack_kernel, GEN_CHUNK)
     g_packed = exchange(g_packed, GATHER)
+    mine, other, own_noise, other_noise = lax.optimization_barrier((mine, other, own_noise, other_noise))
+    packed = pack(pack_score_kernel, SCORE_ROWS)
     g_packed, own_noise, other_noise = lax.optimization_barrier((g_packed, own_noise, other_noise))
     g_other = lax.ppermute(g_packed, "s", SIBLING)
     packed, g_packed, g_other = lax.optimization_barrier((packed, g_packed, g_other))
@@ -597,7 +630,7 @@
         cost_estimate=pl.CostEstimate(flops=12 * 10**9, bytes_accessed=30 * 10**6, transcendentals=0),
         name="generator",
     )(place, own_noise, other_noise, gen_embed, mods, gen_final, g_packed, g_other)
-    packed, part, sums = lax.optimization_barrier((packed, part, sums))
+    packed, part = lax.optimization_barrier((packed, part))
     part = exchange(part, COMBINE)
 
     net_mods = lambda net: pl.BlockSpec((IMAGES, 8, D), lambda *_: (net, 0, 0))
@@ -624,12 +657,12 @@
         grid=(IMAGES,),
         in_specs=[
             smem(), smem(), whole((OWNERS, 24, 128)), noise_rows, noise_rows,
-            whole((C, D)), whole((C, D)), mods_of(1), mods_of(2), whole((C, D)), whole((C, D)),
+            whole((C, D)), whole((C, D)), net_mods(1), net_mods(2), whole((C, D)), whole((C, D)),
             *([whole((CHUNKS, SCORE_ROWS, 128))] * 2),
         ],
         out_specs=[
-            whole((OWNERS, 64, 128)), by_image(C, HALF), by_image(TOKENS, D), by_image(TOKENS, COLS),
-            by_image(TOKENS, COLS),
+            whole((OWNERS, 64, 128)), by_image(C, HALF), by_image(TOKENS, D), whole((IMAGES, TOKENS, COLS)),
+            whole((IMAGES, TOKENS, COLS)),
         ],
         out_shape=[
             jax.ShapeDtypeStruct((OWNERS, 64, 128), BF16),
@@ -638,10 +671,11 @@
         ],
         scratch_shapes=[
             *([pltpu.VMEM((D, COLS), BF16)] * 2), *([pltpu.VMEM((C, 3 * C), BF16)] * 2),
-            *([pltpu.VMEM((C, 128), F32)] * 2), pltpu.VMEM((TOKENS, D), BF16),
+            *([pltpu.VMEM((C, 128), F32)] * 2), *([pltpu.VMEM((IMAGES * TOKENS, D), BF16)] * 2),
+            pltpu.VMEM((IMAGES, TOKENS, C), BF16),
             pltpu.VMEM((OWNERS, 64, 128), F32),
         ],
-        compiler_params=params(22),
+        compiler_params=params(34),
         cost_estimate=pl.CostEstimate(flops=24 * 10**9, bytes_accessed=50 * 10**6, transcendentals=0),
         name="score",
     )(place, score_time, pack1, own_noise, other_noise, teacher_embed, fake_embed, mods, mods,
@@ -666,7 +700,7 @@
     samples = lax.ppermute(samples, "s", SIBLING)
 
     gap = jnp.sum(pack2[:, 48:57, 96].astype(F32).reshape(OWNERS, 3, 3), axis=(0, 2))
-    gap = jnp.broadcast_to(jnp.pad(gap, (0, 5))[None, :, None], (16, 8, 128))
+    gap = jnp.broadcast_to(jnp.pad(gap, (0, 125)), (16, 1, 128))
     gap = exchange(gap, TOKEN_AXES)
     samples, gap = lax.optimization_barrier((samples, gap))
     samples = jnp.where(lax.axis_index("h") == s, own_samples, samples).transpose(0, 2, 1)
@@ -680,7 +714,7 @@
             functools.partial(gradient_kernel, net),
             grid=(4,),
             in_specs=[
-                smem(), whole((OWNERS, 64, 128)), *([whole((16, 8, 128))] * len(gaps)), net_mods(mods_net),
+                smem(), whole((OWNERS, 64, 128)), *([whole((16, 1, 128))] * len(gaps)), net_mods(mods_net),
                 whole((C, D)), *([whole((IMAGES, TOKENS, COLS))] * 2), by_columns,
             ],
             out_specs=[partial_spec, partial_spec],
@@ -694,9 +728,15 @@
 
     pieces = gradient(0, (), 2, fake_final, f_pre, f_res, f_shaped)
     pieces += gradient(1, (gap,), 0, gen_final, g_pre, g_res, g_shaped)
-    both = jnp.concatenate(
-        [(pieces[n].astype(F32) + pieces[n + 1].astype(F32)).astype(BF16) for n in (0, 2)], axis=1
-    )
+    both = pl.pallas_call(
+        add_kernel,
+        grid=(1,),
+        in_specs=[whole((CHUNKS, GEN_ROWS, 128))] * 4,
+        out_specs=whole((CHUNKS, 2 * GEN_ROWS, 128)),
+        out_shape=jax.ShapeDtypeStruct((CHUNKS, 2 * GEN_ROWS, 128), BF16),
+        compiler_params=params(16),
+        name="add",
+    )(*pieces)
     tiles = jax.ShapeDtypeStruct((2, 144, 128), BF16)
     kept, sent = pl.pallas_call(
         sum_kernel,

time: 200 us -> 198 us (0.990)
  waiting for transfers between devices: 55.1 us -> 52.1 us
    pallas_call x1 -> x3, Pallas kernels: 2.11 us -> 4.56 us  [the longest x2 3.27 us: pack(): pl.pallas_call(kernel, grid=(1,), in_specs=[smem()] + [whole((SENT_ROWS,...]
  transfers between devices with their start and end apart: 16 -> 16, of which waited for: 13 -> 13; matrix products, arithmetic and copies ran while one was open for 2% -> 2% of each run, Pallas kernels for 11% -> 12%
where the time goes in v6:
time: 198 us
  waiting for transfers between devices  52.1 us (26%)
  starting transfers between devices  51.6 us (26%)
  Pallas kernels  46.9 us (24%)
  blocking collectives  37.4 us (19%)
  other arithmetic  4.91 us (2%)
  local copies, waits for them, and re-layouts  3.81 us (2%)
    all_to_all x3, blocking collectives, exchange(): return lax.all_to_all(value, axes, 0, 0)  37.4 us
    all_to_all x5, waiting for transfers between devices, exchange(): return lax.all_to_all(value, axes, 0, 0)  31.2 us
    all_to_all x5, starting transfers between devices, exchange(): return lax.all_to_all(value, axes, 0, 0)  30.4 us
    pallas_call x1, Pallas kernels, shards(): pl.pallas_call(score_kernel, grid=(IMAGES,), in_specs=[smem(), smem(), wh...  12.2 us
    pallas_call x2, Pallas kernels, gradient(): pl.pallas_call(functools.partial(gradient_kernel, net), grid=(4,), in_spe...  12.2 us
    pallas_call x1, Pallas kernels, shards(): pl.pallas_call(generator_kernel, grid=(IMAGES,), in_specs=[smem(), noise_...  8.5 us
    ppermute x1, starting transfers between devices, shards(): mine = lax.ppermute(mine, PLACES, SWAP)  7.41 us
    ppermute x1, waiting for transfers between devices, shards(): other = lax.ppermute(other, PLACES, SWAP_TURNED)  6.28 us
  transfers between devices with their start and end apart: 16, of which 13 were waited for; matrix products, arithmetic and copies ran while one was open for 2% of the time, Pallas kernels for 12%

profile of v6, /device:TPU:1, one launch (start us, length us, event | category | flops | bytes accessed | tf_op | source)
XLA Modules:
  0.0 197.5 jit_solution(18082623274930927088)
XLA Ops:
  0.7 0.8 broadcast_multiply_fusion
  1.4 0.1 multiply_cosine_fusion
  1.5 0.6 multiply_convert_fusion.cond_ref
  2.1 0.7 stack.32.place_ref
  2.8 2.4 %split.1 = (bf16[528,128]{1,0:T(8,128)(2,1)}, bf16[528,128]{1,0:T(8,128)(2,1)}, bf16[384,128]{1,0:T(8,128)(2,1)}) custom-call(s32[5]{0:T(128)} %stack.32.place_ref, bf16[6,256]{1,0:T(8,128)(2,1)} %multiply_convert_fusion.cond_ref, bf16[3,64,128]{2,1,0:T(8,128)(2,1)} %bitcast.34, bf16[3,64,128]{2,1,0:T(8,128)(2,1)} %bitcast.35, bf16[96,384]{1,0:T(8,128)(2,1)} %gen_ref.1, ...), custom_call_target="tpu_custom_call" | custom-call | tf_op jit(solution)/shard_map/split/pallas_call | solution.py:559
  5.2 7.4 %collective-permute-start = (bf16[528,128]{1,0:T(8,128)(2,1)}, bf16[528,128]{1,0:T(8,128)(2,1)S(1)}, u32[]{:S(2)}, u32[]{:S(2)}) collective-permute-start(bf16[528,128]{1,0:T(8,128)(2,1)} %get-tuple-element.46), channel_id=1, source_target_pairs={{0,128},{1,136},{2,130},{3,138},{8,129},{9,137},{10,131},{11,139},... | collective-permute-start | bytes 405512 | tf_op jit(solution)/shard_map/ppermute | solution.py:570
  12.6 1.1 collective-permute-start.1
  13.7 2.5 %collective-permute-done.mine_ref = bf16[528,128]{1,0:T(8,128)(2,1)S(1)} collective-permute-done((bf16[528,128]{1,0:T(8,128)(2,1)}, bf16[528,128]{1,0:T(8,128)(2,1)S(1)}, u32[]{:S(2)}, u32[]{:S(2)}) %collective-permute-start) | collective-permute-done | bytes 135200 | tf_op jit(solution)/shard_map/ppermute | solution.py:570
  16.2 6.3 %collective-permute-done.1.other_ref = bf16[528,128]{1,0:T(8,128)(2,1)S(1)} collective-permute-done((bf16[528,128]{1,0:T(8,128)(2,1)}, bf16[528,128]{1,0:T(8,128)(2,1)S(1)}, u32[]{:S(2)}, u32[]{:S(2)}) %collective-permute-start.1) | collective-permute-done | bytes 135200 | tf_op jit(solution)/shard_map/ppermute | solution.py:571
  22.4 0.7 copy-done
  23.1 1.5 pack.3
  24.6 6.4 %all-to-all-start = ((bf16[8,368,128]{2,1,0:T(8,128)(2,1)}), bf16[8,368,128]{2,1,0:T(8,128)(2,1)S(1)}, u32[]{:S(2)}, u32[]{:S(2)}) async-start(bf16[8,368,128]{2,1,0:T(8,128)(2,1)} %pack.3), calls=%async_computation | async-start | bytes 1507328 | tf_op jit(solution)/shard_map/all_to_all | solution.py:529
  31.0 1.4 collective-permute-start.3
  32.4 3.1 %collective-permute-start.2 = (bf16[384,128]{1,0:T(8,128)(2,1)S(1)}, bf16[384,128]{1,0:T(8,128)(2,1)S(1)}, u32[]{:S(2)}, u32[]{:S(2)}) collective-permute-start(bf16[384,128]{1,0:T(8,128)(2,1)S(1)} %copy-done.2), channel_id=1, source_target_pairs={{0,0},{1,200},{2,2},{3,202},{8,193},{9,9},{10,195},{11,11},{64,64}... | collective-permute-start | bytes 294920 | tf_op jit(solution)/shard_map/ppermute | solution.py:573
  35.5 3.6 %collective-permute-done.3.other_ref = bf16[384,128]{1,0:T(8,128)(2,1)S(1)} collective-permute-done((bf16[384,128]{1,0:T(8,128)(2,1)S(1)}, bf16[384,128]{1,0:T(8,128)(2,1)S(1)}, u32[]{:S(2)}, u32[]{:S(2)}) %collective-permute-start.3) | collective-permute-done | bytes 98336 | tf_op jit(solution)/shard_map/ppermute | solution.py:574
  39.1 0.4 collective-permute-done.2.own_ref.noise_ref
  39.5 2.1 %all-to-all-done.own_w_ref = bf16[8,368,128]{2,1,0:T(8,128)(2,1)S(1)} async-done(((bf16[8,368,128]{2,1,0:T(8,128)(2,1)}), bf16[8,368,128]{2,1,0:T(8,128)(2,1)S(1)}, u32[]{:S(2)}, u32[]{:S(2)}) %all-to-all-start) | async-done | bytes 753696 | tf_op jit(solution)/shard_map/all_to_all | solution.py:529
  41.7 0.0 collective-permute-start.4
  41.7 1.7 pack.2
  43.4 0.6 collective-permute-done.4.other_w_ref
  44.0 5.3 %all-to-all-start.1 = ((bf16[8,576,128]{2,1,0:T(8,128)(2,1)}), bf16[8,576,128]{2,1,0:T(8,128)(2,1)S(1)}, u32[]{:S(2)}, u32[]{:S(2)}) async-start(bf16[8,576,128]{2,1,0:T(8,128)(2,1)} %pack.2), calls=%async_computation.1 | async-start | bytes 2359296 | tf_op jit(solution)/shard_map/all_to_all | solution.py:529
  49.3 0.9 broadcast_select_fusion.1
  50.3 0.4 maximum_bitcast_fusion
  50.8 0.1 copy.24
  50.9 0.1 reshape.43
  51.0 1.4 convert_element_type.25
  52.4 1.1 pad_convert_fusion.mods_ref.t_mods_ref.f_mods_ref.refs_0_.refs_1_
  53.5 8.5 %generator.1 = (bf16[16,32,128]{2,1,0:T(8,128)(2,1)}, bf16[3,256,3072]{2,1,0:T(8,128)(2,1)}, f32[3,256,192]{2,1,0:T(8,128)}, f32[3,256,192]{2,1,0:T(8,128)}) custom-call(s32[5]{0:T(128)S(1)} %copy-done.1, bf16[384,128]{1,0:T(8,128)(2,1)S(1)} %collective-permute-done.2.own_ref.noise_ref, bf16[384,128]{1,0:T(8,128)(2,1)S(1)} %collective-permute-done.3.other_ref, ...), custom_call_target="tpu_custom_call" | custom-call | flops 12000000000 | bytes 30000000 | tf_op jit(solution)/shard_map/generator/pallas_call | solution.py:618
  62.0 5.5 %all-to-all-done.1.own_w_ref = bf16[8,576,128]{2,1,0:T(8,128)(2,1)S(1)} async-done(((bf16[8,576,128]{2,1,0:T(8,128)(2,1)}), bf16[8,576,128]{2,1,0:T(8,128)(2,1)S(1)}, u32[]{:S(2)}, u32[]{:S(2)}) %all-to-all-start.1) | async-done | bytes 1179680 | tf_op jit(solution)/shard_map/all_to_all | solution.py:529
  67.5 5.3 %all-to-all-start.2 = ((bf16[16,32,128]{2,1,0:T(8,128)(2,1)}), bf16[16,32,128]{2,1,0:T(8,128)(2,1)S(1)}, u32[]{:S(2)}, u32[]{:S(2)}) async-start(bf16[16,32,128]{2,1,0:T(8,128)(2,1)} %get-tuple-element.64), calls=%async_computation.2 | async-start | bytes 262144 | tf_op jit(solution)/shard_map/all_to_all | solution.py:529
  72.8 0.1 fusion.2
  72.9 1.8 sums.1.sums_ref
  74.7 5.6 %all-to-all-done.2.got_ref = bf16[16,32,128]{2,1,0:T(8,128)(2,1)S(1)} async-done(((bf16[16,32,128]{2,1,0:T(8,128)(2,1)}), bf16[16,32,128]{2,1,0:T(8,128)(2,1)S(1)}, u32[]{:S(2)}, u32[]{:S(2)}) %all-to-all-start.2) | async-done | bytes 131104 | tf_op jit(solution)/shard_map/all_to_all | solution.py:529
  80.2 1.2 samples.1
  81.4 2.8 %collective-permute-start.5 = (bf16[8,576,128]{2,1,0:T(8,128)(2,1)S(1)}, bf16[8,576,128]{2,1,0:T(8,128)(2,1)S(1)}, u32[]{:S(2)}, u32[]{:S(2)}) collective-permute-start(bf16[8,576,128]{2,1,0:T(8,128)(2,1)S(1)} %all-to-all-done.1.own_w_ref), channel_id=1, source_target_pairs={{0,1},{1,0},{2,3},{3,2},{4,5},{5,4},{6,7},{7,6},{8,9},{9,8},{10,11... | collective-permute-start | bytes 3538952 | tf_op jit(solution)/shard_map/ppermute | solution.py:653
  84.1 10.5 %all_to_all.40.got_ref = f32[16,24,128]{2,1,0:T(8,128)S(1)} all-to-all(f32[16,24,128]{2,1,0:T(8,128)S(1)} %get-tuple-element.66), channel_id=1, replica_groups=mesh['g'=4,'x'=4,'h'=2,'w'=2,'v'=2,'s'=2] {'v','h','g'}, dimensions={0} | all-to-all | bytes 393216 | tf_op jit(solution)/shard_map/all_to_all | solution.py:529
  94.6 0.0 collective-permute-done.5.other_w_ref
  94.6 12.2 %score.1 = (bf16[16,64,128]{2,1,0:T(8,128)(2,1)S(1)}, f32[3,64,128]{2,1,0:T(8,128)S(1)}, bf16[3,256,3072]{2,1,0:T(8,128)(2,1)}, f32[3,256,192]{2,1,0:T(8,128)}, f32[3,256,192]{2,1,0:T(8,128)}) custom-call(s32[5]{0:T(128)S(1)} %copy-done.1, f32[3]{0:T(128)S(1)} %get-tuple-element.96.time_ref, f32[16,24,128]{2,1,0:T(8,128)S(1)} %all_to_all.40.got_ref, ...), custom_call_target="tpu_custom_call" | custom-call | flops 24000000000 | bytes 50000000 | tf_op jit(solution)/shard_map/score/pallas_call | solution.py:655
  106.8 13.1 %all_to_all.41.got_ref = bf16[16,64,128]{2,1,0:T(8,128)(2,1)S(1)} all-to-all(bf16[16,64,128]{2,1,0:T(8,128)(2,1)S(1)} %get-tuple-element.69), channel_id=1, replica_groups=mesh['g'=4,'x'=4,'h'=2,'w'=2,'v'=2,'s'=2] {'v','h','g'}, dimensions={0} | all-to-all | bytes 524288 | tf_op jit(solution)/shard_map/all_to_all | solution.py:529
  119.9 2.1 %cotangents.1 = bf16[16,64,128]{2,1,0:T(8,128)(2,1)S(1)} custom-call(s32[5]{0:T(128)S(1)} %copy-done.1, f32[3]{0:T(128)S(1)} %get-tuple-element.95.time_ref.gen_time_ref, f32[3]{0:T(128)S(1)} %get-tuple-element.96.time_ref, bf16[16,64,128]{2,1,0:T(8,128)(2,1)S(1)} %all_to_all.41.got_ref, bf16[384,128]{1,0:T(8,128)(2,1)S(1)} %collective-permute-done.2.own_ref.noise_ref, ...), custom_call_target="tpu_custom_call" | custom-call | tf_op jit(solution)/shard_map/cotangents/pallas_call | solution.py:685
  122.0 13.9 %all_to_all.42.got_ref = bf16[16,64,128]{2,1,0:T(8,128)(2,1)S(1)} all-to-all(bf16[16,64,128]{2,1,0:T(8,128)(2,1)S(1)} %cotangents.1), channel_id=1, replica_groups=mesh['g'=4,'x'=4,'h'=2,'w'=2,'v'=2,'s'=2] {'v','h','g'}, dimensions={0} | all-to-all | bytes 524288 | tf_op jit(solution)/shard_map/all_to_all | solution.py:529
  135.9 0.2 convert_reduce_fusion
  136.1 0.1 reduce_sum.14
  136.2 0.1 reduce_sum.18
  136.3 0.6 broadcast_in_dim.2
  136.9 7.5 %all-to-all-start.6 = ((f32[16,1,128]{2,1,0:T(1,128)}), f32[16,1,128]{2,1,0:T(1,128)S(1)}, u32[]{:S(2)}, u32[]{:S(2)}) async-start(f32[16,1,128]{2,1,0:T(1,128)} %broadcast_in_dim.2), calls=%async_computation.6 | async-start | bytes 16384 | tf_op jit(solution)/shard_map/all_to_all | solution.py:529
  144.4 0.2 collective-permute-start.6
  144.6 6.0 %gradient.2 = (bf16[8,288,128]{2,1,0:T(8,128)(2,1)S(1)}, bf16[8,288,128]{2,1,0:T(8,128)(2,1)S(1)}) custom-call(s32[5]{0:T(128)S(1)} %copy-done.1, bf16[16,64,128]{2,1,0:T(8,128)(2,1)S(1)} %all_to_all.42.got_ref, f32[9,8,3072]{2,1,0:T(8,128)S(1)} %pad_convert_fusion.mods_ref.t_mods_ref.f_mods_ref.refs_0_.refs_1_, bf16[64,3072]{1,0:T(8,128)(2,1)} %bitcast.27, ...), custom_call_target="tpu_custom_call" | custom-call | flops 7000000000 | bytes 20000000 | tf_op jit(solution)/shard_map/gradient/pallas_call | solution.py:713
  150.6 0.4 collective-permute-start.7
  151.0 0.3 all-to-all-done.6.refs_0_
  151.3 6.1 %gradient.3 = (bf16[8,288,128]{2,1,0:T(8,128)(2,1)S(1)}, bf16[8,288,128]{2,1,0:T(8,128)(2,1)S(1)}) custom-call(s32[5]{0:T(128)S(1)} %copy-done.1, bf16[16,64,128]{2,1,0:T(8,128)(2,1)S(1)} %all_to_all.42.got_ref, f32[16,1,128]{2,1,0:T(1,128)S(1)} %all-to-all-done.6.refs_0_, f32[9,8,3072]{2,1,0:T(8,128)S(1)} %pad_convert_fusion.mods_ref.t_mods_ref.f_mods_ref.refs_0_.refs_1_, ...), custom_call_target="tpu_custom_call" | custom-call | flops 7000000000 | bytes 20000000 | tf_op jit(solution)/shard_map/gradient/pallas_call | solution.py:713
  157.4 0.8 collective-permute-start.8
  158.2 0.0 collective-permute-done.7.f_got_ref
  158.2 1.6 collective-permute-done.8.g_got_ref
  159.8 1.3 add.46
  161.1 6.0 %all-to-all-start.7 = ((bf16[8,576,128]{2,1,0:T(8,128)(2,1)}), bf16[8,576,128]{2,1,0:T(8,128)(2,1)S(1)}, u32[]{:S(2)}, u32[]{:S(2)}) async-start(bf16[8,576,128]{2,1,0:T(8,128)(2,1)} %add.46), calls=%async_computation.7 | async-start | bytes 2359296 | tf_op jit(solution)/shard_map/all_to_all | solution.py:529
  167.1 17.7 %all-to-all-done.7.got_ref = bf16[8,576,128]{2,1,0:T(8,128)(2,1)S(1)} async-done(((bf16[8,576,128]{2,1,0:T(8,128)(2,1)}), bf16[8,576,128]{2,1,0:T(8,128)(2,1)S(1)}, u32[]{:S(2)}, u32[]{:S(2)}) %all-to-all-start.7) | async-done | bytes 1179680 | tf_op jit(solution)/shard_map/all_to_all | solution.py:529
  184.9 0.7 sum.1
  185.6 3.5 %collective-permute-start.9 = (bf16[2,144,128]{2,1,0:T(8,128)(2,1)S(1)}, bf16[2,144,128]{2,1,0:T(8,128)(2,1)S(1)}, u32[]{:S(2)}, u32[]{:S(2)}) collective-permute-start(bf16[2,144,128]{2,1,0:T(8,128)(2,1)S(1)} %get-tuple-element.85), channel_id=1, source_target_pairs={{0,128},{1,136},{2,130},{3,138},{8,129},{9,137},{10,131},{11,139},... | collective-permute-start | bytes 221192 | tf_op jit(solution)/shard_map/ppermute | solution.py:750
  189.1 0.5 collective-permute-start.10
  189.6 0.7 select_bitcast_fusion
  190.3 1.4 collective-permute-done.9.keep_ref
  191.7 4.5 %collective-permute-done.10.other_ref = bf16[2,144,128]{2,1,0:T(8,128)(2,1)S(1)} collective-permute-done((bf16[2,144,128]{2,1,0:T(8,128)(2,1)S(1)}, bf16[2,144,128]{2,1,0:T(8,128)(2,1)S(1)}, u32[]{:S(2)}, u32[]{:S(2)}) %collective-permute-start.10) | collective-permute-done | bytes 73760 | tf_op jit(solution)/shard_map/ppermute | solution.py:751
  196.2 1.3 place.1
  (11 shorter events, 0.1 us)
Async XLA Ops:
  5.2 11.0 %collective-permute-start = (bf16[528,128]{1,0:T(8,128)(2,1)}, bf16[528,128]{1,0:T(8,128)(2,1)S(1)}, u32[]{:S(2)}, u32[]{:S(2)}) collective-permute-start(bf16[528,128]{1,0:T(8,128)(2,1)} %get-tuple-element.46), channel_id=1, source_target_pairs={{0,128},{1,136},{2,130},{3,138},{8,129},{9,137},{10,131},{11,139},... | collective-permute-start | bytes 405512 | tf_op jit(solution)/shard_map/ppermute | solution.py:570
  12.6 9.9 %collective-permute-start.1 = (bf16[528,128]{1,0:T(8,128)(2,1)}, bf16[528,128]{1,0:T(8,128)(2,1)S(1)}, u32[]{:S(2)}, u32[]{:S(2)}) collective-permute-start(bf16[528,128]{1,0:T(8,128)(2,1)} %get-tuple-element.47), channel_id=1, source_target_pairs={{0,130},{1,138},{2,128},{3,136},{8,131},{9,139},{10,129},{11,137},... | collective-permute-start | bytes 405512 | tf_op jit(solution)/shard_map/ppermute | solution.py:571
  22.4 0.7 copy-start
  23.1 7.9 %copy-start.2 = (bf16[384,128]{1,0:T(8,128)(2,1)S(1)}, bf16[384,128]{1,0:T(8,128)(2,1)}, u32[]{:S(2)}) copy-start(bf16[384,128]{1,0:T(8,128)(2,1)} %get-tuple-element.51) | copy-start | bytes 294916
  23.1 18.6 %copy-start.1 = (s32[5]{0:T(128)S(1)}, s32[5]{0:T(128)}, u32[]{:S(2)}) copy-start(s32[5]{0:T(128)} %stack.32.place_ref) | copy-start | bytes 64
  24.6 17.0 %all-to-all-start = ((bf16[8,368,128]{2,1,0:T(8,128)(2,1)}), bf16[8,368,128]{2,1,0:T(8,128)(2,1)S(1)}, u32[]{:S(2)}, u32[]{:S(2)}) async-start(bf16[8,368,128]{2,1,0:T(8,128)(2,1)} %pack.3), calls=%async_computation | async-start | bytes 1507328 | tf_op jit(solution)/shard_map/all_to_all | solution.py:529
  31.0 8.1 %collective-permute-start.3 = (bf16[384,128]{1,0:T(8,128)(2,1)S(1)}, bf16[384,128]{1,0:T(8,128)(2,1)S(1)}, u32[]{:S(2)}, u32[]{:S(2)}) collective-permute-start(bf16[384,128]{1,0:T(8,128)(2,1)S(1)} %copy-done.2), channel_id=1, source_target_pairs={{0,2},{1,202},{2,0},{3,200},{8,195},{9,11},{10,193},{11,9},{64,66}... | collective-permute-start | bytes 294920 | tf_op jit(solution)/shard_map/ppermute | solution.py:574
  32.4 7.1 %collective-permute-start.2 = (bf16[384,128]{1,0:T(8,128)(2,1)S(1)}, bf16[384,128]{1,0:T(8,128)(2,1)S(1)}, u32[]{:S(2)}, u32[]{:S(2)}) collective-permute-start(bf16[384,128]{1,0:T(8,128)(2,1)S(1)} %copy-done.2), channel_id=1, source_target_pairs={{0,0},{1,200},{2,2},{3,202},{8,193},{9,9},{10,195},{11,11},{64,64}... | collective-permute-start | bytes 294920 | tf_op jit(solution)/shard_map/ppermute | solution.py:573
  41.7 2.4 %collective-permute-start.4 = (bf16[8,368,128]{2,1,0:T(8,128)(2,1)S(1)}, bf16[8,368,128]{2,1,0:T(8,128)(2,1)}, u32[]{:S(2)}, u32[]{:S(2)}) collective-permute-start(bf16[8,368,128]{2,1,0:T(8,128)(2,1)S(1)} %all-to-all-done.own_w_ref), channel_id=1, source_target_pairs={{0,1},{1,0},{2,3},{3,2},{4,5},{5,4},{6,7},{7,6},{8,9},{9,8},{10,11... | collective-permute-start | bytes 2261000 | tf_op jit(solution)/shard_map/ppermute | solution.py:592
  44.0 23.4 %all-to-all-start.1 = ((bf16[8,576,128]{2,1,0:T(8,128)(2,1)}), bf16[8,576,128]{2,1,0:T(8,128)(2,1)S(1)}, u32[]{:S(2)}, u32[]{:S(2)}) async-start(bf16[8,576,128]{2,1,0:T(8,128)(2,1)} %pack.2), calls=%async_computation.1 | async-start | bytes 2359296 | tf_op jit(solution)/shard_map/all_to_all | solution.py:529
  67.5 12.7 %all-to-all-start.2 = ((bf16[16,32,128]{2,1,0:T(8,128)(2,1)}), bf16[16,32,128]{2,1,0:T(8,128)(2,1)S(1)}, u32[]{:S(2)}, u32[]{:S(2)}) async-start(bf16[16,32,128]{2,1,0:T(8,128)(2,1)} %get-tuple-element.64), calls=%async_computation.2 | async-start | bytes 262144 | tf_op jit(solution)/shard_map/all_to_all | solution.py:529
  81.4 13.2 %collective-permute-start.5 = (bf16[8,576,128]{2,1,0:T(8,128)(2,1)S(1)}, bf16[8,576,128]{2,1,0:T(8,128)(2,1)S(1)}, u32[]{:S(2)}, u32[]{:S(2)}) collective-permute-start(bf16[8,576,128]{2,1,0:T(8,128)(2,1)S(1)} %all-to-all-done.1.own_w_ref), channel_id=1, source_target_pairs={{0,1},{1,0},{2,3},{3,2},{4,5},{5,4},{6,7},{7,6},{8,9},{9,8},{10,11... | collective-permute-start | bytes 3538952 | tf_op jit(solution)/shard_map/ppermute | solution.py:653
  136.9 14.4 %all-to-all-start.6 = ((f32[16,1,128]{2,1,0:T(1,128)}), f32[16,1,128]{2,1,0:T(1,128)S(1)}, u32[]{:S(2)}, u32[]{:S(2)}) async-start(f32[16,1,128]{2,1,0:T(1,128)} %broadcast_in_dim.2), calls=%async_computation.6 | async-start | bytes 16384 | tf_op jit(solution)/shard_map/all_to_all | solution.py:529
  144.4 6.9 %collective-permute-start.6 = (f32[3,64,128]{2,1,0:T(8,128)S(1)}, f32[3,64,128]{2,1,0:T(8,128)S(1)}, u32[]{:S(2)}, u32[]{:S(2)}) collective-permute-start(f32[3,64,128]{2,1,0:T(8,128)S(1)} %get-tuple-element.71), channel_id=1, source_target_pairs={{0,1},{1,0},{2,3},{3,2},{4,5},{5,4},{6,7},{7,6},{8,9},{9,8},{10,11... | collective-permute-start | bytes 294920 | tf_op jit(solution)/shard_map/ppermute | solution.py:700
  150.6 7.6 %collective-permute-start.7 = (bf16[8,288,128]{2,1,0:T(8,128)(2,1)S(1)}, bf16[8,288,128]{2,1,0:T(8,128)(2,1)S(1)}, u32[]{:S(2)}, u32[]{:S(2)}) collective-permute-start(bf16[8,288,128]{2,1,0:T(8,128)(2,1)S(1)} %get-tuple-element.78), channel_id=1, source_target_pairs={{0,1},{1,0},{2,3},{3,2},{4,5},{5,4},{6,7},{7,6},{8,9},{9,8},{10,11... | collective-permute-start | bytes 1769480 | tf_op jit(solution)/shard_map/ppermute | solution.py:727
  157.4 2.4 %collective-permute-start.8 = (bf16[8,288,128]{2,1,0:T(8,128)(2,1)S(1)}, bf16[8,288,128]{2,1,0:T(8,128)(2,1)S(1)}, u32[]{:S(2)}, u32[]{:S(2)}) collective-permute-start(bf16[8,288,128]{2,1,0:T(8,128)(2,1)S(1)} %get-tuple-element.84), channel_id=1, source_target_pairs={{0,1},{1,0},{2,3},{3,2},{4,5},{5,4},{6,7},{7,6},{8,9},{9,8},{10,11... | collective-permute-start | bytes 1769480 | tf_op jit(solution)/shard_map/ppermute | solution.py:727
  161.1 23.8 %all-to-all-start.7 = ((bf16[8,576,128]{2,1,0:T(8,128)(2,1)}), bf16[8,576,128]{2,1,0:T(8,128)(2,1)S(1)}, u32[]{:S(2)}, u32[]{:S(2)}) async-start(bf16[8,576,128]{2,1,0:T(8,128)(2,1)} %add.46), calls=%async_computation.7 | async-start | bytes 2359296 | tf_op jit(solution)/shard_map/all_to_all | solution.py:529
  185.6 6.1 %collective-permute-start.9 = (bf16[2,144,128]{2,1,0:T(8,128)(2,1)S(1)}, bf16[2,144,128]{2,1,0:T(8,128)(2,1)S(1)}, u32[]{:S(2)}, u32[]{:S(2)}) collective-permute-start(bf16[2,144,128]{2,1,0:T(8,128)(2,1)S(1)} %get-tuple-element.85), channel_id=1, source_target_pairs={{0,128},{1,136},{2,130},{3,138},{8,129},{9,137},{10,131},{11,139},... | collective-permute-start | bytes 221192 | tf_op jit(solution)/shard_map/ppermute | solution.py:750
  189.1 7.1 %collective-permute-start.10 = (bf16[2,144,128]{2,1,0:T(8,128)(2,1)S(1)}, bf16[2,144,128]{2,1,0:T(8,128)(2,1)S(1)}, u32[]{:S(2)}, u32[]{:S(2)}) collective-permute-start(bf16[2,144,128]{2,1,0:T(8,128)(2,1)S(1)} %get-tuple-element.86), channel_id=1, source_target_pairs={{0,130},{1,138},{2,128},{3,136},{8,131},{9,139},{10,129},{11,137},... | collective-permute-start | bytes 221192 | tf_op jit(solution)/shard_map/ppermute | solution.py:751

commit v7 on v6

--- a/solution.py
+++ b/solution.py
@@ -279,7 +279,7 @@
 
 
 def generator_kernel(place_ref, own_ref, other_ref, embed_ref, mods_ref, final_ref, own_w_ref, other_w_ref,
-                     part_ref, shaped_ref, pre_ref, res_ref, w_ref, gram_ref, mean_ref, sum_ref):
+                     part_ref, shaped_ref, pre_ref, res_ref, w_ref, gram_ref, mean_ref, sum_ref, all_ref, x_ref):
     i = pl.program_id(0)
     v = place_ref[0]
 
@@ -291,22 +291,26 @@
 
     x = jnp.concatenate(in_order(v, own_ref[:, :C], other_ref[:, :C]), axis=0)
 
+    x_ref[i] = x
+    tokens = pl.ds(pl.multiple_of(i * TOKENS, TOKENS), TOKENS)
+
     def store(cut, shaped):
         shaped_ref[0, :, cut] = shaped
-
-    shape_tokens(x, embed_ref, mods_ref, 0, gram_ref, mean_ref, store)
-    pre = dot(shaped_ref[0], w_ref[...])
-    res, partial, total, square = finish(pre, x, embed_ref, mods_ref, 0, final_ref, place_ref)
-    pre_ref[0] = pre
-    res_ref[0] = res
-    pieces = owned(partial)
-    pieces = jnp.concatenate([pieces[:, :8], pieces[:, 8:]], axis=2)
-    rows = row_pieces([owned(total), owned(square)], 32)
-    sum_ref[:, pl.ds(pl.multiple_of(i * 8, 8), 8), :] = pieces
-    sum_ref[:, pl.ds(24 + i, 1), :] = rows[0]
+        all_ref[tokens, cut] = shaped
+
+    shape_tokens(x, embed_ref, mods_ref, i, gram_ref, mean_ref, store)
 
     @pl.when(i == IMAGES - 1)
     def _():
+        every = dot(all_ref[...], w_ref[...])
+        for n in range(IMAGES):
+            pre = every[n * TOKENS : (n + 1) * TOKENS]
+            res, partial, total, square = finish(pre, x_ref[n], embed_ref, mods_ref, n, final_ref, place_ref)
+            pre_ref[n] = pre
+            res_ref[n] = res
+            pieces = owned(partial)
+            sum_ref[:, 8 * n : 8 * n + 8, :] = jnp.concatenate([pieces[:, :8], pieces[:, 8:]], axis=2)
+            sum_ref[:, 24 + n : 25 + n, :] = row_pieces([owned(total), owned(square)], 32)[0]
         part_ref[...] = sum_ref[...].astype(BF16)
 
 
@@ -569,9 +573,6 @@
       gen_modulation.T, teacher_modulation.T, fake_modulation.T)
     mine = lax.ppermute(mine, PLACES, SWAP)
     other = lax.ppermute(other, PLACES, SWAP_TURNED)
-    mine, other, noise = lax.optimization_barrier((mine, other, noise))
-    own_noise = lax.ppermute(noise, PLACES, NEAR)
-    other_noise = lax.ppermute(noise, PLACES, NEAR_TURNED)
 
     def pack(kernel, rows):
         return pl.pallas_call(
@@ -586,9 +587,10 @@
 
     g_packed = pack(pack_kernel, GEN_CHUNK)
     g_packed = exchange(g_packed, GATHER)
-    mine, other, own_noise, other_noise = lax.optimization_barrier((mine, other, own_noise, other_noise))
+    g_packed, mine, other, noise = lax.optimization_barrier((g_packed, mine, other, noise))
+    own_noise = lax.ppermute(noise, PLACES, NEAR)
+    other_noise = lax.ppermute(noise, PLACES, NEAR_TURNED)
     packed = pack(pack_score_kernel, SCORE_ROWS)
-    g_packed, own_noise, other_noise = lax.optimization_barrier((g_packed, own_noise, other_noise))
     g_other = lax.ppermute(g_packed, "s", SIBLING)
     packed, g_packed, g_other = lax.optimization_barrier((packed, g_packed, g_other))
     packed = exchange(packed, GATHER)
@@ -599,6 +601,7 @@
 
     by_image = lambda *shape: pl.BlockSpec((1, *shape), lambda i: (i,) + (0,) * len(shape))
     noise_rows = pl.BlockSpec((HALF, 128), lambda i: (i, 0))
+    net_mods = lambda net: pl.BlockSpec((IMAGES, 8, D), lambda *_: (net, 0, 0))
     mods_of = lambda net: pl.BlockSpec((1, 8, D), lambda i: (3 * net + i, 0, 0))
     local = pltpu.HBM((IMAGES, TOKENS, COLS), F32)
     wide = pltpu.HBM((IMAGES, TOKENS, D), BF16)
@@ -619,21 +622,21 @@
         generator_kernel,
         grid=(IMAGES,),
         in_specs=[
-            smem(), noise_rows, noise_rows, whole((C, D)), mods_of(0), whole((C, D)),
+            smem(), noise_rows, noise_rows, whole((C, D)), net_mods(0), whole((C, D)),
             *([whole((CHUNKS, GEN_CHUNK, 128))] * 2),
         ],
-        out_specs=[whole((OWNERS, 32, 128)), by_image(TOKENS, D), by_image(TOKENS, COLS), by_image(TOKENS, COLS)],
+        out_specs=[whole((OWNERS, 32, 128)), by_image(TOKENS, D), *([whole((IMAGES, TOKENS, COLS))] * 2)],
         out_shape=[jax.ShapeDtypeStruct((OWNERS, 32, 128), BF16), wide, local, local],
         scratch_shapes=[pltpu.VMEM((D, COLS), BF16), pltpu.VMEM((C, 3 * C), BF16), pltpu.VMEM((C, 128), F32),
-                        pltpu.VMEM((OWNERS, 32, 128), F32)],
-        compiler_params=params(16),
+                        pltpu.VMEM((OWNERS, 32, 128), F32), pltpu.VMEM((IMAGES * TOKENS, D), BF16),
+                        pltpu.VMEM((IMAGES, TOKENS, C), BF16)],
+        compiler_params=params(24),
         cost_estimate=pl.CostEstimate(flops=12 * 10**9, bytes_accessed=30 * 10**6, transcendentals=0),
         name="generator",
     )(place, own_noise, other_noise, gen_embed, mods, gen_final, g_packed, g_other)
     packed, part = lax.optimization_barrier((packed, part))
     part = exchange(part, COMBINE)
 
-    net_mods = lambda net: pl.BlockSpec((IMAGES, 8, D), lambda *_: (net, 0, 0))
     pack1, keep = pl.pallas_call(
         samples_kernel,
         grid=(1,),

time: 198 us -> 199 us (level)
  blocking collectives: 37.4 us -> 53.5 us
  waiting for transfers between devices: 52.1 us -> 40 us
  starting transfers between devices: 51.6 us -> 48.9 us
    all_to_all x3 -> x4, blocking collectives: 37.4 us -> 53.5 us  [exchange(): return lax.all_to_all(value, axes, 0, 0)]
    all_to_all x5 -> x4, waiting for transfers between devices: 31.2 us -> 23.7 us  [exchange(): return lax.all_to_all(value, axes, 0, 0)]
    all_to_all x5 -> x4, starting transfers between devices: 30.4 us -> 25.3 us  [exchange(): return lax.all_to_all(value, axes, 0, 0)]
    ppermute x1, waiting for transfers between devices: 3.57 us -> 0.01 us  [shards(): other_noise = lax.ppermute(noise, PLACES, NEAR_TURNED)]
    ppermute x1, starting transfers between devices: 1.37 us -> 4.69 us  [shards(): other_noise = lax.ppermute(noise, PLACES, NEAR_TURNED)]
  transfers between devices with their start and end apart: 16 -> 15, of which waited for: 13 -> 8; matrix products, arithmetic and copies ran while one was open for 2% -> 2% of each run, Pallas kernels for 12% -> 12%
where the time goes in v7:
time: 199 us; the launch traced here: 198 us
  blocking collectives  53.5 us (27%)
  starting transfers between devices  48.9 us (25%)
  Pallas kernels  46.4 us (23%)
  waiting for transfers between devices  40 us (20%)
  other arithmetic  4.92 us (2%)
  local copies, waits for them, and re-layouts  3.72 us (2%)
    all_to_all x4, blocking collectives, exchange(): return lax.all_to_all(value, axes, 0, 0)  53.5 us
    all_to_all x4, starting transfers between devices, exchange(): return lax.all_to_all(value, axes, 0, 0)  25.3 us
    all_to_all x4, waiting for transfers between devices, exchange(): return lax.all_to_all(value, axes, 0, 0)  23.7 us
    pallas_call x1, Pallas kernels, shards(): pl.pallas_call(score_kernel, grid=(IMAGES,), in_specs=[smem(), smem(), wh...  12.2 us
    pallas_call x2, Pallas kernels, gradient(): pl.pallas_call(functools.partial(gradient_kernel, net), grid=(4,), in_spe...  12.2 us
    pallas_call x1, Pallas kernels, shards(): pl.pallas_call(generator_kernel, grid=(IMAGES,), in_specs=[smem(), noise_...  8.84 us
    ppermute x1, starting transfers between devices, shards(): mine = lax.ppermute(mine, PLACES, SWAP)  7.41 us
    ppermute x1, waiting for transfers between devices, shards(): other = lax.ppermute(other, PLACES, SWAP_TURNED)  6.28 us
  transfers between devices with their start and end apart: 15, of which 8 were waited for; matrix products, arithmetic and copies ran while one was open for 2% of the time, Pallas kernels for 12%

profile of v7, /device:TPU:1, one launch (start us, length us, event | category | flops | bytes accessed | tf_op | source)
XLA Modules:
  0.0 198.2 jit_solution(1339384107861262009)
XLA Ops:
  0.7 0.8 broadcast_multiply_fusion
  1.4 0.1 multiply_cosine_fusion
  1.5 0.6 multiply_convert_fusion.cond_ref
  2.1 0.6 stack.32.place_ref
  2.8 2.4 %split.1 = (bf16[528,128]{1,0:T(8,128)(2,1)}, bf16[528,128]{1,0:T(8,128)(2,1)}, bf16[384,128]{1,0:T(8,128)(2,1)}) custom-call(s32[5]{0:T(128)} %stack.32.place_ref, bf16[6,256]{1,0:T(8,128)(2,1)} %multiply_convert_fusion.cond_ref, bf16[3,64,128]{2,1,0:T(8,128)(2,1)} %bitcast.34, bf16[3,64,128]{2,1,0:T(8,128)(2,1)} %bitcast.35, bf16[96,384]{1,0:T(8,128)(2,1)} %gen_ref.1, ...), custom_call_target="tpu_custom_call" | custom-call | tf_op jit(solution)/shard_map/split/pallas_call | solution.py:563
  5.1 7.4 %collective-permute-start = (bf16[528,128]{1,0:T(8,128)(2,1)}, bf16[528,128]{1,0:T(8,128)(2,1)S(1)}, u32[]{:S(2)}, u32[]{:S(2)}) collective-permute-start(bf16[528,128]{1,0:T(8,128)(2,1)} %get-tuple-element.40), channel_id=1, source_target_pairs={{0,128},{1,136},{2,130},{3,138},{8,129},{9,137},{10,131},{11,139},... | collective-permute-start | bytes 405512 | tf_op jit(solution)/shard_map/ppermute | solution.py:574
  12.5 1.1 collective-permute-start.1
  13.6 2.5 %collective-permute-done.mine_ref = bf16[528,128]{1,0:T(8,128)(2,1)S(1)} collective-permute-done((bf16[528,128]{1,0:T(8,128)(2,1)}, bf16[528,128]{1,0:T(8,128)(2,1)S(1)}, u32[]{:S(2)}, u32[]{:S(2)}) %collective-permute-start) | collective-permute-done | bytes 135200 | tf_op jit(solution)/shard_map/ppermute | solution.py:574
  16.1 6.3 %collective-permute-done.1.other_ref = bf16[528,128]{1,0:T(8,128)(2,1)S(1)} collective-permute-done((bf16[528,128]{1,0:T(8,128)(2,1)}, bf16[528,128]{1,0:T(8,128)(2,1)S(1)}, u32[]{:S(2)}, u32[]{:S(2)}) %collective-permute-start.1) | collective-permute-done | bytes 135200 | tf_op jit(solution)/shard_map/ppermute | solution.py:575
  22.4 0.6 copy-done
  23.0 0.7 pack.2
  23.7 16.1 %all_to_all.40.own_w_ref = bf16[8,368,128]{2,1,0:T(8,128)(2,1)S(1)} all-to-all(bf16[8,368,128]{2,1,0:T(8,128)(2,1)S(1)} %pack.2), channel_id=1, replica_groups=mesh['g'=4,'x'=4,'h'=2,'w'=2,'v'=2,'s'=2] {'x','w'}, dimensions={0} | all-to-all | bytes 1507328 | tf_op jit(solution)/shard_map/all_to_all | solution.py:533
  39.8 0.0 collective-permute-start.2
  39.8 4.7 %collective-permute-start.4 = (bf16[384,128]{1,0:T(8,128)(2,1)S(1)}, bf16[384,128]{1,0:T(8,128)(2,1)S(1)}, u32[]{:S(2)}, u32[]{:S(2)}) collective-permute-start(bf16[384,128]{1,0:T(8,128)(2,1)S(1)} %copy-done.2), channel_id=1, source_target_pairs={{0,2},{1,202},{2,0},{3,200},{8,195},{9,11},{10,193},{11,9},{64,66}... | collective-permute-start | bytes 294920 | tf_op jit(solution)/shard_map/ppermute | solution.py:592
  44.5 2.8 %collective-permute-start.3 = (bf16[384,128]{1,0:T(8,128)(2,1)S(1)}, bf16[384,128]{1,0:T(8,128)(2,1)S(1)}, u32[]{:S(2)}, u32[]{:S(2)}) collective-permute-start(bf16[384,128]{1,0:T(8,128)(2,1)S(1)} %copy-done.2), channel_id=1, source_target_pairs={{0,0},{1,200},{2,2},{3,202},{8,193},{9,9},{10,195},{11,11},{64,64}... | collective-permute-start | bytes 294920 | tf_op jit(solution)/shard_map/ppermute | solution.py:591
  47.3 1.8 pack.3
  49.1 0.0 collective-permute-done.2.other_w_ref
  49.1 3.6 %all-to-all-start.1 = ((bf16[8,576,128]{2,1,0:T(8,128)(2,1)}), bf16[8,576,128]{2,1,0:T(8,128)(2,1)S(1)}, u32[]{:S(2)}, u32[]{:S(2)}) async-start(bf16[8,576,128]{2,1,0:T(8,128)(2,1)} %pack.3), calls=%async_computation.1 | async-start | bytes 2359296 | tf_op jit(solution)/shard_map/all_to_all | solution.py:533
  52.6 0.9 broadcast_select_fusion.1
  53.7 0.4 maximum_bitcast_fusion
  54.1 0.1 copy.24
  54.2 0.1 reshape.43
  54.3 1.4 convert_element_type.25
  55.7 1.1 pad_convert_fusion.mods_ref.t_mods_ref.f_mods_ref.refs_0_.refs_1_
  56.8 0.0 collective-permute-done.4.other_ref
  56.9 0.0 collective-permute-done.3.own_ref.noise_ref
  56.9 8.8 %generator.1 = (bf16[16,32,128]{2,1,0:T(8,128)(2,1)}, bf16[3,256,3072]{2,1,0:T(8,128)(2,1)}, f32[3,256,192]{2,1,0:T(8,128)}, f32[3,256,192]{2,1,0:T(8,128)}) custom-call(s32[5]{0:T(128)S(1)} %copy-done.1, bf16[384,128]{1,0:T(8,128)(2,1)S(1)} %collective-permute-done.3.own_ref.noise_ref, bf16[384,128]{1,0:T(8,128)(2,1)S(1)} %collective-permute-done.4.other_ref, ...), custom_call_target="tpu_custom_call" | custom-call | flops 12000000000 | bytes 30000000 | tf_op jit(solution)/shard_map/generator/pallas_call | solution.py:621
  65.7 0.0 all-to-all-done.1.own_w_ref
  65.7 6.1 %all-to-all-start.2 = ((bf16[16,32,128]{2,1,0:T(8,128)(2,1)}), bf16[16,32,128]{2,1,0:T(8,128)(2,1)S(1)}, u32[]{:S(2)}, u32[]{:S(2)}) async-start(bf16[16,32,128]{2,1,0:T(8,128)(2,1)} %get-tuple-element.52), calls=%async_computation.2 | async-start | bytes 262144 | tf_op jit(solution)/shard_map/all_to_all | solution.py:533
  71.8 0.1 fusion.2
  71.9 1.8 sums.1.sums_ref
  73.6 5.7 %all-to-all-done.2.got_ref = bf16[16,32,128]{2,1,0:T(8,128)(2,1)S(1)} async-done(((bf16[16,32,128]{2,1,0:T(8,128)(2,1)}), bf16[16,32,128]{2,1,0:T(8,128)(2,1)S(1)}, u32[]{:S(2)}, u32[]{:S(2)}) %all-to-all-start.2) | async-done | bytes 131104 | tf_op jit(solution)/shard_map/all_to_all | solution.py:533
  79.3 1.2 samples.1
  80.5 2.2 %collective-permute-start.5 = (bf16[8,576,128]{2,1,0:T(8,128)(2,1)S(1)}, bf16[8,576,128]{2,1,0:T(8,128)(2,1)S(1)}, u32[]{:S(2)}, u32[]{:S(2)}) collective-permute-start(bf16[8,576,128]{2,1,0:T(8,128)(2,1)S(1)} %all-to-all-done.1.own_w_ref), channel_id=1, source_target_pairs={{0,1},{1,0},{2,3},{3,2},{4,5},{5,4},{6,7},{7,6},{8,9},{9,8},{10,11... | collective-permute-start | bytes 3538952 | tf_op jit(solution)/shard_map/ppermute | solution.py:656
  82.6 10.5 %all_to_all.41.got_ref = f32[16,24,128]{2,1,0:T(8,128)S(1)} all-to-all(f32[16,24,128]{2,1,0:T(8,128)S(1)} %get-tuple-element.54), channel_id=1, replica_groups=mesh['g'=4,'x'=4,'h'=2,'w'=2,'v'=2,'s'=2] {'v','h','g'}, dimensions={0} | all-to-all | bytes 393216 | tf_op jit(solution)/shard_map/all_to_all | solution.py:533
  93.1 0.0 collective-permute-done.5.other_w_ref
  93.1 12.2 %score.1 = (bf16[16,64,128]{2,1,0:T(8,128)(2,1)S(1)}, f32[3,64,128]{2,1,0:T(8,128)S(1)}, bf16[3,256,3072]{2,1,0:T(8,128)(2,1)}, f32[3,256,192]{2,1,0:T(8,128)}, f32[3,256,192]{2,1,0:T(8,128)}) custom-call(s32[5]{0:T(128)S(1)} %copy-done.1, f32[3]{0:T(128)S(1)} %get-tuple-element.84.time_ref, f32[16,24,128]{2,1,0:T(8,128)S(1)} %all_to_all.41.got_ref, ...), custom_call_target="tpu_custom_call" | custom-call | flops 24000000000 | bytes 50000000 | tf_op jit(solution)/shard_map/score/pallas_call | solution.py:658
  105.3 13.1 %all_to_all.42.got_ref = bf16[16,64,128]{2,1,0:T(8,128)(2,1)S(1)} all-to-all(bf16[16,64,128]{2,1,0:T(8,128)(2,1)S(1)} %get-tuple-element.57), channel_id=1, replica_groups=mesh['g'=4,'x'=4,'h'=2,'w'=2,'v'=2,'s'=2] {'v','h','g'}, dimensions={0} | all-to-all | bytes 524288 | tf_op jit(solution)/shard_map/all_to_all | solution.py:533
  118.4 2.1 %cotangents.1 = bf16[16,64,128]{2,1,0:T(8,128)(2,1)S(1)} custom-call(s32[5]{0:T(128)S(1)} %copy-done.1, f32[3]{0:T(128)S(1)} %get-tuple-element.83.time_ref.gen_time_ref, f32[3]{0:T(128)S(1)} %get-tuple-element.84.time_ref, bf16[16,64,128]{2,1,0:T(8,128)(2,1)S(1)} %all_to_all.42.got_ref, bf16[384,128]{1,0:T(8,128)(2,1)S(1)} %collective-permute-done.3.own_ref.noise_ref, ...), custom_call_target="tpu_custom_call" | custom-call | tf_op jit(solution)/shard_map/cotangents/pallas_call | solution.py:688
  120.5 13.9 %all_to_all.43.got_ref = bf16[16,64,128]{2,1,0:T(8,128)(2,1)S(1)} all-to-all(bf16[16,64,128]{2,1,0:T(8,128)(2,1)S(1)} %cotangents.1), channel_id=1, replica_groups=mesh['g'=4,'x'=4,'h'=2,'w'=2,'v'=2,'s'=2] {'v','h','g'}, dimensions={0} | all-to-all | bytes 524288 | tf_op jit(solution)/shard_map/all_to_all | solution.py:533
  134.4 0.2 convert_reduce_fusion
  134.5 0.1 reduce_sum.14
  134.6 0.1 reduce_sum.18
  134.8 0.6 broadcast_in_dim.2
  135.4 9.7 %all-to-all-start.6 = ((f32[16,1,128]{2,1,0:T(1,128)}), f32[16,1,128]{2,1,0:T(1,128)S(1)}, u32[]{:S(2)}, u32[]{:S(2)}) async-start(f32[16,1,128]{2,1,0:T(1,128)} %broadcast_in_dim.2), calls=%async_computation.6 | async-start | bytes 16384 | tf_op jit(solution)/shard_map/all_to_all | solution.py:533
  145.1 0.2 collective-permute-start.6
  145.2 6.0 %gradient.2 = (bf16[8,288,128]{2,1,0:T(8,128)(2,1)S(1)}, bf16[8,288,128]{2,1,0:T(8,128)(2,1)S(1)}) custom-call(s32[5]{0:T(128)S(1)} %copy-done.1, bf16[16,64,128]{2,1,0:T(8,128)(2,1)S(1)} %all_to_all.43.got_ref, f32[9,8,3072]{2,1,0:T(8,128)S(1)} %pad_convert_fusion.mods_ref.t_mods_ref.f_mods_ref.refs_0_.refs_1_, bf16[64,3072]{1,0:T(8,128)(2,1)} %bitcast.27, ...), custom_call_target="tpu_custom_call" | custom-call | flops 7000000000 | bytes 20000000 | tf_op jit(solution)/shard_map/gradient/pallas_call | solution.py:716
  151.3 0.4 collective-permute-start.7
  151.7 0.3 all-to-all-done.6.refs_0_
  152.0 0.0 collective-permute-done.6
  152.0 6.1 %gradient.3 = (bf16[8,288,128]{2,1,0:T(8,128)(2,1)S(1)}, bf16[8,288,128]{2,1,0:T(8,128)(2,1)S(1)}) custom-call(s32[5]{0:T(128)S(1)} %copy-done.1, bf16[16,64,128]{2,1,0:T(8,128)(2,1)S(1)} %all_to_all.43.got_ref, f32[16,1,128]{2,1,0:T(1,128)S(1)} %all-to-all-done.6.refs_0_, f32[9,8,3072]{2,1,0:T(8,128)S(1)} %pad_convert_fusion.mods_ref.t_mods_ref.f_mods_ref.refs_0_.refs_1_, ...), custom_call_target="tpu_custom_call" | custom-call | flops 7000000000 | bytes 20000000 | tf_op jit(solution)/shard_map/gradient/pallas_call | solution.py:716
  158.1 0.8 collective-permute-start.8
  158.9 0.0 collective-permute-done.7.f_got_ref
  158.9 1.6 collective-permute-done.8.g_got_ref
  160.5 1.3 add.46
  161.8 6.0 %all-to-all-start.7 = ((bf16[8,576,128]{2,1,0:T(8,128)(2,1)}), bf16[8,576,128]{2,1,0:T(8,128)(2,1)S(1)}, u32[]{:S(2)}, u32[]{:S(2)}) async-start(bf16[8,576,128]{2,1,0:T(8,128)(2,1)} %add.46), calls=%async_computation.7 | async-start | bytes 2359296 | tf_op jit(solution)/shard_map/all_to_all | solution.py:533
  167.8 17.7 %all-to-all-done.7.got_ref = bf16[8,576,128]{2,1,0:T(8,128)(2,1)S(1)} async-done(((bf16[8,576,128]{2,1,0:T(8,128)(2,1)}), bf16[8,576,128]{2,1,0:T(8,128)(2,1)S(1)}, u32[]{:S(2)}, u32[]{:S(2)}) %all-to-all-start.7) | async-done | bytes 1179680 | tf_op jit(solution)/shard_map/all_to_all | solution.py:533
  185.6 0.7 sum.1
  186.3 3.5 %collective-permute-start.9 = (bf16[2,144,128]{2,1,0:T(8,128)(2,1)S(1)}, bf16[2,144,128]{2,1,0:T(8,128)(2,1)S(1)}, u32[]{:S(2)}, u32[]{:S(2)}) collective-permute-start(bf16[2,144,128]{2,1,0:T(8,128)(2,1)S(1)} %get-tuple-element.73), channel_id=1, source_target_pairs={{0,128},{1,136},{2,130},{3,138},{8,129},{9,137},{10,131},{11,139},... | collective-permute-start | bytes 221192 | tf_op jit(solution)/shard_map/ppermute | solution.py:753
  189.8 0.5 collective-permute-start.10
  190.3 0.7 select_bitcast_fusion
  191.0 1.4 collective-permute-done.9.keep_ref
  192.4 4.5 %collective-permute-done.10.other_ref = bf16[2,144,128]{2,1,0:T(8,128)(2,1)S(1)} collective-permute-done((bf16[2,144,128]{2,1,0:T(8,128)(2,1)S(1)}, bf16[2,144,128]{2,1,0:T(8,128)(2,1)S(1)}, u32[]{:S(2)}, u32[]{:S(2)}) %collective-permute-start.10) | collective-permute-done | bytes 73760 | tf_op jit(solution)/shard_map/ppermute | solution.py:754
  196.9 1.3 place.1
  (10 shorter events, 0.1 us)
Async XLA Ops:
  5.1 11.0 %collective-permute-start = (bf16[528,128]{1,0:T(8,128)(2,1)}, bf16[528,128]{1,0:T(8,128)(2,1)S(1)}, u32[]{:S(2)}, u32[]{:S(2)}) collective-permute-start(bf16[528,128]{1,0:T(8,128)(2,1)} %get-tuple-element.40), channel_id=1, source_target_pairs={{0,128},{1,136},{2,130},{3,138},{8,129},{9,137},{10,131},{11,139},... | collective-permute-start | bytes 405512 | tf_op jit(solution)/shard_map/ppermute | solution.py:574
  12.5 34.8 %copy-start.1 = (s32[5]{0:T(128)S(1)}, s32[5]{0:T(128)}, u32[]{:S(2)}) copy-start(s32[5]{0:T(128)} %stack.32.place_ref) | copy-start | bytes 64
  12.5 9.9 %collective-permute-start.1 = (bf16[528,128]{1,0:T(8,128)(2,1)}, bf16[528,128]{1,0:T(8,128)(2,1)S(1)}, u32[]{:S(2)}, u32[]{:S(2)}) collective-permute-start(bf16[528,128]{1,0:T(8,128)(2,1)} %get-tuple-element.41), channel_id=1, source_target_pairs={{0,130},{1,138},{2,128},{3,136},{8,131},{9,139},{10,129},{11,137},... | collective-permute-start | bytes 405512 | tf_op jit(solution)/shard_map/ppermute | solution.py:575
  22.4 0.6 copy-start
  23.0 16.8 %copy-start.2 = (bf16[384,128]{1,0:T(8,128)(2,1)S(1)}, bf16[384,128]{1,0:T(8,128)(2,1)}, u32[]{:S(2)}) copy-start(bf16[384,128]{1,0:T(8,128)(2,1)} %get-tuple-element.47) | copy-start | bytes 294916
  39.8 9.3 %collective-permute-start.2 = (bf16[8,368,128]{2,1,0:T(8,128)(2,1)S(1)}, bf16[8,368,128]{2,1,0:T(8,128)(2,1)}, u32[]{:S(2)}, u32[]{:S(2)}) collective-permute-start(bf16[8,368,128]{2,1,0:T(8,128)(2,1)S(1)} %all_to_all.40.own_w_ref), channel_id=1, source_target_pairs={{0,1},{1,0},{2,3},{3,2},{4,5},{5,4},{6,7},{7,6},{8,9},{9,8},{10,11... | collective-permute-start | bytes 2261000 | tf_op jit(solution)/shard_map/ppermute | solution.py:594
  39.8 17.0 %collective-permute-start.4 = (bf16[384,128]{1,0:T(8,128)(2,1)S(1)}, bf16[384,128]{1,0:T(8,128)(2,1)S(1)}, u32[]{:S(2)}, u32[]{:S(2)}) collective-permute-start(bf16[384,128]{1,0:T(8,128)(2,1)S(1)} %copy-done.2), channel_id=1, source_target_pairs={{0,2},{1,202},{2,0},{3,200},{8,195},{9,11},{10,193},{11,9},{64,66}... | collective-permute-start | bytes 294920 | tf_op jit(solution)/shard_map/ppermute | solution.py:592
  44.5 12.4 %collective-permute-start.3 = (bf16[384,128]{1,0:T(8,128)(2,1)S(1)}, bf16[384,128]{1,0:T(8,128)(2,1)S(1)}, u32[]{:S(2)}, u32[]{:S(2)}) collective-permute-start(bf16[384,128]{1,0:T(8,128)(2,1)S(1)} %copy-done.2), channel_id=1, source_target_pairs={{0,0},{1,200},{2,2},{3,202},{8,193},{9,9},{10,195},{11,11},{64,64}... | collective-permute-start | bytes 294920 | tf_op jit(solution)/shard_map/ppermute | solution.py:591
  49.1 16.6 %all-to-all-start.1 = ((bf16[8,576,128]{2,1,0:T(8,128)(2,1)}), bf16[8,576,128]{2,1,0:T(8,128)(2,1)S(1)}, u32[]{:S(2)}, u32[]{:S(2)}) async-start(bf16[8,576,128]{2,1,0:T(8,128)(2,1)} %pack.3), calls=%async_computation.1 | async-start | bytes 2359296 | tf_op jit(solution)/shard_map/all_to_all | solution.py:533
  65.7 13.6 %all-to-all-start.2 = ((bf16[16,32,128]{2,1,0:T(8,128)(2,1)}), bf16[16,32,128]{2,1,0:T(8,128)(2,1)S(1)}, u32[]{:S(2)}, u32[]{:S(2)}) async-start(bf16[16,32,128]{2,1,0:T(8,128)(2,1)} %get-tuple-element.52), calls=%async_computation.2 | async-start | bytes 262144 | tf_op jit(solution)/shard_map/all_to_all | solution.py:533
  80.5 12.6 %collective-permute-start.5 = (bf16[8,576,128]{2,1,0:T(8,128)(2,1)S(1)}, bf16[8,576,128]{2,1,0:T(8,128)(2,1)S(1)}, u32[]{:S(2)}, u32[]{:S(2)}) collective-permute-start(bf16[8,576,128]{2,1,0:T(8,128)(2,1)S(1)} %all-to-all-done.1.own_w_ref), channel_id=1, source_target_pairs={{0,1},{1,0},{2,3},{3,2},{4,5},{5,4},{6,7},{7,6},{8,9},{9,8},{10,11... | collective-permute-start | bytes 3538952 | tf_op jit(solution)/shard_map/ppermute | solution.py:656
  135.4 16.6 %all-to-all-start.6 = ((f32[16,1,128]{2,1,0:T(1,128)}), f32[16,1,128]{2,1,0:T(1,128)S(1)}, u32[]{:S(2)}, u32[]{:S(2)}) async-start(f32[16,1,128]{2,1,0:T(1,128)} %broadcast_in_dim.2), calls=%async_computation.6 | async-start | bytes 16384 | tf_op jit(solution)/shard_map/all_to_all | solution.py:533
  145.1 6.9 %collective-permute-start.6 = (f32[3,64,128]{2,1,0:T(8,128)S(1)}, f32[3,64,128]{2,1,0:T(8,128)S(1)}, u32[]{:S(2)}, u32[]{:S(2)}) collective-permute-start(f32[3,64,128]{2,1,0:T(8,128)S(1)} %get-tuple-element.59), channel_id=1, source_target_pairs={{0,1},{1,0},{2,3},{3,2},{4,5},{5,4},{6,7},{7,6},{8,9},{9,8},{10,11... | collective-permute-start | bytes 294920 | tf_op jit(solution)/shard_map/ppermute | solution.py:703
  151.3 7.6 %collective-permute-start.7 = (bf16[8,288,128]{2,1,0:T(8,128)(2,1)S(1)}, bf16[8,288,128]{2,1,0:T(8,128)(2,1)S(1)}, u32[]{:S(2)}, u32[]{:S(2)}) collective-permute-start(bf16[8,288,128]{2,1,0:T(8,128)(2,1)S(1)} %get-tuple-element.66), channel_id=1, source_target_pairs={{0,1},{1,0},{2,3},{3,2},{4,5},{5,4},{6,7},{7,6},{8,9},{9,8},{10,11... | collective-permute-start | bytes 1769480 | tf_op jit(solution)/shard_map/ppermute | solution.py:730
  158.1 2.4 %collective-permute-start.8 = (bf16[8,288,128]{2,1,0:T(8,128)(2,1)S(1)}, bf16[8,288,128]{2,1,0:T(8,128)(2,1)S(1)}, u32[]{:S(2)}, u32[]{:S(2)}) collective-permute-start(bf16[8,288,128]{2,1,0:T(8,128)(2,1)S(1)} %get-tuple-element.72), channel_id=1, source_target_pairs={{0,1},{1,0},{2,3},{3,2},{4,5},{5,4},{6,7},{7,6},{8,9},{9,8},{10,11... | collective-permute-start | bytes 1769480 | tf_op jit(solution)/shard_map/ppermute | solution.py:730
  161.8 23.7 %all-to-all-start.7 = ((bf16[8,576,128]{2,1,0:T(8,128)(2,1)}), bf16[8,576,128]{2,1,0:T(8,128)(2,1)S(1)}, u32[]{:S(2)}, u32[]{:S(2)}) async-start(bf16[8,576,128]{2,1,0:T(8,128)(2,1)} %add.46), calls=%async_computation.7 | async-start | bytes 2359296 | tf_op jit(solution)/shard_map/all_to_all | solution.py:533
  186.3 6.1 %collective-permute-start.9 = (bf16[2,144,128]{2,1,0:T(8,128)(2,1)S(1)}, bf16[2,144,128]{2,1,0:T(8,128)(2,1)S(1)}, u32[]{:S(2)}, u32[]{:S(2)}) collective-permute-start(bf16[2,144,128]{2,1,0:T(8,128)(2,1)S(1)} %get-tuple-element.73), channel_id=1, source_target_pairs={{0,128},{1,136},{2,130},{3,138},{8,129},{9,137},{10,131},{11,139},... | collective-permute-start | bytes 221192 | tf_op jit(solution)/shard_map/ppermute | solution.py:753
  189.8 7.1 %collective-permute-start.10 = (bf16[2,144,128]{2,1,0:T(8,128)(2,1)S(1)}, bf16[2,144,128]{2,1,0:T(8,128)(2,1)S(1)}, u32[]{:S(2)}, u32[]{:S(2)}) collective-permute-start(bf16[2,144,128]{2,1,0:T(8,128)(2,1)S(1)} %get-tuple-element.74), channel_id=1, source_target_pairs={{0,130},{1,138},{2,128},{3,136},{8,131},{9,139},{10,129},{11,137},... | collective-permute-start | bytes 221192 | tf_op jit(solution)/shard_map/ppermute | solution.py:754

commit v8 on v6

--- a/solution.py
+++ b/solution.py
@@ -41,6 +41,7 @@
 GEN_CHUNK = 368
 SCORE_ROWS = 576
 CHUNKS = 8
+OFFSETS = [(2, 1), (1, 1), (3, 1), (2, 0), (1, 0), (3, 0), (0, 1), (0, 0)]
 BLOCK = 512
 
 PLACES = ("g", "h", "v", "s")
@@ -466,9 +467,8 @@
             res_grad = inverse * (out_grad * (1.0 + scale)) - slope * res_ref[i] + offset
             act_grad = res_grad * gate
             if net == 1:
-                lane = lax.broadcasted_iota(jnp.int32, gaps.shape, 1)
-                total = jnp.sum(jnp.where(lane == i, gaps, 0.0), axis=1, keepdims=True)
-                act_grad = act_grad * (1.0 / (total / (S * C) + gap_epsilon))
+                inverse_gap = 1.0 / (gaps[i : i + 1, :] / (S * C) + gap_epsilon)
+                act_grad = act_grad * jnp.concatenate([inverse_gap, inverse_gap[:, :NARROW]], axis=1)
             grad = act_grad * gelu_slope(pre_ref[i])
             turned = jnp.concatenate([grad, jnp.zeros((TOKENS, NARROW), F32)], axis=1).T
             left_ref[:, i * TOKENS : (i + 1) * TOKENS] = turned[:COLS].astype(BF16)
@@ -489,20 +489,22 @@
             send_ref[w, n * ROWS : (n + 1) * ROWS, :] = jnp.where(first, high, low)
 
 
-def add_kernel(f_keep_ref, f_got_ref, g_keep_ref, g_got_ref, out_ref):
-    for n, (keep_ref, got_ref) in enumerate(((f_keep_ref, f_got_ref), (g_keep_ref, g_got_ref))):
-        for k in range(CHUNKS):
-            total = keep_ref[k].astype(F32) + got_ref[k].astype(F32)
-            out_ref[k, n * GEN_ROWS : (n + 1) * GEN_ROWS] = total.astype(BF16)
-
-
-def sum_kernel(place_ref, got_ref, keep_ref, send_ref):
+def add_kernel(place_ref, f_keep_ref, f_got_ref, g_keep_ref, g_got_ref, *out_refs):
+    for (dx, dw), out_ref in zip(OFFSETS, out_refs, strict=True):
+        at = lax.rem(place_ref[5] + dx, 4) * 2 + lax.rem(place_ref[6] + dw, 2)
+        for n, (keep_ref, got_ref) in enumerate(((f_keep_ref, f_got_ref), (g_keep_ref, g_got_ref))):
+            total = keep_ref[at].astype(F32) + got_ref[at].astype(F32)
+            out_ref[n * GEN_ROWS : (n + 1) * GEN_ROWS] = total.astype(BF16)
+
+
+def sum_kernel(place_ref, *refs):
+    got_refs, (keep_ref, send_ref) = refs[:CHUNKS], refs[CHUNKS:]
     v = place_ref[0]
     for n in range(2):
         rows = slice(n * GEN_ROWS, (n + 1) * GEN_ROWS)
-        total = got_ref[0, rows].astype(F32)
-        for k in range(1, CHUNKS):
-            total = total + got_ref[k, rows].astype(F32)
+        total = got_refs[0][rows].astype(F32)
+        for got_ref in got_refs[1:]:
+            total = total + got_ref[rows].astype(F32)
         def folded(rows, part):
             return jnp.concatenate([rows, jnp.concatenate([part[:48], part[48:]], axis=1)], axis=0)
 
@@ -550,7 +552,9 @@
     v, s = lax.axis_index("v"), lax.axis_index("s")
     start = (lax.rem(lax.axis_index("g") + 2, 4) * 2 + lax.axis_index("h")) * 384
     member = lax.axis_index(("h", "g"))
-    place = jnp.stack([v, start + 256 * v, start + 128, member * OWNED, s]).astype(jnp.int32)
+    place = jnp.stack(
+        [v, start + 256 * v, start + 128, member * OWNED, s, lax.axis_index("x"), lax.axis_index("w")]
+    ).astype(jnp.int32)
     gen_final, teacher_final, fake_final = gen_final.T, teacher_final.T, fake_final.T
 
     times, conds = time_features(jnp.concatenate([gen_steps, score_steps]), gen_modulation.shape[0])
@@ -630,7 +634,7 @@
         cost_estimate=pl.CostEstimate(flops=12 * 10**9, bytes_accessed=30 * 10**6, transcendentals=0),
         name="generator",
     )(place, own_noise, other_noise, gen_embed, mods, gen_final, g_packed, g_other)
-    packed, part = lax.optimization_barrier((packed, part))
+    packed, part, sums = lax.optimization_barrier((packed, part, sums))
     part = exchange(part, COMBINE)
 
     net_mods = lambda net: pl.BlockSpec((IMAGES, 8, D), lambda *_: (net, 0, 0))
@@ -700,7 +704,7 @@
     samples = lax.ppermute(samples, "s", SIBLING)
 
     gap = jnp.sum(pack2[:, 48:57, 96].astype(F32).reshape(OWNERS, 3, 3), axis=(0, 2))
-    gap = jnp.broadcast_to(jnp.pad(gap, (0, 125)), (16, 1, 128))
+    gap = jnp.broadcast_to(jnp.pad(gap, (0, 5))[None, :, None], (16, 8, 128))
     gap = exchange(gap, TOKEN_AXES)
     samples, gap = lax.optimization_barrier((samples, gap))
     samples = jnp.where(lax.axis_index("h") == s, own_samples, samples).transpose(0, 2, 1)
@@ -714,7 +718,7 @@
             functools.partial(gradient_kernel, net),
             grid=(4,),
             in_specs=[
-                smem(), whole((OWNERS, 64, 128)), *([whole((16, 1, 128))] * len(gaps)), net_mods(mods_net),
+                smem(), whole((OWNERS, 64, 128)), *([whole((16, 8, 128))] * len(gaps)), net_mods(mods_net),
                 whole((C, D)), *([whole((IMAGES, TOKENS, COLS))] * 2), by_columns,
             ],
             out_specs=[partial_spec, partial_spec],
@@ -728,25 +732,31 @@
 
     pieces = gradient(0, (), 2, fake_final, f_pre, f_res, f_shaped)
     pieces += gradient(1, (gap,), 0, gen_final, g_pre, g_res, g_shaped)
-    both = pl.pallas_call(
+    partials = pl.pallas_call(
         add_kernel,
         grid=(1,),
-        in_specs=[whole((CHUNKS, GEN_ROWS, 128))] * 4,
-        out_specs=whole((CHUNKS, 2 * GEN_ROWS, 128)),
-        out_shape=jax.ShapeDtypeStruct((CHUNKS, 2 * GEN_ROWS, 128), BF16),
+        in_specs=[smem()] + [whole((CHUNKS, GEN_ROWS, 128))] * 4,
+        out_specs=[whole((2 * GEN_ROWS, 128))] * CHUNKS,
+        out_shape=[jax.ShapeDtypeStruct((2 * GEN_ROWS, 128), BF16)] * CHUNKS,
         compiler_params=params(16),
         name="add",
-    )(*pieces)
+    )(place, *pieces)
+    partials = [
+        lax.ppermute(
+            part, GATHER, [(x * 2 + w, (x + dx) % 4 * 2 + (w + dw) % 2) for x in range(4) for w in range(2)]
+        ) if dx or dw else part
+        for (dx, dw), part in zip(OFFSETS, partials, strict=True)
+    ]
     tiles = jax.ShapeDtypeStruct((2, 144, 128), BF16)
     kept, sent = pl.pallas_call(
         sum_kernel,
         grid=(1,),
-        in_specs=[smem(), whole((CHUNKS, 2 * GEN_ROWS, 128))],
+        in_specs=[smem()] + [whole((2 * GEN_ROWS, 128))] * CHUNKS,
         out_specs=[whole((2, 144, 128))] * 2,
         out_shape=[tiles, tiles],
         compiler_params=params(8),
         name="sum",
-    )(place, exchange(both, GATHER))
+    )(place, *partials)
     kept = lax.ppermute(kept, PLACES, SWAP)
     sent = lax.ppermute(sent, PLACES, SWAP_TURNED)
     fake_grad, gen_grad = pl.pallas_call(

time: 198 us -> 198 us (level)
  waiting for transfers between devices: 52.1 us -> 41 us
  starting transfers between devices: 51.6 us -> 62.6 us
    all_to_all x5 -> x4, waiting for transfers between devices: 31.2 us -> 13.9 us  [exchange(): return lax.all_to_all(value, axes, 0, 0)]
    ppermute x0 -> x7, starting transfers between devices: none -> 14.3 us  [shards(): lax.ppermute(part, GATHER, [(x * 2 + w, (x + dx) % 4 * 2 + (w + dw) % 2)...]
    all_to_all x5 -> x4, starting transfers between devices: 30.4 us -> 24.4 us  [exchange(): return lax.all_to_all(value, axes, 0, 0)]
    ppermute x0 -> x7, waiting for transfers between devices: none -> 5.74 us  [shards(): lax.ppermute(part, GATHER, [(x * 2 + w, (x + dx) % 4 * 2 + (w + dw) % 2)...]
    ppermute x1, starting transfers between devices: 3.47 us -> 6.85 us  [shards(): kept = lax.ppermute(kept, PLACES, SWAP)]
  transfers between devices with their start and end apart: 16 -> 22, of which waited for: 13 -> 16; matrix products, arithmetic and copies ran while one was open for 2% -> 2% of each run, Pallas kernels for 12% -> 12%
where the time goes in v8:
time: 198 us; the launch traced here: 197 us
  starting transfers between devices  62.6 us (32%)
  Pallas kernels  46.4 us (23%)
  waiting for transfers between devices  41 us (21%)
  blocking collectives  37.4 us (19%)
  other arithmetic  4.91 us (2%)
  local copies, waits for them, and re-layouts  3.78 us (2%)
    all_to_all x3, blocking collectives, exchange(): return lax.all_to_all(value, axes, 0, 0)  37.4 us
    all_to_all x4, starting transfers between devices, exchange(): return lax.all_to_all(value, axes, 0, 0)  24.4 us
    ppermute x7, starting transfers between devices, shards(): lax.ppermute(part, GATHER, [(x * 2 + w, (x + dx) % 4 * 2 + (w + dw) % 2)...  14.3 us
    all_to_all x4, waiting for transfers between devices, exchange(): return lax.all_to_all(value, axes, 0, 0)  13.9 us
    pallas_call x1, Pallas kernels, shards(): pl.pallas_call(score_kernel, grid=(IMAGES,), in_specs=[smem(), smem(), wh...  12.2 us
    pallas_call x2, Pallas kernels, gradient(): pl.pallas_call(functools.partial(gradient_kernel, net), grid=(4,), in_spe...  12.2 us
    pallas_call x1, Pallas kernels, shards(): pl.pallas_call(generator_kernel, grid=(IMAGES,), in_specs=[smem(), noise_...  8.49 us
    ppermute x1, starting transfers between devices, shards(): mine = lax.ppermute(mine, PLACES, SWAP)  7.41 us
  transfers between devices with their start and end apart: 22, of which 16 were waited for; matrix products, arithmetic and copies ran while one was open for 2% of the time, Pallas kernels for 12%

profile of v8, /device:TPU:1, one launch (start us, length us, event | category | flops | bytes accessed | tf_op | source)
XLA Modules:
  0.0 196.9 jit_solution(5912483242423563049)
XLA Ops:
  0.7 0.8 broadcast_multiply_fusion
  1.5 0.6 multiply_convert_fusion.cond_ref
  2.1 0.6 stack.40.place_ref
  2.8 2.4 %split.1 = (bf16[528,128]{1,0:T(8,128)(2,1)}, bf16[528,128]{1,0:T(8,128)(2,1)}, bf16[384,128]{1,0:T(8,128)(2,1)}) custom-call(s32[7]{0:T(128)} %stack.40.place_ref, bf16[6,256]{1,0:T(8,128)(2,1)} %multiply_convert_fusion.cond_ref, bf16[3,64,128]{2,1,0:T(8,128)(2,1)} %bitcast.36, bf16[3,64,128]{2,1,0:T(8,128)(2,1)} %bitcast.37, bf16[96,384]{1,0:T(8,128)(2,1)} %gen_ref.1, ...), custom_call_target="tpu_custom_call" | custom-call | tf_op jit(solution)/shard_map/split/pallas_call | solution.py:563
  5.1 7.4 %collective-permute-start = (bf16[528,128]{1,0:T(8,128)(2,1)}, bf16[528,128]{1,0:T(8,128)(2,1)S(1)}, u32[]{:S(2)}, u32[]{:S(2)}) collective-permute-start(bf16[528,128]{1,0:T(8,128)(2,1)} %get-tuple-element.55), channel_id=1, source_target_pairs={{0,128},{1,136},{2,130},{3,138},{8,129},{9,137},{10,131},{11,139},... | collective-permute-start | bytes 405512 | tf_op jit(solution)/shard_map/ppermute | solution.py:574
  12.5 1.1 collective-permute-start.1
  13.6 2.5 %collective-permute-done.mine_ref = bf16[528,128]{1,0:T(8,128)(2,1)S(1)} collective-permute-done((bf16[528,128]{1,0:T(8,128)(2,1)}, bf16[528,128]{1,0:T(8,128)(2,1)S(1)}, u32[]{:S(2)}, u32[]{:S(2)}) %collective-permute-start) | collective-permute-done | bytes 135200 | tf_op jit(solution)/shard_map/ppermute | solution.py:574
  16.1 6.3 %collective-permute-done.1.other_ref = bf16[528,128]{1,0:T(8,128)(2,1)S(1)} collective-permute-done((bf16[528,128]{1,0:T(8,128)(2,1)}, bf16[528,128]{1,0:T(8,128)(2,1)S(1)}, u32[]{:S(2)}, u32[]{:S(2)}) %collective-permute-start.1) | collective-permute-done | bytes 135200 | tf_op jit(solution)/shard_map/ppermute | solution.py:575
  22.4 0.6 copy-done
  23.0 1.5 pack.3
  24.5 6.4 %all-to-all-start = ((bf16[8,368,128]{2,1,0:T(8,128)(2,1)}), bf16[8,368,128]{2,1,0:T(8,128)(2,1)S(1)}, u32[]{:S(2)}, u32[]{:S(2)}) async-start(bf16[8,368,128]{2,1,0:T(8,128)(2,1)} %pack.3), calls=%async_computation | async-start | bytes 1507328 | tf_op jit(solution)/shard_map/all_to_all | solution.py:531
  30.9 1.4 collective-permute-start.3
  32.3 3.1 %collective-permute-start.2 = (bf16[384,128]{1,0:T(8,128)(2,1)S(1)}, bf16[384,128]{1,0:T(8,128)(2,1)S(1)}, u32[]{:S(2)}, u32[]{:S(2)}) collective-permute-start(bf16[384,128]{1,0:T(8,128)(2,1)S(1)} %copy-done.2), channel_id=1, source_target_pairs={{0,0},{1,200},{2,2},{3,202},{8,193},{9,9},{10,195},{11,11},{64,64}... | collective-permute-start | bytes 294920 | tf_op jit(solution)/shard_map/ppermute | solution.py:577
  35.4 3.6 %collective-permute-done.3.other_ref = bf16[384,128]{1,0:T(8,128)(2,1)S(1)} collective-permute-done((bf16[384,128]{1,0:T(8,128)(2,1)S(1)}, bf16[384,128]{1,0:T(8,128)(2,1)S(1)}, u32[]{:S(2)}, u32[]{:S(2)}) %collective-permute-start.3) | collective-permute-done | bytes 98336 | tf_op jit(solution)/shard_map/ppermute | solution.py:578
  39.0 0.4 collective-permute-done.2.own_ref.noise_ref
  39.4 2.1 %all-to-all-done.own_w_ref = bf16[8,368,128]{2,1,0:T(8,128)(2,1)S(1)} async-done(((bf16[8,368,128]{2,1,0:T(8,128)(2,1)}), bf16[8,368,128]{2,1,0:T(8,128)(2,1)S(1)}, u32[]{:S(2)}, u32[]{:S(2)}) %all-to-all-start) | async-done | bytes 753696 | tf_op jit(solution)/shard_map/all_to_all | solution.py:531
  41.5 1.7 pack.2
  43.3 0.6 collective-permute-done.4.other_w_ref
  43.9 5.3 %all-to-all-start.1 = ((bf16[8,576,128]{2,1,0:T(8,128)(2,1)}), bf16[8,576,128]{2,1,0:T(8,128)(2,1)S(1)}, u32[]{:S(2)}, u32[]{:S(2)}) async-start(bf16[8,576,128]{2,1,0:T(8,128)(2,1)} %pack.2), calls=%async_computation.1 | async-start | bytes 2359296 | tf_op jit(solution)/shard_map/all_to_all | solution.py:531
  49.2 0.9 broadcast_select_fusion.1
  50.2 0.4 maximum_bitcast_fusion
  50.9 1.4 convert_element_type.25
  52.3 1.1 pad_convert_fusion.mods_ref.t_mods_ref.f_mods_ref.refs_0_.refs_1_
  53.4 1.8 sums.1.sums_ref
  55.2 8.5 %generator.1 = (bf16[16,32,128]{2,1,0:T(8,128)(2,1)}, bf16[3,256,3072]{2,1,0:T(8,128)(2,1)}, f32[3,256,192]{2,1,0:T(8,128)}, f32[3,256,192]{2,1,0:T(8,128)}) custom-call(s32[7]{0:T(128)S(1)} %copy-done.1, bf16[384,128]{1,0:T(8,128)(2,1)S(1)} %collective-permute-done.2.own_ref.noise_ref, bf16[384,128]{1,0:T(8,128)(2,1)S(1)} %collective-permute-done.3.other_ref, ...), custom_call_target="tpu_custom_call" | custom-call | flops 12000000000 | bytes 30000000 | tf_op jit(solution)/shard_map/generator/pallas_call | solution.py:622
  63.7 3.7 %all-to-all-done.1.own_w_ref = bf16[8,576,128]{2,1,0:T(8,128)(2,1)S(1)} async-done(((bf16[8,576,128]{2,1,0:T(8,128)(2,1)}), bf16[8,576,128]{2,1,0:T(8,128)(2,1)S(1)}, u32[]{:S(2)}, u32[]{:S(2)}) %all-to-all-start.1) | async-done | bytes 1179680 | tf_op jit(solution)/shard_map/all_to_all | solution.py:531
  67.4 5.3 %all-to-all-start.2 = ((bf16[16,32,128]{2,1,0:T(8,128)(2,1)}), bf16[16,32,128]{2,1,0:T(8,128)(2,1)S(1)}, u32[]{:S(2)}, u32[]{:S(2)}) async-start(bf16[16,32,128]{2,1,0:T(8,128)(2,1)} %get-tuple-element.73), calls=%async_computation.2 | async-start | bytes 262144 | tf_op jit(solution)/shard_map/all_to_all | solution.py:531
  72.7 7.3 %all-to-all-done.2.got_ref = bf16[16,32,128]{2,1,0:T(8,128)(2,1)S(1)} async-done(((bf16[16,32,128]{2,1,0:T(8,128)(2,1)}), bf16[16,32,128]{2,1,0:T(8,128)(2,1)S(1)}, u32[]{:S(2)}, u32[]{:S(2)}) %all-to-all-start.2) | async-done | bytes 131104 | tf_op jit(solution)/shard_map/all_to_all | solution.py:531
  80.1 1.2 samples.1
  81.2 2.8 %collective-permute-start.5 = (bf16[8,576,128]{2,1,0:T(8,128)(2,1)S(1)}, bf16[8,576,128]{2,1,0:T(8,128)(2,1)S(1)}, u32[]{:S(2)}, u32[]{:S(2)}) collective-permute-start(bf16[8,576,128]{2,1,0:T(8,128)(2,1)S(1)} %all-to-all-done.1.own_w_ref), channel_id=1, source_target_pairs={{0,1},{1,0},{2,3},{3,2},{4,5},{5,4},{6,7},{7,6},{8,9},{9,8},{10,11... | collective-permute-start | bytes 3538952 | tf_op jit(solution)/shard_map/ppermute | solution.py:657
  84.0 10.5 %all_to_all.35.got_ref = f32[16,24,128]{2,1,0:T(8,128)S(1)} all-to-all(f32[16,24,128]{2,1,0:T(8,128)S(1)} %get-tuple-element.76), channel_id=1, replica_groups=mesh['g'=4,'x'=4,'h'=2,'w'=2,'v'=2,'s'=2] {'v','h','g'}, dimensions={0} | all-to-all | bytes 393216 | tf_op jit(solution)/shard_map/all_to_all | solution.py:531
  94.5 12.2 %score.1 = (bf16[16,64,128]{2,1,0:T(8,128)(2,1)S(1)}, f32[3,64,128]{2,1,0:T(8,128)S(1)}, bf16[3,256,3072]{2,1,0:T(8,128)(2,1)}, f32[3,256,192]{2,1,0:T(8,128)}, f32[3,256,192]{2,1,0:T(8,128)}) custom-call(s32[7]{0:T(128)S(1)} %copy-done.1, f32[3]{0:T(128)S(1)} %get-tuple-element.114.time_ref, f32[16,24,128]{2,1,0:T(8,128)S(1)} %all_to_all.35.got_ref, ...), custom_call_target="tpu_custom_call" | custom-call | flops 24000000000 | bytes 50000000 | tf_op jit(solution)/shard_map/score/pallas_call | solution.py:659
  106.7 13.1 %all_to_all.36.got_ref = bf16[16,64,128]{2,1,0:T(8,128)(2,1)S(1)} all-to-all(bf16[16,64,128]{2,1,0:T(8,128)(2,1)S(1)} %get-tuple-element.79), channel_id=1, replica_groups=mesh['g'=4,'x'=4,'h'=2,'w'=2,'v'=2,'s'=2] {'v','h','g'}, dimensions={0} | all-to-all | bytes 524288 | tf_op jit(solution)/shard_map/all_to_all | solution.py:531
  119.8 2.1 %cotangents.1 = bf16[16,64,128]{2,1,0:T(8,128)(2,1)S(1)} custom-call(s32[7]{0:T(128)S(1)} %copy-done.1, f32[3]{0:T(128)S(1)} %get-tuple-element.113.time_ref.gen_time_ref, f32[3]{0:T(128)S(1)} %get-tuple-element.114.time_ref, bf16[16,64,128]{2,1,0:T(8,128)(2,1)S(1)} %all_to_all.36.got_ref, bf16[384,128]{1,0:T(8,128)(2,1)S(1)} %collective-permute-done.2.own_ref.noise_ref, ...), custom_call_target="tpu_custom_call" | custom-call | tf_op jit(solution)/shard_map/cotangents/pallas_call | solution.py:689
  121.9 13.9 %all_to_all.37.got_ref = bf16[16,64,128]{2,1,0:T(8,128)(2,1)S(1)} all-to-all(bf16[16,64,128]{2,1,0:T(8,128)(2,1)S(1)} %cotangents.1), channel_id=1, replica_groups=mesh['g'=4,'x'=4,'h'=2,'w'=2,'v'=2,'s'=2] {'v','h','g'}, dimensions={0} | all-to-all | bytes 524288 | tf_op jit(solution)/shard_map/all_to_all | solution.py:531
  135.8 0.2 convert_reduce_fusion
  136.0 0.1 reduce_sum.18
  136.2 0.7 broadcast_in_dim.2
  136.9 7.5 %all-to-all-start.6 = ((f32[16,8,128]{2,1,0:T(8,128)}), f32[16,8,128]{2,1,0:T(8,128)S(1)}, u32[]{:S(2)}, u32[]{:S(2)}) async-start(f32[16,8,128]{2,1,0:T(8,128)} %broadcast_in_dim.2), calls=%async_computation.6 | async-start | bytes 131072 | tf_op jit(solution)/shard_map/all_to_all | solution.py:531
  144.3 0.2 collective-permute-start.6
  144.5 6.0 %gradient.2 = (bf16[8,288,128]{2,1,0:T(8,128)(2,1)S(1)}, bf16[8,288,128]{2,1,0:T(8,128)(2,1)S(1)}) custom-call(s32[7]{0:T(128)S(1)} %copy-done.1, bf16[16,64,128]{2,1,0:T(8,128)(2,1)S(1)} %all_to_all.37.got_ref, f32[9,8,3072]{2,1,0:T(8,128)S(1)} %pad_convert_fusion.mods_ref.t_mods_ref.f_mods_ref.refs_0_.refs_1_, bf16[64,3072]{1,0:T(8,128)(2,1)} %bitcast.29, ...), custom_call_target="tpu_custom_call" | custom-call | flops 7000000000 | bytes 20000000 | tf_op jit(solution)/shard_map/gradient/pallas_call | solution.py:717
  150.6 0.4 collective-permute-start.7
  151.0 0.7 all-to-all-done.6.refs_0_
  151.7 6.1 %gradient.3 = (bf16[8,288,128]{2,1,0:T(8,128)(2,1)S(1)}, bf16[8,288,128]{2,1,0:T(8,128)(2,1)S(1)}) custom-call(s32[7]{0:T(128)S(1)} %copy-done.1, bf16[16,64,128]{2,1,0:T(8,128)(2,1)S(1)} %all_to_all.37.got_ref, f32[16,8,128]{2,1,0:T(8,128)S(1)} %all-to-all-done.6.refs_0_, f32[9,8,3072]{2,1,0:T(8,128)S(1)} %pad_convert_fusion.mods_ref.t_mods_ref.f_mods_ref.refs_0_.refs_1_, ...), custom_call_target="tpu_custom_call" | custom-call | flops 7000000000 | bytes 20000000 | tf_op jit(solution)/shard_map/gradient/pallas_call | solution.py:717
  157.8 0.5 collective-permute-start.8
  158.3 1.6 collective-permute-done.8.g_got_ref
  160.0 0.8 add.46
  160.8 4.9 %collective-permute-start.9 = (bf16[576,128]{1,0:T(8,128)(2,1)S(1)}, bf16[576,128]{1,0:T(8,128)(2,1)S(1)}, u32[]{:S(2)}, u32[]{:S(2)}) collective-permute-start(bf16[576,128]{1,0:T(8,128)(2,1)S(1)} %get-tuple-element.95), channel_id=1, source_target_pairs={{0,36},{4,32},{16,52},{20,48},{32,4},{36,0},{48,20},{52,16},{1,37}... | collective-permute-start | bytes 442376 | tf_op jit(solution)/shard_map/ppermute | solution.py:745
  165.7 0.3 collective-permute-start.10
  165.9 4.8 %collective-permute-start.11 = (bf16[576,128]{1,0:T(8,128)(2,1)S(1)}, bf16[576,128]{1,0:T(8,128)(2,1)S(1)}, u32[]{:S(2)}, u32[]{:S(2)}) collective-permute-start(bf16[576,128]{1,0:T(8,128)(2,1)S(1)} %get-tuple-element.97), channel_id=1, source_target_pairs={{0,52},{4,48},{16,4},{20,0},{32,20},{36,16},{48,36},{52,32},{1,53}... | collective-permute-start | bytes 442376 | tf_op jit(solution)/shard_map/ppermute | solution.py:745
  170.7 0.3 collective-permute-start.13
  171.0 2.4 %collective-permute-start.14 = (bf16[576,128]{1,0:T(8,128)(2,1)S(1)}, bf16[576,128]{1,0:T(8,128)(2,1)S(1)}, u32[]{:S(2)}, u32[]{:S(2)}) collective-permute-start(bf16[576,128]{1,0:T(8,128)(2,1)S(1)} %get-tuple-element.100), channel_id=1, source_target_pairs={{0,48},{4,52},{16,0},{20,4},{32,16},{36,20},{48,32},{52,36},{1,49}... | collective-permute-start | bytes 442376 | tf_op jit(solution)/shard_map/ppermute | solution.py:745
  173.4 1.7 collective-permute-done.10.refs_1_
  175.1 1.7 collective-permute-start.15
  176.8 0.8 collective-permute-done.12.refs_3_
  177.6 2.3 %collective-permute-done.13.refs_4_ = bf16[576,128]{1,0:T(8,128)(2,1)S(1)} collective-permute-done((bf16[576,128]{1,0:T(8,128)(2,1)S(1)}, bf16[576,128]{1,0:T(8,128)(2,1)S(1)}, u32[]{:S(2)}, u32[]{:S(2)}) %collective-permute-start.13) | collective-permute-done | bytes 147488 | tf_op jit(solution)/shard_map/ppermute | solution.py:745
  179.9 0.9 collective-permute-done.14.refs_5_
  180.8 0.7 sum.1
  181.5 6.8 %collective-permute-start.16 = (bf16[2,144,128]{2,1,0:T(8,128)(2,1)S(1)}, bf16[2,144,128]{2,1,0:T(8,128)(2,1)S(1)}, u32[]{:S(2)}, u32[]{:S(2)}) collective-permute-start(bf16[2,144,128]{2,1,0:T(8,128)(2,1)S(1)} %get-tuple-element.103), channel_id=1, source_target_pairs={{0,128},{1,136},{2,130},{3,138},{8,129},{9,137},{10,131},{11,139},... | collective-permute-start | bytes 221192 | tf_op jit(solution)/shard_map/ppermute | solution.py:760
  188.4 0.2 collective-permute-start.17
  188.6 0.7 select_bitcast_fusion
  189.2 1.4 collective-permute-done.16.keep_ref
  190.7 4.9 %collective-permute-done.17.other_ref = bf16[2,144,128]{2,1,0:T(8,128)(2,1)S(1)} collective-permute-done((bf16[2,144,128]{2,1,0:T(8,128)(2,1)S(1)}, bf16[2,144,128]{2,1,0:T(8,128)(2,1)S(1)}, u32[]{:S(2)}, u32[]{:S(2)}) %collective-permute-start.17) | collective-permute-done | bytes 73760 | tf_op jit(solution)/shard_map/ppermute | solution.py:761
  195.5 1.3 place.1
  (23 shorter events, 0.6 us)
Async XLA Ops:
  5.1 11.0 %collective-permute-start = (bf16[528,128]{1,0:T(8,128)(2,1)}, bf16[528,128]{1,0:T(8,128)(2,1)S(1)}, u32[]{:S(2)}, u32[]{:S(2)}) collective-permute-start(bf16[528,128]{1,0:T(8,128)(2,1)} %get-tuple-element.55), channel_id=1, source_target_pairs={{0,128},{1,136},{2,130},{3,138},{8,129},{9,137},{10,131},{11,139},... | collective-permute-start | bytes 405512 | tf_op jit(solution)/shard_map/ppermute | solution.py:574
  12.5 9.9 %collective-permute-start.1 = (bf16[528,128]{1,0:T(8,128)(2,1)}, bf16[528,128]{1,0:T(8,128)(2,1)S(1)}, u32[]{:S(2)}, u32[]{:S(2)}) collective-permute-start(bf16[528,128]{1,0:T(8,128)(2,1)} %get-tuple-element.56), channel_id=1, source_target_pairs={{0,130},{1,138},{2,128},{3,136},{8,131},{9,139},{10,129},{11,137},... | collective-permute-start | bytes 405512 | tf_op jit(solution)/shard_map/ppermute | solution.py:575
  22.4 0.6 copy-start
  23.0 7.9 %copy-start.2 = (bf16[384,128]{1,0:T(8,128)(2,1)S(1)}, bf16[384,128]{1,0:T(8,128)(2,1)}, u32[]{:S(2)}) copy-start(bf16[384,128]{1,0:T(8,128)(2,1)} %get-tuple-element.60) | copy-start | bytes 294916
  23.0 18.6 %copy-start.1 = (s32[7]{0:T(128)S(1)}, s32[7]{0:T(128)}, u32[]{:S(2)}) copy-start(s32[7]{0:T(128)} %stack.40.place_ref) | copy-start | bytes 88
  24.5 17.0 %all-to-all-start = ((bf16[8,368,128]{2,1,0:T(8,128)(2,1)}), bf16[8,368,128]{2,1,0:T(8,128)(2,1)S(1)}, u32[]{:S(2)}, u32[]{:S(2)}) async-start(bf16[8,368,128]{2,1,0:T(8,128)(2,1)} %pack.3), calls=%async_computation | async-start | bytes 1507328 | tf_op jit(solution)/shard_map/all_to_all | solution.py:531
  30.9 8.1 %collective-permute-start.3 = (bf16[384,128]{1,0:T(8,128)(2,1)S(1)}, bf16[384,128]{1,0:T(8,128)(2,1)S(1)}, u32[]{:S(2)}, u32[]{:S(2)}) collective-permute-start(bf16[384,128]{1,0:T(8,128)(2,1)S(1)} %copy-done.2), channel_id=1, source_target_pairs={{0,2},{1,202},{2,0},{3,200},{8,195},{9,11},{10,193},{11,9},{64,66}... | collective-permute-start | bytes 294920 | tf_op jit(solution)/shard_map/ppermute | solution.py:578
  32.3 7.1 %collective-permute-start.2 = (bf16[384,128]{1,0:T(8,128)(2,1)S(1)}, bf16[384,128]{1,0:T(8,128)(2,1)S(1)}, u32[]{:S(2)}, u32[]{:S(2)}) collective-permute-start(bf16[384,128]{1,0:T(8,128)(2,1)S(1)} %copy-done.2), channel_id=1, source_target_pairs={{0,0},{1,200},{2,2},{3,202},{8,193},{9,9},{10,195},{11,11},{64,64}... | collective-permute-start | bytes 294920 | tf_op jit(solution)/shard_map/ppermute | solution.py:577
  41.5 2.4 %collective-permute-start.4 = (bf16[8,368,128]{2,1,0:T(8,128)(2,1)S(1)}, bf16[8,368,128]{2,1,0:T(8,128)(2,1)}, u32[]{:S(2)}, u32[]{:S(2)}) collective-permute-start(bf16[8,368,128]{2,1,0:T(8,128)(2,1)S(1)} %all-to-all-done.own_w_ref), channel_id=1, source_target_pairs={{0,1},{1,0},{2,3},{3,2},{4,5},{5,4},{6,7},{7,6},{8,9},{9,8},{10,11... | collective-permute-start | bytes 2261000 | tf_op jit(solution)/shard_map/ppermute | solution.py:596
  43.9 23.4 %all-to-all-start.1 = ((bf16[8,576,128]{2,1,0:T(8,128)(2,1)}), bf16[8,576,128]{2,1,0:T(8,128)(2,1)S(1)}, u32[]{:S(2)}, u32[]{:S(2)}) async-start(bf16[8,576,128]{2,1,0:T(8,128)(2,1)} %pack.2), calls=%async_computation.1 | async-start | bytes 2359296 | tf_op jit(solution)/shard_map/all_to_all | solution.py:531
  67.4 12.7 %all-to-all-start.2 = ((bf16[16,32,128]{2,1,0:T(8,128)(2,1)}), bf16[16,32,128]{2,1,0:T(8,128)(2,1)S(1)}, u32[]{:S(2)}, u32[]{:S(2)}) async-start(bf16[16,32,128]{2,1,0:T(8,128)(2,1)} %get-tuple-element.73), calls=%async_computation.2 | async-start | bytes 262144 | tf_op jit(solution)/shard_map/all_to_all | solution.py:531
  81.2 13.2 %collective-permute-start.5 = (bf16[8,576,128]{2,1,0:T(8,128)(2,1)S(1)}, bf16[8,576,128]{2,1,0:T(8,128)(2,1)S(1)}, u32[]{:S(2)}, u32[]{:S(2)}) collective-permute-start(bf16[8,576,128]{2,1,0:T(8,128)(2,1)S(1)} %all-to-all-done.1.own_w_ref), channel_id=1, source_target_pairs={{0,1},{1,0},{2,3},{3,2},{4,5},{5,4},{6,7},{7,6},{8,9},{9,8},{10,11... | collective-permute-start | bytes 3538952 | tf_op jit(solution)/shard_map/ppermute | solution.py:657
  136.9 14.8 %all-to-all-start.6 = ((f32[16,8,128]{2,1,0:T(8,128)}), f32[16,8,128]{2,1,0:T(8,128)S(1)}, u32[]{:S(2)}, u32[]{:S(2)}) async-start(f32[16,8,128]{2,1,0:T(8,128)} %broadcast_in_dim.2), calls=%async_computation.6 | async-start | bytes 131072 | tf_op jit(solution)/shard_map/all_to_all | solution.py:531
  144.3 7.4 %collective-permute-start.6 = (f32[3,64,128]{2,1,0:T(8,128)S(1)}, f32[3,64,128]{2,1,0:T(8,128)S(1)}, u32[]{:S(2)}, u32[]{:S(2)}) collective-permute-start(f32[3,64,128]{2,1,0:T(8,128)S(1)} %get-tuple-element.81), channel_id=1, source_target_pairs={{0,1},{1,0},{2,3},{3,2},{4,5},{5,4},{6,7},{7,6},{8,9},{9,8},{10,11... | collective-permute-start | bytes 294920 | tf_op jit(solution)/shard_map/ppermute | solution.py:704
  150.6 7.8 %collective-permute-start.7 = (bf16[8,288,128]{2,1,0:T(8,128)(2,1)S(1)}, bf16[8,288,128]{2,1,0:T(8,128)(2,1)S(1)}, u32[]{:S(2)}, u32[]{:S(2)}) collective-permute-start(bf16[8,288,128]{2,1,0:T(8,128)(2,1)S(1)} %get-tuple-element.88), channel_id=1, source_target_pairs={{0,1},{1,0},{2,3},{3,2},{4,5},{5,4},{6,7},{7,6},{8,9},{9,8},{10,11... | collective-permute-start | bytes 1769480 | tf_op jit(solution)/shard_map/ppermute | solution.py:731
  157.8 2.1 %collective-permute-start.8 = (bf16[8,288,128]{2,1,0:T(8,128)(2,1)S(1)}, bf16[8,288,128]{2,1,0:T(8,128)(2,1)S(1)}, u32[]{:S(2)}, u32[]{:S(2)}) collective-permute-start(bf16[8,288,128]{2,1,0:T(8,128)(2,1)S(1)} %get-tuple-element.94), channel_id=1, source_target_pairs={{0,1},{1,0},{2,3},{3,2},{4,5},{5,4},{6,7},{7,6},{8,9},{9,8},{10,11... | collective-permute-start | bytes 1769480 | tf_op jit(solution)/shard_map/ppermute | solution.py:731
  160.8 10.2 %collective-permute-start.9 = (bf16[576,128]{1,0:T(8,128)(2,1)S(1)}, bf16[576,128]{1,0:T(8,128)(2,1)S(1)}, u32[]{:S(2)}, u32[]{:S(2)}) collective-permute-start(bf16[576,128]{1,0:T(8,128)(2,1)S(1)} %get-tuple-element.95), channel_id=1, source_target_pairs={{0,36},{4,32},{16,52},{20,48},{32,4},{36,0},{48,20},{52,16},{1,37}... | collective-permute-start | bytes 442376 | tf_op jit(solution)/shard_map/ppermute | solution.py:745
  165.7 9.5 %collective-permute-start.10 = (bf16[576,128]{1,0:T(8,128)(2,1)S(1)}, bf16[576,128]{1,0:T(8,128)(2,1)S(1)}, u32[]{:S(2)}, u32[]{:S(2)}) collective-permute-start(bf16[576,128]{1,0:T(8,128)(2,1)S(1)} %get-tuple-element.96), channel_id=1, source_target_pairs={{0,20},{4,16},{16,36},{20,32},{32,52},{36,48},{48,4},{52,0},{1,21}... | collective-permute-start | bytes 442376 | tf_op jit(solution)/shard_map/ppermute | solution.py:745
  165.9 10.9 %collective-permute-start.11 = (bf16[576,128]{1,0:T(8,128)(2,1)S(1)}, bf16[576,128]{1,0:T(8,128)(2,1)S(1)}, u32[]{:S(2)}, u32[]{:S(2)}) collective-permute-start(bf16[576,128]{1,0:T(8,128)(2,1)S(1)} %get-tuple-element.97), channel_id=1, source_target_pairs={{0,52},{4,48},{16,4},{20,0},{32,20},{36,16},{48,36},{52,32},{1,53}... | collective-permute-start | bytes 442376 | tf_op jit(solution)/shard_map/ppermute | solution.py:745
  170.7 6.9 %collective-permute-start.12 = (bf16[576,128]{1,0:T(8,128)(2,1)S(1)}, bf16[576,128]{1,0:T(8,128)(2,1)S(1)}, u32[]{:S(2)}, u32[]{:S(2)}) collective-permute-start(bf16[576,128]{1,0:T(8,128)(2,1)S(1)} %get-tuple-element.98), channel_id=1, source_target_pairs={{0,32},{4,36},{16,48},{20,52},{32,0},{36,4},{48,16},{52,20},{1,33}... | collective-permute-start | bytes 442376 | tf_op jit(solution)/shard_map/ppermute | solution.py:745
  170.7 9.2 %collective-permute-start.13 = (bf16[576,128]{1,0:T(8,128)(2,1)S(1)}, bf16[576,128]{1,0:T(8,128)(2,1)S(1)}, u32[]{:S(2)}, u32[]{:S(2)}) collective-permute-start(bf16[576,128]{1,0:T(8,128)(2,1)S(1)} %get-tuple-element.99), channel_id=1, source_target_pairs={{0,16},{4,20},{16,32},{20,36},{32,48},{36,52},{48,0},{52,4},{1,17}... | collective-permute-start | bytes 442376 | tf_op jit(solution)/shard_map/ppermute | solution.py:745
  171.0 9.8 %collective-permute-start.14 = (bf16[576,128]{1,0:T(8,128)(2,1)S(1)}, bf16[576,128]{1,0:T(8,128)(2,1)S(1)}, u32[]{:S(2)}, u32[]{:S(2)}) collective-permute-start(bf16[576,128]{1,0:T(8,128)(2,1)S(1)} %get-tuple-element.100), channel_id=1, source_target_pairs={{0,48},{4,52},{16,0},{20,4},{32,16},{36,20},{48,32},{52,36},{1,49}... | collective-permute-start | bytes 442376 | tf_op jit(solution)/shard_map/ppermute | solution.py:745
  175.1 5.7 %collective-permute-start.15 = (bf16[576,128]{1,0:T(8,128)(2,1)S(1)}, bf16[576,128]{1,0:T(8,128)(2,1)S(1)}, u32[]{:S(2)}, u32[]{:S(2)}) collective-permute-start(bf16[576,128]{1,0:T(8,128)(2,1)S(1)} %get-tuple-element.101), channel_id=1, source_target_pairs={{0,4},{4,0},{16,20},{20,16},{32,36},{36,32},{48,52},{52,48},{1,5},... | collective-permute-start | bytes 442376 | tf_op jit(solution)/shard_map/ppermute | solution.py:745
  181.5 9.1 %collective-permute-start.16 = (bf16[2,144,128]{2,1,0:T(8,128)(2,1)S(1)}, bf16[2,144,128]{2,1,0:T(8,128)(2,1)S(1)}, u32[]{:S(2)}, u32[]{:S(2)}) collective-permute-start(bf16[2,144,128]{2,1,0:T(8,128)(2,1)S(1)} %get-tuple-element.103), channel_id=1, source_target_pairs={{0,128},{1,136},{2,130},{3,138},{8,129},{9,137},{10,131},{11,139},... | collective-permute-start | bytes 221192 | tf_op jit(solution)/shard_map/ppermute | solution.py:760
  188.4 7.1 %collective-permute-start.17 = (bf16[2,144,128]{2,1,0:T(8,128)(2,1)S(1)}, bf16[2,144,128]{2,1,0:T(8,128)(2,1)S(1)}, u32[]{:S(2)}, u32[]{:S(2)}) collective-permute-start(bf16[2,144,128]{2,1,0:T(8,128)(2,1)S(1)} %get-tuple-element.104), channel_id=1, source_target_pairs={{0,130},{1,138},{2,128},{3,136},{8,131},{9,139},{10,129},{11,137},... | collective-permute-start | bytes 221192 | tf_op jit(solution)/shard_map/ppermute | solution.py:761
